TPU v7x, 32 devices: a whole 2x2x4 slice. The times are simulated.
32 devices in a mesh: seq: 32 (over z, y, x, core), mp: 1.
Axes of the slice: x: 2, y: 2, z: 4, core: 2. Of those that a mesh axis runs over, the one named last changes fastest.
Arguments:
- state: bfloat16 [15360, 1024], P('seq'), may hold values from -60 to 60
- condition: bfloat16 [15360, 1024], P('seq'), may hold values from -6 to 6
- time_vector: bfloat16 [1024], replicated, may hold values from -4 to 4
- norm_gain: bfloat16 [1024], replicated, may hold values from 0.59765625 to 1.3984375
- w_qkv: bfloat16 [3, 1024, 1024], P(None, None, 'mp'), may hold values from -2 to 2
- w_out: bfloat16 [1024, 1024], P('mp'), may hold values from -0.75 to 0.75
- utterance_ids: int32 [15360], P('seq'), may hold values from 0 to 59, never falling along the last dimension, each value on 1 to 1024 neighbouring positions
Outputs:
- final_state: bfloat16 [15360, 1024], P('seq', 'mp')
Inputs may be any that keep to these rules, and one draw needn't show every extreme that they name: `utterance_ids`: never falling along the frames; each utterance has 1 to 1024 frames and one has exactly 1024.
All inputs are finite; a program needn't handle non-finite values.
Results may differ from a plain program's by a relative error of at most 0.03.
Values may be sent and summed in bfloat16 or wider, within the bound.
No kernel may reach another device: no remote copies, remote signals or barrier semaphores. Data moves between devices by JAX's collectives and lax.ppermute only.
A program may use at most 64 MiB of HBM per device.

v0:
```python
import jax
import jax.numpy as jnp
from jax import lax
from jax.sharding import PartitionSpec as P

HEAD_DIM = 64
BLOCK = 24


def shifted(shard, axis, by):
    count = lax.axis_size(axis)
    pairs = [(i, i + by) for i in range(count) if 0 <= i + by < count]
    return lax.ppermute(shard, axis, pairs)


def banded_attention(q, keys_values, seg_ext, seg_plus, head_dim):
    frames = q.shape[0]
    width = q.shape[1]
    nblocks = frames // BLOCK
    heads = width // head_dim
    rows = (jnp.arange(nblocks, dtype=jnp.int32) * BLOCK)[:, None] + jnp.arange(
        4 * BLOCK, dtype=jnp.int32
    )[None, :]
    window = keys_values[rows]
    k_rows = window[:, :, :width].reshape(nblocks, 4 * BLOCK, heads, head_dim)
    v_rows = window[:, :, width:].reshape(nblocks, 4 * BLOCK, heads, head_dim)
    q_rows = q.reshape(nblocks, BLOCK, heads, head_dim)
    scores = (
        jnp.einsum("bqhe,bkhe->bhqk", q_rows, k_rows, preferred_element_type=jnp.float32) * 0.125
    )
    k_seg = seg_ext[rows]
    q_seg = seg_plus.reshape(nblocks, BLOCK)
    allowed = (q_seg[:, :, None] == k_seg[:, None, :])[:, None]
    scores = jnp.where(allowed, scores, -1e30)
    top = jnp.max(scores, axis=-1, keepdims=True)
    expo = jnp.exp(scores - top)
    probs = (expo / jnp.sum(expo, axis=-1, keepdims=True)).astype(jnp.bfloat16)
    out = jnp.einsum("bhqk,bkhe->bqhe", probs, v_rows, preferred_element_type=jnp.float32)
    return out.astype(jnp.bfloat16).reshape(frames, width)


def velocity_terms(x_full, condition, time_vector, norm_gain, w_qkv, w_out, seg_ext, seg_plus, t):
    h = x_full + condition.astype(jnp.float32) + t * time_vector.astype(jnp.float32)
    scale = lax.rsqrt(jnp.mean(h * h, axis=-1, keepdims=True) + 1e-06)
    normed = (h * scale * norm_gain.astype(jnp.float32)).astype(jnp.bfloat16)
    q = jnp.dot(normed, w_qkv[0], preferred_element_type=jnp.float32).astype(jnp.bfloat16)
    k = jnp.dot(normed, w_qkv[1], preferred_element_type=jnp.float32).astype(jnp.bfloat16)
    v = jnp.dot(normed, w_qkv[2], preferred_element_type=jnp.float32).astype(jnp.bfloat16)
    joined = jnp.concatenate([k, v], axis=1)
    behind = shifted(joined[-2 * BLOCK :], "seq", 1)
    before = shifted(joined[:BLOCK], "seq", -1)
    keys_values = jnp.concatenate([behind, joined, before], axis=0)
    attended = banded_attention(q, keys_values, seg_ext, seg_plus, HEAD_DIM)
    return jnp.dot(attended, w_out, preferred_element_type=jnp.float32)


def shards(state, condition, time_vector, norm_gain, w_qkv, w_out, utterance_ids):
    seg_plus = utterance_ids + 1
    seg_behind = shifted(seg_plus[-2 * BLOCK :], "seq", 1)
    seg_before = shifted(seg_plus[:BLOCK], "seq", -1)
    seg_ext = jnp.concatenate([seg_behind, seg_plus, seg_before], axis=0)
    x_full = state.astype(jnp.float32)
    parts = lax.axis_size("mp")
    share = x_full.shape[1] // parts
    for step in range(2):
        terms = velocity_terms(
            x_full, condition, time_vector, norm_gain, w_qkv, w_out, seg_ext, seg_plus, 0.5 * step
        )
        total = lax.psum(terms.astype(jnp.bfloat16), "mp").astype(jnp.float32)
        x_full = x_full + 0.5 * total
    mine = lax.dynamic_slice_in_dim(x_full, lax.axis_index("mp") * share, share, 1)
    return mine.astype(jnp.bfloat16)


def solution(mesh):
    in_specs = (
        P("seq", None),
        P("seq", None),
        P(),
        P(),
        P(None, None, "mp"),
        P("mp", None),
        P("seq"),
    )
    out_specs = P("seq", "mp")
    return jax.shard_map(shards, mesh=mesh, in_specs=in_specs, out_specs=out_specs, check_vma=False)
```

profile of v0, /device:TPU:8, one launch (start us, length us, event | category | flops | bytes accessed | tf_op | source)
XLA Modules:
  0.0 186.1 jit_solution(15630633197445109567)
XLA Ops:
  0.0 0.8 convert_multiply_fusion
  0.8 2.1 %multiply_reduce_fusion.1 = f32[480]{0:T(512)S(1)} fusion(bf16[480,1024]{1,0:T(8,128)(2,1)} %param.8, bf16[480,1024]{1,0:T(8,128)(2,1)} %param.7, f32[1024]{0:T(1024)S(1)} %get-tuple-element.10), kind=kLoop, calls=%fused_computation.50 | loop fusion | flops 2948640 | bytes 1972096 | tf_op jit(solution)/shard_map/reduce_sum | solution.py:44
  2.9 0.7 convert_element_type.75
  3.6 0.4 multiply_convert_fusion.1
  4.1 0.0 slice-start.1
  4.1 3.0 %fusion.38 = bf16[480,1024]{1,0:T(8,128)(2,1)S(1)} fusion(bf16[480,1024]{1,0:T(8,128)(2,1)S(1)} %multiply_convert_fusion.1, bf16[3,1024,1024]{2,1,0:T(8,128)(2,1)} %param.11), kind=kOutput, calls=%fused_computation.59 | convolution fusion | flops 1007124480 | bytes 4063232 | tf_op jit(solution)/shard_map/dot_general | solution.py:47
  7.1 0.1 slice-done.1
  7.2 1.2 fusion.44
  8.4 0.0 copy-start.6
  8.4 0.0 copy-start.10
  8.5 1.9 %collective-permute-start = (bf16[48,2048]{1,0:T(8,128)(2,1)S(1)}, bf16[48,2048]{1,0:T(8,128)(2,1)S(1)}, u32[]{:S(2)}, u32[]{:S(2)}) collective-permute-start(bf16[48,2048]{1,0:T(8,128)(2,1)S(1)} %pad_maximum_fusion.3), channel_id=1, source_target_pairs={{0,1},{1,2},{2,3},{3,4},{4,5},{5,6},{6,7},{7,8},{8,9},{9,10},{10,1... | collective-permute-start | bytes 589832 | tf_op jit(solution)/shard_map/ppermute | solution.py:13
  10.4 0.6 pad_maximum_fusion.5
  11.1 5.4 %collective-permute-start.1 = (bf16[24,2048]{1,0:T(8,128)(2,1)}, bf16[24,2048]{1,0:T(8,128)(2,1)}, u32[]{:S(2)}, u32[]{:S(2)}) collective-permute-start(bf16[24,2048]{1,0:T(8,128)(2,1)} %pad_maximum_fusion.5), channel_id=1, source_target_pairs={{1,0},{2,1},{3,2},{4,3},{5,4},{6,5},{7,6},{8,7},{9,8},{10,9},{11,1... | collective-permute-start | bytes 294920 | tf_op jit(solution)/shard_map/ppermute | solution.py:13
  16.5 0.1 slice.47
  16.6 1.9 %collective-permute-start.2 = (s32[48]{0:T(128)S(1)}, s32[48]{0:T(128)S(1)}, u32[]{:S(2)}, u32[]{:S(2)}) collective-permute-start(s32[48]{0:T(128)S(1)} %slice.47), channel_id=1, source_target_pairs={{0,1},{1,2},{2,3},{3,4},{4,5},{5,6},{6,7},{7,8},{8,9},{9,10},{10,1... | collective-permute-start | bytes 584 | tf_op jit(solution)/shard_map/ppermute | solution.py:13
  18.5 5.6 %collective-permute-start.3 = (s32[24]{0:T(128)S(1)}, s32[24]{0:T(128)S(1)}, u32[]{:S(2)}, u32[]{:S(2)}) collective-permute-start(s32[24]{0:T(128)S(1)} %slice.48), channel_id=1, source_target_pairs={{1,0},{2,1},{3,2},{4,3},{5,4},{6,5},{7,6},{8,7},{9,8},{10,9},{11,1... | collective-permute-start | bytes 296 | tf_op jit(solution)/shard_map/ppermute | solution.py:13
  24.2 2.2 %fusion.50 = bf16[480,1024]{1,0:T(8,128)(2,1)} fusion(bf16[480,1024]{1,0:T(8,128)(2,1)S(1)} %multiply_convert_fusion.1, bf16[3,1024,1024]{2,1,0:T(8,128)(2,1)S(1)} %bitcast.64), kind=kOutput, calls=%fused_computation.63 | convolution fusion | flops 1007124480 | bytes 4063232 | tf_op jit(solution)/shard_map/dot_general | solution.py:46
  26.4 0.1 compare_select_fusion
  26.4 0.1 reshape.103
  26.5 0.7 eq.12
  27.2 3.8 %reshape.94 = bf16[20,24,16,64]{3,2,1,0:T(8,128)(2,1)} reshape(bf16[480,1024]{1,0:T(8,128)(2,1)} %fusion.50) | data formatting | bytes 1966080 | tf_op jit(solution)/shard_map/reshape | solution.py:27
  31.0 0.0 collective-permute-done.3
  31.0 0.0 collective-permute-done.2
  31.0 0.1 pad_add_fusion
  31.1 7.2 %gather_fusion.1 = s32[1920]{0:T(1024)S(1)} fusion(s32[552]{0:T(1024)S(1)} %pad_add_fusion, s32[2048]{0:T(1024)S(1)} %pad_clamp_fusion), kind=kCustom, calls=%fused_computation.1 | custom fusion | bytes 23040 | tf_op jit(solution)/shard_map/gather | solution.py:31
  38.3 0.7 reshape.110
  39.0 0.9 broadcast_compare_fusion
  39.9 0.0 collective-permute-done.1
  39.9 0.0 collective-permute-done
  39.9 3.3 %pad_maximum_fusion = bf16[552,2048]{1,0:T(8,128)(2,1)} fusion(bf16[24,2048]{1,0:T(8,128)(2,1)} %collective-permute-done.1, bf16[480,1024]{1,0:T(8,128)(2,1)} %copy-done.6, bf16[480,1024]{1,0:T(8,128)(2,1)} %copy-done.5, bf16[48,2048]{1,0:T(8,128)(2,1)S(1)} %collective-permute-done), kind=kLoop, calls=%fused_computation.16 | loop fusion | flops 9043968 | bytes 4521984 | tf_op jit(solution)/shard_map/concatenate | solution.py:52
  43.1 18.2 %gather_fusion = bf16[1920,2048]{1,0:T(8,128)(2,1)} fusion(bf16[552,2048]{1,0:T(8,128)(2,1)} %pad_maximum_fusion, s32[2048]{0:T(1024)S(1)} %pad_clamp_fusion), kind=kCustom, calls=%fused_computation | custom fusion | bytes 15736320 | tf_op jit(solution)/shard_map/gather | solution.py:24
  61.3 6.0 %fusion.61 = (bf16[20,96,1024]{2,1,0:T(8,128)(2,1)}, bf16[20,96,1024]{2,1,0:T(8,128)(2,1)}) fusion(bf16[20,96,2048]{2,1,0:T(8,128)(2,1)} %bitcast.58), kind=kLoop, calls=%fused_computation.86 | loop fusion | bytes 15728640 | tf_op jit(solution)/shard_map/slice | solution.py:25
  67.3 7.2 %copy.23 = bf16[20,96,1024]{1,2,0:T(8,128)(2,1)} copy(bf16[20,96,1024]{2,1,0:T(8,128)(2,1)} %get-tuple-element.7) | data formatting | bytes 7864320
  74.5 7.2 %copy.22 = bf16[20,96,1024]{1,2,0:T(8,128)(2,1)} copy(bf16[20,96,1024]{2,1,0:T(8,128)(2,1)} %get-tuple-element.8) | data formatting | bytes 7864320
  81.7 4.6 %fusion.22 = f32[20,16,24,96]{3,2,1,0:T(8,128)S(1)} fusion(bf16[20,96,16,64]{1,3,2,0:T(8,128)(2,1)} %bitcast.59, bf16[20,24,16,64]{3,2,1,0:T(8,128)(2,1)} %reshape.94), kind=kOutput, calls=%fused_computation.36 | convolution fusion | flops 94371840 | bytes 7864320 | tf_op jit(solution)/shard_map/bqhe,bkhe->bhqk/dot_general | solution.py:29
  86.3 4.6 %fusion.62 = (f32[20,16,24]{2,1,0:T(8,128)S(1)}, f32[20,16,24,96]{3,2,1,0:T(8,128)S(1)}) fusion(f32[20,16,24,96]{3,2,1,0:T(8,128)S(1)} %fusion.22, pred[20,24,96]{2,1,0:T(8,128)(4,1)S(1)} %broadcast_compare_fusion), kind=kOutput, calls=%fused_computation.87 | output fusion | flops 4423775 | bytes 5975040 | tf_op jit(solution)/shard_map/sub | solution.py:36
  90.8 3.1 %convert_bitcast_fusion.1 = bf16[20,24,16,64]{3,1,2,0:T(8,128)(2,1)S(1)} fusion(bf16[20,96,16,64]{1,3,2,0:T(8,128)(2,1)S(1)} %bitcast.61, f32[20,16,24,96]{3,2,1,0:T(8,128)S(1)} %get-tuple-element.12, f32[20,16,24]{2,1,0:T(8,128)S(1)} %get-tuple-element.11), kind=kOutput, calls=%fused_computation.43 | convolution fusion | flops 96337920 | bytes 7895040 | tf_op jit(solution)/shard_map/bhqk,bkhe->bqhe/dot_general | solution.py:38
  94.0 1.7 copy.17
  95.7 3.9 %reshape.96 = bf16[480,1024]{1,0:T(8,128)(2,1)} reshape(bf16[20,24,16,64]{3,2,1,0:T(8,128)(2,1)} %copy.17) | data formatting | bytes 1966080 | tf_op jit(solution)/shard_map/reshape | solution.py:39
  99.6 0.0 slice-start.3
  99.7 3.3 %multiply_reduce_fusion = (f32[480]{0:T(512)S(1)}, bf16[480,1024]{1,0:T(8,128)(2,1)S(1)}) fusion(bf16[480,1024]{1,0:T(8,128)(2,1)S(1)} %copy-done.1, bf16[480,1024]{1,0:T(8,128)(2,1)} %param.7, f32[1024]{0:T(1024)S(1)} %get-tuple-element.9, bf16[480,1024]{1,0:T(8,128)(2,1)} %reshape.96, bf16[1024,1024]{1,0:T(8,128)(2,1)S(1)} %copy-done), kind=kOutput, calls=%fused_computation.42 | convolution fusion | flops 1011547648 | bytes 6035328 | tf_op jit(solution)/shard_map/dot_general | solution.py:54
  102.9 0.0 copy-start.9
  103.0 0.6 multiply_convert_fusion
  103.6 1.2 fusion.41
  104.8 1.2 fusion.47
  106.1 0.9 copy-done.7
  107.0 0.6 pad_maximum_fusion.4
  107.6 1.9 %collective-permute-start.4 = (bf16[48,2048]{1,0:T(8,128)(2,1)S(1)}, bf16[48,2048]{1,0:T(8,128)(2,1)S(1)}, u32[]{:S(2)}, u32[]{:S(2)}) collective-permute-start(bf16[48,2048]{1,0:T(8,128)(2,1)S(1)} %pad_maximum_fusion.2), channel_id=1, source_target_pairs={{0,1},{1,2},{2,3},{3,4},{4,5},{5,6},{6,7},{7,8},{8,9},{9,10},{10,1... | collective-permute-start | bytes 589832 | tf_op jit(solution)/shard_map/ppermute | solution.py:13
  109.5 5.4 %collective-permute-start.5 = (bf16[24,2048]{1,0:T(8,128)(2,1)}, bf16[24,2048]{1,0:T(8,128)(2,1)}, u32[]{:S(2)}, u32[]{:S(2)}) collective-permute-start(bf16[24,2048]{1,0:T(8,128)(2,1)} %pad_maximum_fusion.4), channel_id=1, source_target_pairs={{1,0},{2,1},{3,2},{4,3},{5,4},{6,5},{7,6},{8,7},{9,8},{10,9},{11,1... | collective-permute-start | bytes 294920 | tf_op jit(solution)/shard_map/ppermute | solution.py:13
  115.0 2.1 %fusion.53 = bf16[480,1024]{1,0:T(8,128)(2,1)} fusion(bf16[480,1024]{1,0:T(8,128)(2,1)S(1)} %multiply_convert_fusion, bf16[3,1024,1024]{2,1,0:T(8,128)(2,1)S(1)} %bitcast.66), kind=kOutput, calls=%fused_computation.64 | convolution fusion | flops 1007124480 | bytes 4063232 | tf_op jit(solution)/shard_map/dot_general | solution.py:46
  117.1 3.8 %reshape.98 = bf16[20,24,16,64]{3,2,1,0:T(8,128)(2,1)} reshape(bf16[480,1024]{1,0:T(8,128)(2,1)} %fusion.53) | data formatting | bytes 1966080 | tf_op jit(solution)/shard_map/reshape | solution.py:27
  120.9 0.0 collective-permute-done.5
  120.9 0.0 collective-permute-done.4
  120.9 3.0 %pad_maximum_fusion.1 = bf16[552,2048]{1,0:T(8,128)(2,1)} fusion(bf16[24,2048]{1,0:T(8,128)(2,1)} %collective-permute-done.5, bf16[480,1024]{1,0:T(8,128)(2,1)} %copy-done.7, bf16[480,1024]{1,0:T(8,128)(2,1)S(1)} %fusion.41, bf16[48,2048]{1,0:T(8,128)(2,1)S(1)} %collective-permute-done.4), kind=kLoop, calls=%fused_computation.17 | loop fusion | flops 9043968 | bytes 4521984 | tf_op jit(solution)/shard_map/concatenate | solution.py:52
  123.9 18.2 %gather_fusion.2 = bf16[1920,2048]{1,0:T(8,128)(2,1)} fusion(bf16[552,2048]{1,0:T(8,128)(2,1)} %pad_maximum_fusion.1, s32[2048]{0:T(1024)S(1)} %pad_clamp_fusion), kind=kCustom, calls=%fused_computation.2 | custom fusion | bytes 15736320 | tf_op jit(solution)/shard_map/gather | solution.py:24
  142.1 5.8 %fusion.60 = (bf16[20,96,1024]{2,1,0:T(8,128)(2,1)}, bf16[20,96,1024]{2,1,0:T(8,128)(2,1)}) fusion(bf16[20,96,2048]{2,1,0:T(8,128)(2,1)} %bitcast.57), kind=kLoop, calls=%fused_computation.85 | loop fusion | bytes 15728640 | tf_op jit(solution)/shard_map/slice | solution.py:25
  147.8 7.2 %copy.25 = bf16[20,96,1024]{1,2,0:T(8,128)(2,1)} copy(bf16[20,96,1024]{2,1,0:T(8,128)(2,1)} %get-tuple-element.5) | data formatting | bytes 7864320
  155.0 4.6 %fusion.20 = f32[20,16,24,96]{3,2,1,0:T(8,128)S(1)} fusion(bf16[20,96,16,64]{1,3,2,0:T(8,128)(2,1)} %bitcast.60, bf16[20,24,16,64]{3,2,1,0:T(8,128)(2,1)} %reshape.98), kind=kOutput, calls=%fused_computation.34 | convolution fusion | flops 94371840 | bytes 7864320 | tf_op jit(solution)/shard_map/bqhe,bkhe->bhqk/dot_general | solution.py:29
  159.6 3.2 %fusion.63 = (f32[20,16,24]{2,1,0:T(8,128)S(1)}, f32[20,16,24,96]{3,2,1,0:T(8,128)}) fusion(f32[20,16,24,96]{3,2,1,0:T(8,128)S(1)} %fusion.20, pred[20,24,96]{2,1,0:T(8,128)(4,1)S(1)} %broadcast_compare_fusion), kind=kOutput, calls=%fused_computation.88 | output fusion | flops 4423775 | bytes 5975040 | tf_op jit(solution)/shard_map/sub | solution.py:36
  162.9 7.2 %copy.24 = bf16[20,96,1024]{1,2,0:T(8,128)(2,1)} copy(bf16[20,96,1024]{2,1,0:T(8,128)(2,1)} %get-tuple-element.6) | data formatting | bytes 7864320
  170.1 6.6 %convert_bitcast_fusion = bf16[20,24,16,64]{3,1,2,0:T(8,128)(2,1)S(1)} fusion(bf16[20,96,16,64]{1,3,2,0:T(8,128)(2,1)} %bitcast.62, f32[20,16,24,96]{3,2,1,0:T(8,128)} %get-tuple-element.16, f32[20,16,24]{2,1,0:T(8,128)S(1)} %get-tuple-element.15), kind=kOutput, calls=%fused_computation.39 | convolution fusion | flops 96337920 | bytes 7895040 | tf_op jit(solution)/shard_map/bhqk,bkhe->bqhe/dot_general | solution.py:38
  176.6 1.7 copy.21
  178.4 4.0 %reshape.100 = bf16[480,1024]{1,0:T(8,128)(2,1)} reshape(bf16[20,24,16,64]{3,2,1,0:T(8,128)(2,1)} %copy.21) | data formatting | bytes 1966080 | tf_op jit(solution)/shard_map/reshape | solution.py:39
  182.4 3.7 %add_convert_fusion = bf16[480,1024]{1,0:T(8,128)(2,1)} fusion(bf16[480,1024]{1,0:T(8,128)(2,1)} %copy-done.9, bf16[480,1024]{1,0:T(8,128)(2,1)S(1)} %copy-done.4, bf16[480,1024]{1,0:T(8,128)(2,1)} %reshape.100, bf16[1024,1024]{1,0:T(8,128)(2,1)S(1)} %copy-done), kind=kOutput, calls=%fused_computation.38 | convolution fusion | flops 1011056640 | bytes 6029312 | tf_op jit(solution)/shard_map/dot_general | solution.py:54
  (33 shorter events, 0.1 us)
Async XLA Ops:
  0.0 99.6 %copy-start = (bf16[1024,1024]{1,0:T(8,128)(2,1)S(1)}, bf16[1024,1024]{1,0:T(8,128)(2,1)}, u32[]{:S(2)}) copy-start(bf16[1024,1024]{1,0:T(8,128)(2,1)} %param.12) | copy-start | bytes 6291460
  0.0 3.6 %copy-start.2 = (bf16[480,1024]{1,0:T(8,128)(2,1)S(1)}, bf16[480,1024]{1,0:T(8,128)(2,1)}, u32[]{:S(2)}) copy-start(bf16[480,1024]{1,0:T(8,128)(2,1)} %param.7) | copy-start | bytes 2949124
  0.0 3.6 %copy-start.1 = (bf16[480,1024]{1,0:T(8,128)(2,1)S(1)}, bf16[480,1024]{1,0:T(8,128)(2,1)}, u32[]{:S(2)}) copy-start(bf16[480,1024]{1,0:T(8,128)(2,1)} %param.8) | copy-start | bytes 2949124
  3.6 3.5 %slice-start = ((s8[6291456]{0:T(1024)(128)(4,1)}), s8[4194304]{0:T(1024)(128)(4,1)S(1)}, s32[]{:S(2)}) async-start(s8[6291456]{0:T(1024)(128)(4,1)} %bitcast.63), calls=%async_computation | async-start | bytes 8388608
  4.1 3.2 %slice-start.1 = ((s8[6291456]{0:T(1024)(128)(4,1)}), s8[2097152]{0:T(1024)(128)(4,1)S(1)}, s32[]{:S(2)}) async-start(s8[6291456]{0:T(1024)(128)(4,1)} %bitcast.63), calls=%async_computation.1 | async-start | bytes 4194304
  7.2 3.2 %copy-start.5 = (bf16[480,1024]{1,0:T(8,128)(2,1)}, bf16[480,1024]{1,0:T(8,128)(2,1)S(1)}, u32[]{:S(2)}) copy-start(bf16[480,1024]{1,0:T(8,128)(2,1)S(1)} %fusion.38) | copy-start | bytes 2949124
  8.4 17.9 %copy-start.6 = (bf16[480,1024]{1,0:T(8,128)(2,1)}, bf16[480,1024]{1,0:T(8,128)(2,1)S(1)}, u32[]{:S(2)}) copy-start(bf16[480,1024]{1,0:T(8,128)(2,1)S(1)} %fusion.44) | copy-start | bytes 2949124
  8.4 8.1 %copy-start.10 = (s32[480]{0:T(512)S(1)}, s32[480]{0:T(512)}, u32[]{:S(2)}) copy-start(s32[480]{0:T(512)} %param.13) | copy-start | bytes 5764
  8.5 31.4 %collective-permute-start = (bf16[48,2048]{1,0:T(8,128)(2,1)S(1)}, bf16[48,2048]{1,0:T(8,128)(2,1)S(1)}, u32[]{:S(2)}, u32[]{:S(2)}) collective-permute-start(bf16[48,2048]{1,0:T(8,128)(2,1)S(1)} %pad_maximum_fusion.3), channel_id=1, source_target_pairs={{0,1},{1,2},{2,3},{3,4},{4,5},{5,6},{6,7},{7,8},{8,9},{9,10},{10,1... | collective-permute-start | bytes 589832 | tf_op jit(solution)/shard_map/ppermute | solution.py:13
  11.1 28.8 %collective-permute-start.1 = (bf16[24,2048]{1,0:T(8,128)(2,1)}, bf16[24,2048]{1,0:T(8,128)(2,1)}, u32[]{:S(2)}, u32[]{:S(2)}) collective-permute-start(bf16[24,2048]{1,0:T(8,128)(2,1)} %pad_maximum_fusion.5), channel_id=1, source_target_pairs={{1,0},{2,1},{3,2},{4,3},{5,4},{6,5},{7,6},{8,7},{9,8},{10,9},{11,1... | collective-permute-start | bytes 294920 | tf_op jit(solution)/shard_map/ppermute | solution.py:13
  16.6 14.4 %collective-permute-start.2 = (s32[48]{0:T(128)S(1)}, s32[48]{0:T(128)S(1)}, u32[]{:S(2)}, u32[]{:S(2)}) collective-permute-start(s32[48]{0:T(128)S(1)} %slice.47), channel_id=1, source_target_pairs={{0,1},{1,2},{2,3},{3,4},{4,5},{5,6},{6,7},{7,8},{8,9},{9,10},{10,1... | collective-permute-start | bytes 584 | tf_op jit(solution)/shard_map/ppermute | solution.py:13
  18.5 12.5 %collective-permute-start.3 = (s32[24]{0:T(128)S(1)}, s32[24]{0:T(128)S(1)}, u32[]{:S(2)}, u32[]{:S(2)}) collective-permute-start(s32[24]{0:T(128)S(1)} %slice.48), channel_id=1, source_target_pairs={{1,0},{2,1},{3,2},{4,3},{5,4},{6,5},{7,6},{8,7},{9,8},{10,9},{11,1... | collective-permute-start | bytes 296 | tf_op jit(solution)/shard_map/ppermute | solution.py:13
  86.3 4.6 %copy-start.8 = (bf16[20,96,1024]{1,2,0:T(8,128)(2,1)S(1)}, bf16[20,96,1024]{1,2,0:T(8,128)(2,1)}, u32[]{:S(2)}) copy-start(bf16[20,96,1024]{1,2,0:T(8,128)(2,1)} %copy.22) | copy-start | bytes 11796484
  99.6 4.0 %slice-start.2 = ((s8[6291456]{0:T(1024)(128)(4,1)}), s8[4194304]{0:T(1024)(128)(4,1)S(1)}, s32[]{:S(2)}) async-start(s8[6291456]{0:T(1024)(128)(4,1)} %bitcast.65), calls=%async_computation.2 | async-start | bytes 8388608
  99.6 3.3 %copy-start.3 = (bf16[480,1024]{1,0:T(8,128)(2,1)S(1)}, bf16[480,1024]{1,0:T(8,128)(2,1)}, u32[]{:S(2)}) copy-start(bf16[480,1024]{1,0:T(8,128)(2,1)} %param.7) | copy-start | bytes 2949124
  99.6 4.0 %slice-start.3 = ((s8[6291456]{0:T(1024)(128)(4,1)}), s8[2097152]{0:T(1024)(128)(4,1)S(1)}, s32[]{:S(2)}) async-start(s8[6291456]{0:T(1024)(128)(4,1)} %bitcast.65), calls=%async_computation.3 | async-start | bytes 4194304
  102.9 1.9 %copy-start.9 = (bf16[480,1024]{1,0:T(8,128)(2,1)}, bf16[480,1024]{1,0:T(8,128)(2,1)S(1)}, u32[]{:S(2)}) copy-start(bf16[480,1024]{1,0:T(8,128)(2,1)S(1)} %get-tuple-element.14) | copy-start | bytes 2949124
  106.0 0.9 copy-start.7
  107.6 13.3 %collective-permute-start.4 = (bf16[48,2048]{1,0:T(8,128)(2,1)S(1)}, bf16[48,2048]{1,0:T(8,128)(2,1)S(1)}, u32[]{:S(2)}, u32[]{:S(2)}) collective-permute-start(bf16[48,2048]{1,0:T(8,128)(2,1)S(1)} %pad_maximum_fusion.2), channel_id=1, source_target_pairs={{0,1},{1,2},{2,3},{3,4},{4,5},{5,6},{6,7},{7,8},{8,9},{9,10},{10,1... | collective-permute-start | bytes 589832 | tf_op jit(solution)/shard_map/ppermute | solution.py:13
  109.5 11.4 %collective-permute-start.5 = (bf16[24,2048]{1,0:T(8,128)(2,1)}, bf16[24,2048]{1,0:T(8,128)(2,1)}, u32[]{:S(2)}, u32[]{:S(2)}) collective-permute-start(bf16[24,2048]{1,0:T(8,128)(2,1)} %pad_maximum_fusion.4), channel_id=1, source_target_pairs={{1,0},{2,1},{3,2},{4,3},{5,4},{6,5},{7,6},{8,7},{9,8},{10,9},{11,1... | collective-permute-start | bytes 294920 | tf_op jit(solution)/shard_map/ppermute | solution.py:13
  178.4 4.0 %copy-start.4 = (bf16[480,1024]{1,0:T(8,128)(2,1)S(1)}, bf16[480,1024]{1,0:T(8,128)(2,1)}, u32[]{:S(2)}) copy-start(bf16[480,1024]{1,0:T(8,128)(2,1)} %param.7) | copy-start | bytes 2949124
where the time goes:
time: 187 us; the launch traced here: 186 us
  local copies, waits for them, and re-layouts  106 us (57%)
  matrix products  36.7 us (20%)
  starting transfers between devices  22.2 us (12%)
  other arithmetic  21 us (11%)
    gather x2, local copies, waits for them, and re-layouts, banded_attention(): window = keys_values[rows]  36.3 us
    unnamed x34, local copies, waits for them, and re-layouts  29.9 us
    ppermute x6, starting transfers between devices, shifted(): return lax.ppermute(shard, axis, pairs)  22.2 us
    slice x2, local copies, waits for them, and re-layouts, banded_attention(): k_rows = window[:, :, :width].reshape(nblocks, 4 * BLOCK, heads, head_dim)  11.7 us
    dot_general x2, matrix products, banded_attention(): jnp.einsum('bhqk,bkhe->bqhe', probs, v_rows, preferred_element_type=jnp.f...  9.69 us
    dot_general x2, matrix products, banded_attention(): jnp.einsum('bqhe,bkhe->bhqk', q_rows, k_rows, preferred_element_type=jnp....  9.13 us
    reshape x2, local copies, waits for them, and re-layouts, banded_attention(): return out.astype(jnp.bfloat16).reshape(frames, width)  7.98 us
    gather x2, local copies, waits for them, and re-layouts, banded_attention(): k_seg = seg_ext[rows]  7.88 us
  transfers between devices with their start and end apart: 6, of which 0 were waited for; matrix products, arithmetic and copies ran while one was open for 12% of the time, Pallas kernels for 0%

commit v1 on v0

v1 whole, which is shorter than its diff:
```python
import functools
import math

import jax
import jax.numpy as jnp
from jax import lax
from jax.experimental import pallas as pl
from jax.experimental.pallas import tpu as pltpu
from jax.sharding import PartitionSpec as P

HEAD_DIM = 64
BLOCK = 24
UNIT = 2 * BLOCK
BEHIND = 4 * BLOCK
AHEAD = 2 * BLOCK
WINDOW = 128
SPARE = WINDOW - 2 * UNIT
PAIR = 2 * HEAD_DIM
TILE = 256
F32 = jnp.float32
BF16 = jnp.bfloat16
NEG = -1e30


def shifted(shard, axis, by):
    count = lax.axis_size(axis)
    pairs = [(i, i + by) for i in range(count) if 0 <= i + by < count]
    return lax.ppermute(shard, axis, pairs)


def column_of(row):
    n = row.shape[1]
    same = lax.broadcasted_iota(jnp.int32, (n, n), 0) == lax.broadcasted_iota(jnp.int32, (n, n), 1)
    column = jnp.sum(jnp.where(same, row, 0.0), axis=1, keepdims=True)
    return jnp.broadcast_to(column, (n, 128))


def build_masks(behind_ref, ahead_ref, ids_ref, seg_ref, bias_ref):
    own = ids_ref.shape[1]
    seg_ref[0:BEHIND, :] = column_of(behind_ref[BEHIND : BEHIND + 1, 0:BEHIND].astype(F32))
    for at in range(0, own, 128):
        n = min(128, own - at)
        row = (ids_ref[:, at : at + n] + 1).astype(F32)
        seg_ref[BEHIND + at : BEHIND + at + n, :] = column_of(row)
    end = BEHIND + own
    seg_ref[end : end + AHEAD, :] = column_of(ahead_ref[AHEAD : AHEAD + 1, 0:AHEAD].astype(F32))
    end = end + AHEAD
    seg_ref[end : end + SPARE, :] = jnp.full((SPARE, 128), -1.0, F32)

    def one(unit, carry):
        start = pl.multiple_of(unit * UNIT, 16)
        window = seg_ref[pl.ds(pl.multiple_of(start - UNIT, 16), WINDOW), :]
        r = lax.broadcasted_iota(jnp.int32, (WINDOW, WINDOW), 0)
        c = lax.broadcasted_iota(jnp.int32, (WINDOW, WINDOW), 1)
        keys = jnp.sum(jnp.where(r == c, window, 0.0), axis=0, keepdims=True)
        queries = seg_ref[pl.ds(start, UNIT), :]
        row = lax.broadcasted_iota(jnp.int32, (UNIT, WINDOW), 0)
        col = lax.broadcasted_iota(jnp.int32, (UNIT, WINDOW), 1)
        first = jnp.where(row < BLOCK, 0, BLOCK)
        band = (col >= first) & (col < first + 4 * BLOCK)
        bias_ref[unit] = jnp.where(band & (queries == keys), 0.0, NEG)
        return carry

    lax.fori_loop(1, bias_ref.shape[0], one, 0)


def normalize(h_ref, normed_ref, gain, first, last):
    rows = UNIT

    def one(i, carry):
        at = pl.ds(pl.multiple_of(first + i * rows, 16), rows)
        h = h_ref[at, :]
        scale = lax.rsqrt(jnp.mean(h * h, axis=-1, keepdims=True) + 1e-06)
        normed_ref[at, :] = (h * scale * gain).astype(BF16)
        return carry

    lax.fori_loop(0, (last - first) // rows, one, 0)


def project(normed_ref, w_ref, which, first, last, outs):
    width = w_ref.shape[2]
    tile = min(TILE, width)
    for at in range(0, width, tile):
        out = jnp.dot(
            normed_ref[first:last, :], w_ref[which, :, at : at + tile], preferred_element_type=F32
        ).astype(BF16)
        if len(outs) == 1:
            outs[0][first:last, at : at + tile] = out
        else:
            lane = lax.broadcasted_iota(jnp.int32, out.shape, 1) % PAIR
            zero = jnp.zeros_like(out)
            outs[0][first:last, at : at + tile] = jnp.where(lane < HEAD_DIM, out, zero)
            outs[1][first:last, at : at + tile] = jnp.where(lane < HEAD_DIM, zero, out)


def attend(q_ref, k_refs, v_refs, att_ref, bias_ref, first, last):
    pairs = q_ref.shape[1] // PAIR
    lane = lax.broadcasted_iota(jnp.int32, (WINDOW, PAIR), 1)
    ones = [(lane < HEAD_DIM).astype(BF16), (lane >= HEAD_DIM).astype(BF16)]
    factor = HEAD_DIM**-0.5 * math.log2(math.e)

    def one(unit, carry):
        start = pl.multiple_of(unit * UNIT, 16)
        rows = pl.ds(start, UNIT)
        window = pl.ds(pl.multiple_of(start - UNIT, 16), WINDOW)
        bias = bias_ref[unit]
        bias = jnp.concatenate([bias, bias], axis=1)
        scores = []
        for p in range(pairs):
            lanes = slice(p * PAIR, (p + 1) * PAIR)
            keys = jnp.concatenate([k_refs[0][window, lanes], k_refs[1][window, lanes]], axis=0)
            scores.append(
                lax.dot_general(
                    q_ref[rows, lanes], keys, (((1,), (1,)), ((), ())), preferred_element_type=F32
                )
            )
        probs = []
        for p in range(pairs):
            s = scores[p] * factor + bias
            halves = []
            for half in (s[:, :WINDOW], s[:, WINDOW:]):
                top = jnp.max(half, axis=-1, keepdims=True)
                halves.append(jnp.exp2(half - top).astype(BF16))
            probs.append(jnp.concatenate(halves, axis=1))
        for p in range(pairs):
            lanes = slice(p * PAIR, (p + 1) * PAIR)
            values = jnp.concatenate(
                [
                    jnp.concatenate([v_refs[0][window, lanes], ones[0]], axis=1),
                    jnp.concatenate([v_refs[1][window, lanes], ones[1]], axis=1),
                ],
                axis=0,
            )
            out = jnp.dot(probs[p], values, preferred_element_type=F32)
            att_ref[rows, lanes] = (out[:, :PAIR] / out[:, PAIR:]).astype(BF16)
        return carry

    lax.fori_loop(first, last, one, 0)


def clear_spare(refs):
    for ref in refs:
        ref[ref.shape[0] - SPARE :, :] = jnp.zeros((SPARE, ref.shape[1]), ref.dtype)


def both_steps(
    state_ref, cond_ref, time_ref, gain_ref, behind_ref, ahead_ref, ids_ref, wqkv_hbm, wout_hbm,
    out_ref,
    wqkv, wout, h_ref, normed_ref, q_ref, ka_ref, kb_ref, va_ref, vb_ref, att_ref, seg_ref, bias_ref,
    sems,
):
    own = state_ref.shape[0]
    total = BEHIND + own + AHEAD
    k_refs, v_refs = (ka_ref, kb_ref), (va_ref, vb_ref)
    copies = [pltpu.make_async_copy(wqkv_hbm.at[i], wqkv.at[i], sems.at[i]) for i in (0, 1, 2)]
    copies.append(pltpu.make_async_copy(wout_hbm, wout, sems.at[3]))
    for which in (1, 2, 0, 3):
        copies[which].start()
    gain = gain_ref[...].astype(F32)
    half_time = 0.5 * time_ref[...].astype(F32)

    h_ref[0:BEHIND, :] = behind_ref[0:BEHIND, :].astype(F32)
    h_ref[BEHIND : BEHIND + own, :] = state_ref[...].astype(F32) + cond_ref[...].astype(F32)
    h_ref[BEHIND + own : total, :] = ahead_ref[0:AHEAD, :].astype(F32)
    build_masks(behind_ref, ahead_ref, ids_ref, seg_ref, bias_ref)
    clear_spare(k_refs + v_refs)

    normalize(h_ref, normed_ref, gain, 0, total)
    copies[1].wait()
    project(normed_ref, wqkv, 1, 0, total, k_refs)
    copies[2].wait()
    project(normed_ref, wqkv, 2, 0, total, v_refs)
    copies[0].wait()
    project(normed_ref, wqkv, 0, UNIT, total, [q_ref])
    attend(q_ref, k_refs, v_refs, att_ref, bias_ref, 1, total // UNIT)
    copies[3].wait()
    depth = wout.shape[1]
    for at in range(0, depth, TILE):
        cols = slice(at, at + TILE)
        moved = jnp.dot(att_ref[UNIT:total, :], wout[:, cols], preferred_element_type=F32)
        h_ref[UNIT:total, cols] = h_ref[UNIT:total, cols] + 0.5 * moved + half_time[:, cols]

    normalize(h_ref, normed_ref, gain, UNIT, total)
    project(normed_ref, wqkv, 1, UNIT, total, k_refs)
    project(normed_ref, wqkv, 2, UNIT, total, v_refs)
    project(normed_ref, wqkv, 0, BEHIND, BEHIND + own, [q_ref])
    attend(q_ref, k_refs, v_refs, att_ref, bias_ref, BEHIND // UNIT, (BEHIND + own) // UNIT)
    for at in range(0, depth, TILE):
        cols = slice(at, at + TILE)
        moved = jnp.dot(att_ref[BEHIND : BEHIND + own, :], wout[:, cols], preferred_element_type=F32)
        x = h_ref[BEHIND : BEHIND + own, cols] - cond_ref[:, cols].astype(F32) - half_time[:, cols]
        out_ref[:, cols] = (x + 0.5 * moved).astype(BF16)


def one_step(
    final, h_ref, gain_ref, behind_ref, ahead_ref, ids_ref, wqkv, wout,
    out_ref,
    normed_ref, q_ref, ka_ref, kb_ref, va_ref, vb_ref, att_ref, seg_ref, bias_ref,
):
    own = ids_ref.shape[1]
    total = BEHIND + own + AHEAD
    k_refs, v_refs = (ka_ref, kb_ref), (va_ref, vb_ref)
    kv_first = UNIT if final else 0
    first, last = (BEHIND, BEHIND + own) if final else (UNIT, total)
    build_masks(behind_ref, ahead_ref, ids_ref, seg_ref, bias_ref)
    clear_spare(k_refs + v_refs)
    normalize(h_ref, normed_ref, gain_ref[...].astype(F32), kv_first, total)
    project(normed_ref, wqkv, 1, kv_first, total, k_refs)
    project(normed_ref, wqkv, 2, kv_first, total, v_refs)
    project(normed_ref, wqkv, 0, first, last, [q_ref])
    attend(q_ref, k_refs, v_refs, att_ref, bias_ref, first // UNIT, last // UNIT)
    for at in range(0, wout.shape[1], TILE):
        cols = slice(at, at + TILE)
        out_ref[:, cols] = jnp.dot(
            att_ref[first:last, :], wout[:, cols], preferred_element_type=F32
        ).astype(BF16)


def work_shapes(own, depth, width):
    total = BEHIND + own + AHEAD
    return (
        [pltpu.VMEM((total, depth), BF16), pltpu.VMEM((total, width), BF16)]
        + [pltpu.VMEM((total + SPARE, width), BF16)] * 4
        + [
            pltpu.VMEM((total, width), BF16),
            pltpu.VMEM((total + SPARE, 128), F32),
            pltpu.VMEM((total // UNIT, UNIT, WINDOW), F32),
        ]
    )


def shards(state, condition, time_vector, norm_gain, w_qkv, w_out, utterance_ids):
    own, depth = state.shape
    width = w_qkv.shape[2]
    total = BEHIND + own + AHEAD
    parts = lax.axis_size("mp")
    gain = norm_gain.reshape(1, depth)
    ids = utterance_ids.reshape(1, own)

    def edge(rows, by):
        hidden = state[rows].astype(F32) + condition[rows].astype(F32)
        numbers = (utterance_ids[rows] + 1).astype(BF16)[None, :]
        numbers = jnp.pad(numbers, ((0, 15), (0, depth - numbers.shape[1])))
        return shifted(jnp.concatenate([hidden.astype(BF16), numbers], axis=0), "seq", by)

    behind = edge(slice(own - BEHIND, own), 1)
    ahead = edge(slice(0, AHEAD), -1)
    vmem = pl.BlockSpec(memory_space=pltpu.VMEM)
    if parts == 1:
        hbm = pl.BlockSpec(memory_space=pl.ANY)
        return pl.pallas_call(
            both_steps,
            out_shape=jax.ShapeDtypeStruct((own, depth), BF16),
            in_specs=[vmem] * 7 + [hbm] * 2,
            out_specs=vmem,
            scratch_shapes=[
                pltpu.VMEM(w_qkv.shape, BF16),
                pltpu.VMEM(w_out.shape, BF16),
                pltpu.VMEM((total, depth), F32),
            ]
            + work_shapes(own, depth, width)
            + [pltpu.SemaphoreType.DMA((4,))],
            compiler_params=pltpu.CompilerParams(vmem_limit_bytes=40 * 2**20),
        )(state, condition, time_vector.reshape(1, depth), gain, behind, ahead, ids, w_qkv, w_out)

    def terms(h, final):
        rows = own if final else total - UNIT
        mine = pl.pallas_call(
            functools.partial(one_step, final),
            out_shape=jax.ShapeDtypeStruct((rows, depth), BF16),
            in_specs=[vmem] * 7,
            out_specs=vmem,
            scratch_shapes=work_shapes(own, depth, width),
            compiler_params=pltpu.CompilerParams(vmem_limit_bytes=40 * 2**20),
        )(h, gain, behind, ahead, ids, w_qkv, w_out)
        return lax.psum(mine, "mp").astype(F32)

    start = state.astype(F32)
    h = jnp.concatenate(
        [behind[:BEHIND].astype(F32), start + condition.astype(F32), ahead[:AHEAD].astype(F32)]
    )
    velocity = terms(h, False)
    later = jnp.pad(velocity, ((UNIT, 0), (0, 0))) * 0.5 + 0.5 * time_vector.astype(F32)
    x = start + 0.5 * velocity[UNIT : UNIT + own] + 0.5 * terms(h + later, True)
    share = depth // parts
    mine = lax.dynamic_slice_in_dim(x, lax.axis_index("mp") * share, share, 1)
    return mine.astype(BF16)


def solution(mesh):
    in_specs = (
        P("seq", None),
        P("seq", None),
        P(),
        P(),
        P(None, None, "mp"),
        P("mp", None),
        P("seq"),
    )
    out_specs = P("seq", "mp")
    return jax.shard_map(shards, mesh=mesh, in_specs=in_specs, out_specs=out_specs, check_vma=False)
```

time: 187 us -> 50.7 us (0.27)
  the two profiles are of different devices: /device:TPU:8 before, /device:TPU:15 now
where the time goes in v1:
time: 50.7 us; the launch traced here: 50.2 us
  Pallas kernels  27.5 us (54%)
  local copies, waits for them, and re-layouts  8.83 us (17%)
  starting transfers between devices  5.6 us (11%)
  waiting for transfers between devices  4.78 us (9%)
  other arithmetic  3.44 us (7%)
    pallas_call x1, Pallas kernels, shards(): pl.pallas_call(both_steps, out_shape=jax.ShapeDtypeStruct((own, depth), B...  27.5 us
    unnamed x10, local copies, waits for them, and re-layouts  7.46 us
    ppermute x2, starting transfers between devices, shifted(): return lax.ppermute(shard, axis, pairs)  5.6 us
    ppermute x2, waiting for transfers between devices, shifted(): return lax.ppermute(shard, axis, pairs)  4.78 us
    convert_element_type x2, other arithmetic, edge(): hidden.astype(BF16)  2.03 us
    broadcast_in_dim x2, other arithmetic, edge(): numbers = (utterance_ids[rows] + 1).astype(BF16)[None, :]  1.38 us
  transfers between devices with their start and end apart: 2, of which 1 were waited for; matrix products, arithmetic and copies ran while one was open for 6% of the time, Pallas kernels for 0%

profile of v1, /device:TPU:15, one launch (start us, length us, event | category | flops | bytes accessed | tf_op | source)
XLA Modules:
  0.0 50.2 jit_solution(12907167580831177575)
XLA Ops:
  0.0 0.7 %convert_bitcast_fusion.1 = bf16[1,96]{1,0:T(2,128)(2,1)S(1)} fusion(s32[480]{0:T(512)} %param.13), kind=kLoop, calls=%fused_computation.9 | loop fusion | flops 192 | bytes 576 | tf_op jit(solution)/shard_map/broadcast_in_dim | solution.py:242
  0.7 1.1 %add_convert_fusion = bf16[96,1024]{1,0:T(8,128)(2,1)S(1)} fusion(bf16[480,1024]{1,0:T(8,128)(2,1)} %cond_ref.1, bf16[480,1024]{1,0:T(8,128)(2,1)} %state_ref.1), kind=kLoop, calls=%fused_computation.2 | loop fusion | flops 393216 | bytes 589824 | tf_op jit(solution)/shard_map/convert_element_type | solution.py:244
  1.8 3.7 %collective-permute-start = (bf16[112,1024]{1,0:T(8,128)(2,1)S(1)}, bf16[112,1024]{1,0:T(8,128)(2,1)S(1)}, u32[]{:S(2)}, u32[]{:S(2)}) collective-permute-start(bf16[112,1024]{1,0:T(8,128)(2,1)S(1)} %fusion.2), channel_id=1, source_target_pairs={{0,1},{1,2},{2,3},{3,4},{4,5},{5,6},{6,7},{7,8},{8,9},{9,10},{10,1... | collective-permute-start | bytes 688136 | tf_op jit(solution)/shard_map/ppermute | solution.py:28
  5.5 0.7 %convert_bitcast_fusion = bf16[1,48]{1,0:T(2,128)(2,1)S(1)} fusion(s32[480]{0:T(512)} %param.13), kind=kLoop, calls=%fused_computation.8 | loop fusion | flops 96 | bytes 288 | tf_op jit(solution)/shard_map/broadcast_in_dim | solution.py:242
  6.2 1.0 %add_convert_fusion.1 = bf16[48,1024]{1,0:T(8,128)(2,1)S(1)} fusion(bf16[480,1024]{1,0:T(8,128)(2,1)} %cond_ref.1, bf16[480,1024]{1,0:T(8,128)(2,1)} %state_ref.1), kind=kLoop, calls=%fused_computation.6 | loop fusion | flops 196608 | bytes 294912 | tf_op jit(solution)/shard_map/convert_element_type | solution.py:244
  7.2 1.9 %collective-permute-start.1 = (bf16[64,1024]{1,0:T(8,128)(2,1)S(1)}, bf16[64,1024]{1,0:T(8,128)(2,1)S(1)}, u32[]{:S(2)}, u32[]{:S(2)}) collective-permute-start(bf16[64,1024]{1,0:T(8,128)(2,1)S(1)} %fusion.3), channel_id=1, source_target_pairs={{1,0},{2,1},{3,2},{4,3},{5,4},{6,5},{7,6},{8,7},{9,8},{10,9},{11,1... | collective-permute-start | bytes 393224 | tf_op jit(solution)/shard_map/ppermute | solution.py:28
  9.1 0.7 %reshape.9.time_ref = bf16[1,1024]{1,0:T(2,128)(2,1)S(1)} reshape(bf16[1024]{0:T(1024)(128)(2,1)} %param.9) | data formatting | bytes 4096 | tf_op jit(solution)/shard_map/reshape | solution.py:264
  9.8 0.7 %reshape.10.gain_ref = bf16[1,1024]{1,0:T(2,128)(2,1)S(1)} reshape(bf16[1024]{0:T(1024)(128)(2,1)} %param.10) | data formatting | bytes 4096 | tf_op jit(solution)/shard_map/reshape | solution.py:237
  10.5 4.8 %collective-permute-done.1.ahead_ref = bf16[64,1024]{1,0:T(8,128)(2,1)S(1)} collective-permute-done((bf16[64,1024]{1,0:T(8,128)(2,1)S(1)}, bf16[64,1024]{1,0:T(8,128)(2,1)S(1)}, u32[]{:S(2)}, u32[]{:S(2)}) %collective-permute-start.1) | collective-permute-done | bytes 131104 | tf_op jit(solution)/shard_map/ppermute | solution.py:28
  15.2 0.0 collective-permute-done.behind_ref
  15.2 0.0 copy-start
  15.2 2.8 %copy-done = bf16[3,1024,1024]{2,1,0:T(8,128)(2,1)S(1)} copy-done((bf16[3,1024,1024]{2,1,0:T(8,128)(2,1)S(1)}, bf16[3,1024,1024]{2,1,0:T(8,128)(2,1)}, u32[]{:S(2)}) %copy-start) | copy-done | bytes 6291480
  18.0 0.0 copy-start.1
  18.0 1.6 %copy-done.1 = bf16[1024,1024]{1,0:T(8,128)(2,1)S(1)} copy-done((bf16[1024,1024]{1,0:T(8,128)(2,1)S(1)}, bf16[1024,1024]{1,0:T(8,128)(2,1)}, u32[]{:S(2)}) %copy-start.1) | copy-done | bytes 2097176
  19.6 0.0 copy-start.2
  19.6 1.2 %copy-done.2 = bf16[480,1024]{1,0:T(8,128)(2,1)S(1)} copy-done((bf16[480,1024]{1,0:T(8,128)(2,1)S(1)}, bf16[480,1024]{1,0:T(8,128)(2,1)}, u32[]{:S(2)}) %copy-start.2) | copy-done | bytes 983064
  20.8 0.0 copy-start.3
  20.8 1.2 %copy-done.3 = bf16[480,1024]{1,0:T(8,128)(2,1)S(1)} copy-done((bf16[480,1024]{1,0:T(8,128)(2,1)S(1)}, bf16[480,1024]{1,0:T(8,128)(2,1)}, u32[]{:S(2)}) %copy-start.3) | copy-done | bytes 983064
  22.0 0.0 copy-start.4
  22.0 0.7 %copy-done.4 = s32[480]{0:T(512)S(1)} copy-done((s32[480]{0:T(512)S(1)}, s32[480]{0:T(512)}, u32[]{:S(2)}) %copy-start.4) | copy-done | bytes 1944
  22.7 27.5 %shard_map.73 = bf16[480,1024]{1,0:T(8,128)(2,1)} custom-call(bf16[480,1024]{1,0:T(8,128)(2,1)S(1)} %copy-done.2, bf16[480,1024]{1,0:T(8,128)(2,1)S(1)} %copy-done.3, bf16[1,1024]{1,0:T(2,128)(2,1)S(1)} %reshape.9.time_ref, bf16[1,1024]{1,0:T(2,128)(2,1)S(1)} %reshape.10.gain_ref, bf16[112,1024]{1,0:T(8,128)(2,1)S(1)} %collective-permute-done.behind_ref, ...), custom_call_target="tpu_custom_call" | custom-call | tf_op jit(solution)/shard_map/pallas_call | solution.py:251
  (2 shorter events, 0.0 us)
Async XLA Ops:
  1.8 13.5 %collective-permute-start = (bf16[112,1024]{1,0:T(8,128)(2,1)S(1)}, bf16[112,1024]{1,0:T(8,128)(2,1)S(1)}, u32[]{:S(2)}, u32[]{:S(2)}) collective-permute-start(bf16[112,1024]{1,0:T(8,128)(2,1)S(1)} %fusion.2), channel_id=1, source_target_pairs={{0,1},{1,2},{2,3},{3,4},{4,5},{5,6},{6,7},{7,8},{8,9},{9,10},{10,1... | collective-permute-start | bytes 688136 | tf_op jit(solution)/shard_map/ppermute | solution.py:28
  7.2 8.1 %collective-permute-start.1 = (bf16[64,1024]{1,0:T(8,128)(2,1)S(1)}, bf16[64,1024]{1,0:T(8,128)(2,1)S(1)}, u32[]{:S(2)}, u32[]{:S(2)}) collective-permute-start(bf16[64,1024]{1,0:T(8,128)(2,1)S(1)} %fusion.3), channel_id=1, source_target_pairs={{1,0},{2,1},{3,2},{4,3},{5,4},{6,5},{7,6},{8,7},{9,8},{10,9},{11,1... | collective-permute-start | bytes 393224 | tf_op jit(solution)/shard_map/ppermute | solution.py:28
  15.2 2.8 %copy-start = (bf16[3,1024,1024]{2,1,0:T(8,128)(2,1)S(1)}, bf16[3,1024,1024]{2,1,0:T(8,128)(2,1)}, u32[]{:S(2)}) copy-start(bf16[3,1024,1024]{2,1,0:T(8,128)(2,1)} %wqkv_hbm.1) | copy-start | bytes 18874372
  18.0 1.6 %copy-start.1 = (bf16[1024,1024]{1,0:T(8,128)(2,1)S(1)}, bf16[1024,1024]{1,0:T(8,128)(2,1)}, u32[]{:S(2)}) copy-start(bf16[1024,1024]{1,0:T(8,128)(2,1)} %wout_hbm.1) | copy-start | bytes 6291460
  19.6 1.2 %copy-start.2 = (bf16[480,1024]{1,0:T(8,128)(2,1)S(1)}, bf16[480,1024]{1,0:T(8,128)(2,1)}, u32[]{:S(2)}) copy-start(bf16[480,1024]{1,0:T(8,128)(2,1)} %state_ref.1) | copy-start | bytes 2949124
  20.8 1.2 %copy-start.3 = (bf16[480,1024]{1,0:T(8,128)(2,1)S(1)}, bf16[480,1024]{1,0:T(8,128)(2,1)}, u32[]{:S(2)}) copy-start(bf16[480,1024]{1,0:T(8,128)(2,1)} %cond_ref.1) | copy-start | bytes 2949124
  22.0 0.7 %copy-start.4 = (s32[480]{0:T(512)S(1)}, s32[480]{0:T(512)}, u32[]{:S(2)}) copy-start(s32[480]{0:T(512)} %param.13) | copy-start | bytes 5764

commit v2 on v1

v2 whole, which is shorter than its diff:
```python
import functools
import math

import jax
import jax.numpy as jnp
from jax import lax
from jax.experimental import pallas as pl
from jax.experimental.pallas import tpu as pltpu
from jax.sharding import PartitionSpec as P

HEAD_DIM = 64
BLOCK = 24
UNIT = 2 * BLOCK
BEHIND = 4 * BLOCK
AHEAD = 2 * BLOCK
WINDOW = 128
SPARE = WINDOW - 2 * UNIT
PAIR = 2 * HEAD_DIM
PAYLOAD = BEHIND + 16
TILE = 256
LIMIT = 53
EDGE_LIMIT = 56
F32 = jnp.float32
BF16 = jnp.bfloat16
NEG = -1e30


def column_of(row):
    n = row.shape[1]
    same = lax.broadcasted_iota(jnp.int32, (n, n), 0) == lax.broadcasted_iota(jnp.int32, (n, n), 1)
    column = jnp.sum(jnp.where(same, row, 0.0), axis=1, keepdims=True)
    return jnp.broadcast_to(column, (n, 128))


def own_segments(ids_ref, seg_ref):
    own = ids_ref.shape[1]
    for at in range(0, own, 128):
        n = min(128, own - at)
        row = (ids_ref[:, at : at + n] + 1).astype(F32)
        seg_ref[BEHIND + at : BEHIND + at + n, :] = column_of(row)


def edge_segments(behind_ref, ahead_ref, seg_ref):
    end = seg_ref.shape[0] - SPARE
    seg_ref[0:BEHIND, :] = column_of(behind_ref[BEHIND : BEHIND + 1, 0:BEHIND].astype(F32))
    seg_ref[end - AHEAD : end, :] = column_of(ahead_ref[BEHIND : BEHIND + 1, 0:AHEAD].astype(F32))
    seg_ref[end : end + SPARE, :] = jnp.full((SPARE, 128), -1.0, F32)


def build_mask(unit, seg_ref, bias_ref):
    start = unit * UNIT
    if not isinstance(unit, int):
        start = pl.multiple_of(start, 16)
    window = seg_ref[pl.ds(start - UNIT, WINDOW), :]
    r = lax.broadcasted_iota(jnp.int32, (WINDOW, WINDOW), 0)
    c = lax.broadcasted_iota(jnp.int32, (WINDOW, WINDOW), 1)
    keys = jnp.sum(jnp.where(r == c, window, 0.0), axis=0, keepdims=True)
    queries = seg_ref[pl.ds(start, UNIT), :]
    row = lax.broadcasted_iota(jnp.int32, (UNIT, WINDOW), 0)
    col = lax.broadcasted_iota(jnp.int32, (UNIT, WINDOW), 1)
    first = jnp.where(row < BLOCK, 0, BLOCK)
    band = (col >= first) & (col < first + 4 * BLOCK)
    bias_ref[unit] = jnp.where(band & (queries == keys), 0.0, NEG)


def build_masks(units, seg_ref, bias_ref):
    def one(unit, carry):
        build_mask(unit, seg_ref, bias_ref)
        return carry

    lax.fori_loop(units[0], units[1], one, 0)


def normalize(h_ref, normed_ref, gain, first, last):
    def one(i, carry):
        at = pl.ds(pl.multiple_of(first + i * UNIT, 16), UNIT)
        h = h_ref[at, :]
        scale = lax.rsqrt(jnp.mean(h * h, axis=-1, keepdims=True) + 1e-06)
        normed_ref[at, :] = (h * scale * gain).astype(BF16)
        return carry

    lax.fori_loop(0, (last - first) // UNIT, one, 0)


def project(normed_ref, w_ref, first, last, outs):
    width = w_ref.shape[1]
    tile = min(TILE, width)
    for at in range(0, width, tile):
        cols = slice(at, at + tile)
        out = jnp.dot(
            normed_ref[first:last, :], w_ref[:, cols], preferred_element_type=F32
        ).astype(BF16)
        if len(outs) == 1:
            outs[0][first:last, cols] = out
        else:
            lane = lax.broadcasted_iota(jnp.int32, out.shape, 1) % PAIR
            zero = jnp.zeros_like(out)
            outs[0][first:last, cols] = jnp.where(lane < HEAD_DIM, out, zero)
            outs[1][first:last, cols] = jnp.where(lane < HEAD_DIM, zero, out)


def attend(first, last, q_ref, k_refs, v_refs, att_ref, bias_ref, score_ref, prob_ref):
    pairs = q_ref.shape[1] // PAIR
    lane = lax.broadcasted_iota(jnp.int32, (WINDOW, PAIR), 1)
    ones = [(lane < HEAD_DIM).astype(BF16), (lane >= HEAD_DIM).astype(BF16)]
    factor = HEAD_DIM**-0.5 * math.log2(math.e)

    def at(unit):
        start = pl.multiple_of(unit * UNIT, 16)
        return pl.ds(start, UNIT), pl.ds(pl.multiple_of(start - UNIT, 16), WINDOW)

    def score(unit):
        rows, window = at(unit)
        for p in range(pairs):
            lanes = slice(p * PAIR, (p + 1) * PAIR)
            keys = jnp.concatenate([k_refs[0][window, lanes], k_refs[1][window, lanes]], axis=0)
            score_ref[:, 2 * p * WINDOW : 2 * (p + 1) * WINDOW] = lax.dot_general(
                q_ref[rows, lanes], keys, (((1,), (1,)), ((), ())), preferred_element_type=F32
            )

    def soften(unit):
        bias = bias_ref[unit]
        for head in range(2 * pairs):
            lanes = slice(head * WINDOW, (head + 1) * WINDOW)
            s = score_ref[:, lanes] * factor + bias
            prob_ref[:, lanes] = jnp.exp2(s - jnp.max(s, axis=-1, keepdims=True)).astype(BF16)

    def mix(unit):
        rows, window = at(unit)
        for p in range(pairs):
            lanes = slice(p * PAIR, (p + 1) * PAIR)
            values = jnp.concatenate(
                [
                    jnp.concatenate([v_refs[0][window, lanes], ones[0]], axis=1),
                    jnp.concatenate([v_refs[1][window, lanes], ones[1]], axis=1),
                ],
                axis=0,
            )
            out = jnp.dot(
                prob_ref[:, 2 * p * WINDOW : 2 * (p + 1) * WINDOW],
                values,
                preferred_element_type=F32,
            )
            att_ref[rows, lanes] = (out[:, :PAIR] / out[:, PAIR:]).astype(BF16)

    score(first)
    soften(first)
    score(first + 1)

    def one(unit, carry):
        mix(unit)
        soften(unit + 1)
        score(unit + 2)
        return carry

    lax.fori_loop(first, last - 2, one, 0)
    mix(last - 2)
    soften(last - 1)
    mix(last - 1)


def edge_kernel(
    state_hbm, cond_hbm, ids_ref, time_ref, gain_ref,
    cross_ref, core_ref,
    state_last, cond_last, state_first, cond_first, sems,
):
    own = state_hbm.shape[0]
    copies = [
        pltpu.make_async_copy(source.at[pl.ds(first, rows)], target, sems.at[i])
        for i, (source, first, rows, target) in enumerate(
            (
                (state_hbm, own - BEHIND, BEHIND, state_last),
                (cond_hbm, own - BEHIND, BEHIND, cond_last),
                (state_hbm, 0, AHEAD, state_first),
                (cond_hbm, 0, AHEAD, cond_first),
            )
        )
    ]
    for copy in copies:
        copy.start()
    even = lax.rem(lax.axis_index("seq"), 2) == 0
    time = time_ref[...].astype(F32).reshape(1, -1)
    gain = gain_ref[...].astype(F32).reshape(1, -1)
    for copy in copies:
        copy.wait()

    def fill(ref, state, cond, ids):
        rows = state.shape[0]
        ref[0:rows, :] = (state[...].astype(F32) + cond[...].astype(F32)).astype(BF16)
        if rows < BEHIND:
            ref[rows:BEHIND, :] = jnp.zeros((BEHIND - rows, ref.shape[1]), BF16)
        depth = ref.shape[1]
        number_row = jnp.concatenate([(ids + 1).astype(F32), jnp.zeros((1, depth - BEHIND), F32)], axis=1)
        spare = jnp.zeros((PAYLOAD - BEHIND - 3, depth), F32)
        ref[BEHIND:, :] = jnp.concatenate([number_row, time, gain, spare], axis=0).astype(BF16)

    def fill_both(to_next, to_previous):
        fill(to_next, state_last, cond_last, ids_ref[:, own - BEHIND :])
        fill(to_previous, state_first, cond_first, ids_ref[:, :BEHIND])

    @pl.when(even)
    def _():
        fill_both(core_ref, cross_ref)

    @pl.when(jnp.logical_not(even))
    def _():
        fill_both(cross_ref, core_ref)


def both_steps(
    cross_ref, core_ref, state_hbm, cond_hbm, ids_ref, wqkv_hbm, wout_hbm,
    out_ref,
    state_ref, cond_ref, wqkv, wout, behind_ref, ahead_ref, h_ref,
    normed_ref, q_ref, ka_ref, kb_ref, va_ref, vb_ref, att_ref, seg_ref, bias_ref, score_ref, prob_ref,
    sems,
):
    own = state_ref.shape[0]
    end = BEHIND + own
    total = end + AHEAD
    k_refs, v_refs = (ka_ref, kb_ref), (va_ref, vb_ref)
    copies = [
        pltpu.make_async_copy(source, target, sems.at[i])
        for i, (source, target) in enumerate(
            (
                (state_hbm, state_ref),
                (cond_hbm, cond_ref),
                (wqkv_hbm.at[1], wqkv.at[1]),
                (wqkv_hbm.at[2], wqkv.at[2]),
                (wqkv_hbm.at[0], wqkv.at[0]),
                (wout_hbm, wout),
            )
        )
    ]
    for copy in copies:
        copy.start()
    half_time = 0.5 * core_ref[BEHIND + 1 : BEHIND + 2, :].astype(F32)
    gain = core_ref[BEHIND + 2 : BEHIND + 3, :].astype(F32)
    even = lax.rem(lax.axis_index("seq"), 2) == 0

    def take(before, after):
        behind_ref[...] = before[...]
        ahead_ref[...] = after[...]

    @pl.when(even)
    def _():
        take(cross_ref, core_ref)

    @pl.when(jnp.logical_not(even))
    def _():
        take(core_ref, cross_ref)

    own_segments(ids_ref, seg_ref)
    edge_segments(behind_ref, ahead_ref, seg_ref)
    build_masks((1, total // UNIT), seg_ref, bias_ref)
    clear_spare(k_refs + v_refs)
    h_ref[0:BEHIND, :] = behind_ref[0:BEHIND, :].astype(F32)
    h_ref[end:total, :] = ahead_ref[0:AHEAD, :].astype(F32)
    copies[0].wait()
    copies[1].wait()
    h_ref[BEHIND:end, :] = state_ref[...].astype(F32) + cond_ref[...].astype(F32)
    normalize(h_ref, normed_ref, gain, 0, total)
    copies[2].wait()
    project(normed_ref, wqkv.at[1], 0, total, k_refs)
    copies[3].wait()
    project(normed_ref, wqkv.at[2], 0, total, v_refs)
    copies[4].wait()
    project(normed_ref, wqkv.at[0], UNIT, total, [q_ref])
    attend(1, total // UNIT, q_ref, k_refs, v_refs, att_ref, bias_ref, score_ref, prob_ref)
    copies[5].wait()
    depth = wout.shape[1]
    for at in range(0, depth, TILE):
        cols = slice(at, at + TILE)
        moved = jnp.dot(att_ref[UNIT:total, :], wout[:, cols], preferred_element_type=F32)
        h_ref[UNIT:total, cols] = h_ref[UNIT:total, cols] + 0.5 * moved + half_time[:, cols]

    normalize(h_ref, normed_ref, gain, UNIT, total)
    project(normed_ref, wqkv.at[1], UNIT, total, k_refs)
    project(normed_ref, wqkv.at[2], UNIT, total, v_refs)
    project(normed_ref, wqkv.at[0], BEHIND, end, [q_ref])
    attend(
        BEHIND // UNIT, end // UNIT, q_ref, k_refs, v_refs, att_ref, bias_ref, score_ref, prob_ref
    )
    for at in range(0, depth, TILE):
        cols = slice(at, at + TILE)
        moved = jnp.dot(att_ref[BEHIND:end, :], wout[:, cols], preferred_element_type=F32)
        x = h_ref[BEHIND:end, cols] - cond_ref[:, cols].astype(F32) - half_time[:, cols]
        out_ref[:, cols] = (x + 0.5 * moved).astype(BF16)


def clear_spare(refs):
    for ref in refs:
        ref[ref.shape[0] - SPARE :, :] = jnp.zeros((SPARE, ref.shape[1]), ref.dtype)


def one_step(
    final, h_ref, gain_ref, behind_ref, ahead_ref, ids_ref, wqkv, wout,
    out_ref,
    normed_ref, q_ref, ka_ref, kb_ref, va_ref, vb_ref, att_ref, seg_ref, bias_ref, score_ref, prob_ref,
):
    own = ids_ref.shape[1]
    total = BEHIND + own + AHEAD
    k_refs, v_refs = (ka_ref, kb_ref), (va_ref, vb_ref)
    kv_first = UNIT if final else 0
    first, last = (BEHIND, BEHIND + own) if final else (UNIT, total)
    own_segments(ids_ref, seg_ref)
    edge_segments(behind_ref, ahead_ref, seg_ref)
    build_masks((1, total // UNIT), seg_ref, bias_ref)
    clear_spare(k_refs + v_refs)
    normalize(h_ref, normed_ref, gain_ref[...].astype(F32), kv_first, total)
    project(normed_ref, wqkv.at[1], kv_first, total, k_refs)
    project(normed_ref, wqkv.at[2], kv_first, total, v_refs)
    project(normed_ref, wqkv.at[0], first, last, [q_ref])
    attend(
        first // UNIT, last // UNIT,
        q_ref, k_refs, v_refs, att_ref, bias_ref, score_ref, prob_ref,
    )
    for at in range(0, wout.shape[1], TILE):
        cols = slice(at, at + TILE)
        out_ref[:, cols] = jnp.dot(
            att_ref[first:last, :], wout[:, cols], preferred_element_type=F32
        ).astype(BF16)


def shards(state, condition, time_vector, norm_gain, w_qkv, w_out, utterance_ids):
    own, depth = state.shape
    width = w_qkv.shape[2]
    total = BEHIND + own + AHEAD
    parts = lax.axis_size("mp")
    count = lax.axis_size("seq")
    ids = utterance_ids.reshape(1, own)
    vmem = pl.BlockSpec(memory_space=pltpu.VMEM)
    hbm = pl.BlockSpec(memory_space=pltpu.HBM)

    def limit(mib):
        return pltpu.CompilerParams(vmem_limit_bytes=mib * 2**20)

    cross, core = pl.pallas_call(
        edge_kernel,
        out_shape=[jax.ShapeDtypeStruct((PAYLOAD, depth), BF16)] * 2,
        in_specs=[hbm, hbm, vmem, vmem, vmem],
        out_specs=[vmem, vmem],
        scratch_shapes=[pltpu.VMEM((BEHIND, depth), BF16)] * 2
        + [pltpu.VMEM((AHEAD, depth), BF16)] * 2
        + [pltpu.SemaphoreType.DMA((4,))],
        compiler_params=limit(EDGE_LIMIT),
    )(state, condition, ids, time_vector, norm_gain)
    ends = [(i, i + 1) for i in range(1, count - 1, 2)]
    cross = lax.ppermute(cross, "seq", ends + [(j, i) for i, j in ends])
    ends = [(i, i + 1) for i in range(0, count - 1, 2)]
    core = lax.ppermute(core, "seq", ends + [(j, i) for i, j in ends])

    work = [((total, depth), BF16), ((total, width), BF16)]
    work += [((total + SPARE, width), BF16)] * 4
    work += [
        ((total, width), BF16),
        ((total + SPARE, 128), F32),
        ((total // UNIT, UNIT, WINDOW), F32),
        ((UNIT, width // HEAD_DIM * WINDOW), F32),
        ((UNIT, width // HEAD_DIM * WINDOW), BF16),
    ]
    if parts == 1:
        first = [((own, depth), BF16)] * 2 + [(w_qkv.shape, BF16), (w_out.shape, BF16)]
        first += [((PAYLOAD, depth), BF16)] * 2 + [((total, depth), F32)]
        return pl.pallas_call(
            both_steps,
            out_shape=jax.ShapeDtypeStruct((own, depth), BF16),
            in_specs=[vmem, vmem, hbm, hbm, vmem, hbm, hbm],
            out_specs=vmem,
            scratch_shapes=[pltpu.VMEM(*one) for one in first + work]
            + [pltpu.SemaphoreType.DMA((6,))],
            compiler_params=limit(LIMIT),
        )(cross, core, state, condition, ids, w_qkv, w_out)

    even = lax.axis_index("seq") % 2 == 0
    behind = jnp.where(even, cross, core)
    ahead = jnp.where(even, core, cross)
    gain = norm_gain.reshape(1, depth)

    def terms(h, final):
        rows = own if final else total - UNIT
        mine = pl.pallas_call(
            functools.partial(one_step, final),
            out_shape=jax.ShapeDtypeStruct((rows, depth), BF16),
            in_specs=[vmem] * 7,
            out_specs=vmem,
            scratch_shapes=[pltpu.VMEM(*one) for one in work],
            compiler_params=limit(LIMIT),
        )(h, gain, behind, ahead, ids, w_qkv, w_out)
        return lax.psum(mine, "mp").astype(F32)

    start = state.astype(F32)
    h = jnp.concatenate(
        [behind[:BEHIND].astype(F32), start + condition.astype(F32), ahead[:AHEAD].astype(F32)]
    )
    velocity = terms(h, False)
    later = jnp.pad(velocity, ((UNIT, 0), (0, 0))) * 0.5 + 0.5 * time_vector.astype(F32)
    x = start + 0.5 * velocity[UNIT : UNIT + own] + 0.5 * terms(h + later, True)
    share = depth // parts
    mine = lax.dynamic_slice_in_dim(x, lax.axis_index("mp") * share, share, 1)
    return mine.astype(BF16)


def solution(mesh):
    in_specs = (
        P("seq", None),
        P("seq", None),
        P(),
        P(),
        P(None, None, "mp"),
        P("mp", None),
        P("seq"),
    )
    out_specs = P("seq", "mp")
    return jax.shard_map(shards, mesh=mesh, in_specs=in_specs, out_specs=out_specs, check_vma=False)
```

time: 50.7 us -> 40.8 us (0.80)
  the two profiles are of different devices: /device:TPU:15 before, /device:TPU:27 now
where the time goes in v2:
time: 40.8 us; the launch traced here: 40.6 us
  Pallas kernels  29.1 us (71%)
  waiting for transfers between devices  7.09 us (17%)
  starting transfers between devices  3.75 us (9%)
  local copies, waits for them, and re-layouts  0.68 us (2%)
    pallas_call x1, Pallas kernels, shards(): pl.pallas_call(both_steps, out_shape=jax.ShapeDtypeStruct((own, depth), B...  26.3 us
    ppermute x1, waiting for transfers between devices, shards(): cross = lax.ppermute(cross, 'seq', ends + [(j, i) for i, j in ends])  7.09 us
    ppermute x1, starting transfers between devices, shards(): cross = lax.ppermute(cross, 'seq', ends + [(j, i) for i, j in ends])  3.68 us
    pallas_call x1, Pallas kernels, shards(): pl.pallas_call(edge_kernel, out_shape=[jax.ShapeDtypeStruct((PAYLOAD, dep...  2.72 us
  transfers between devices with their start and end apart: 2, of which 1 were waited for; matrix products, arithmetic and copies ran while one was open for 0% of the time, Pallas kernels for 0%

profile of v2, /device:TPU:27, one launch (start us, length us, event | category | flops | bytes accessed | tf_op | source)
XLA Modules:
  0.0 40.6 jit_solution(15191361258714921312)
XLA Ops:
  0.0 2.7 %shard_map.73 = (bf16[112,1024]{1,0:T(8,128)(2,1)}, bf16[112,1024]{1,0:T(8,128)(2,1)}) custom-call(bf16[480,1024]{1,0:T(8,128)(2,1)} %state_hbm.3, bf16[480,1024]{1,0:T(8,128)(2,1)} %cond_hbm.3, s32[1,480]{1,0:T(1,128)} %bitcast.1, bf16[1024]{0:T(1024)(128)(2,1)} %time_ref.1, bf16[1024]{0:T(1024)(128)(2,1)} %gain_ref.1), custom_call_target="tpu_custom_call" | custom-call | tf_op jit(solution)/shard_map/pallas_call | solution.py:337
  2.7 3.7 %collective-permute-start = (bf16[112,1024]{1,0:T(8,128)(2,1)}, bf16[112,1024]{1,0:T(8,128)(2,1)S(1)}, u32[]{:S(2)}, u32[]{:S(2)}) collective-permute-start(bf16[112,1024]{1,0:T(8,128)(2,1)} %get-tuple-element.7), channel_id=1, source_target_pairs={{1,2},{3,4},{5,6},{7,8},{9,10},{11,12},{13,14},{15,16},{17,18},{19... | collective-permute-start | bytes 688136 | tf_op jit(solution)/shard_map/ppermute | solution.py:348
  6.4 0.1 collective-permute-start.1
  6.5 7.1 %collective-permute-done.cross_ref = bf16[112,1024]{1,0:T(8,128)(2,1)S(1)} collective-permute-done((bf16[112,1024]{1,0:T(8,128)(2,1)}, bf16[112,1024]{1,0:T(8,128)(2,1)S(1)}, u32[]{:S(2)}, u32[]{:S(2)}) %collective-permute-start) | collective-permute-done | bytes 229408 | tf_op jit(solution)/shard_map/ppermute | solution.py:348
  13.6 0.0 collective-permute-done.1.core_ref
  13.6 0.0 copy-start
  13.6 0.7 %copy-done = s32[480]{0:T(512)S(1)} copy-done((s32[480]{0:T(512)S(1)}, s32[480]{0:T(512)}, u32[]{:S(2)}) %copy-start) | copy-done | bytes 1944
  14.3 26.3 %shard_map.74 = bf16[480,1024]{1,0:T(8,128)(2,1)} custom-call(bf16[112,1024]{1,0:T(8,128)(2,1)S(1)} %collective-permute-done.cross_ref, bf16[112,1024]{1,0:T(8,128)(2,1)S(1)} %collective-permute-done.1.core_ref, bf16[480,1024]{1,0:T(8,128)(2,1)} %state_hbm.3, bf16[480,1024]{1,0:T(8,128)(2,1)} %cond_hbm.3, s32[1,480]{1,0:T(1,128)S(1)} %bitcast.2, ...), custom_call_target="tpu_custom_call" | custom-call | tf_op jit(solution)/shard_map/pallas_call | solution.py:364
Async XLA Ops:
  2.7 10.9 %collective-permute-start = (bf16[112,1024]{1,0:T(8,128)(2,1)}, bf16[112,1024]{1,0:T(8,128)(2,1)S(1)}, u32[]{:S(2)}, u32[]{:S(2)}) collective-permute-start(bf16[112,1024]{1,0:T(8,128)(2,1)} %get-tuple-element.7), channel_id=1, source_target_pairs={{1,2},{3,4},{5,6},{7,8},{9,10},{11,12},{13,14},{15,16},{17,18},{19... | collective-permute-start | bytes 688136 | tf_op jit(solution)/shard_map/ppermute | solution.py:348
  6.4 7.2 %collective-permute-start.1 = (bf16[112,1024]{1,0:T(8,128)(2,1)}, bf16[112,1024]{1,0:T(8,128)(2,1)S(1)}, u32[]{:S(2)}, u32[]{:S(2)}) collective-permute-start(bf16[112,1024]{1,0:T(8,128)(2,1)} %get-tuple-element.8), channel_id=1, source_target_pairs={{0,1},{2,3},{4,5},{6,7},{8,9},{10,11},{12,13},{14,15},{16,17},{18,... | collective-permute-start | bytes 688136 | tf_op jit(solution)/shard_map/ppermute | solution.py:350
  13.6 0.7 %copy-start = (s32[480]{0:T(512)S(1)}, s32[480]{0:T(512)}, u32[]{:S(2)}) copy-start(s32[480]{0:T(512)} %param.13) | copy-start | bytes 5764

commit v3 on v2

v3 whole, which is shorter than its diff:
```python
import functools
import math

import jax
import jax.numpy as jnp
from jax import lax
from jax.experimental import pallas as pl
from jax.experimental.pallas import tpu as pltpu
from jax.sharding import PartitionSpec as P

HEAD_DIM = 64
BLOCK = 24
UNIT = 2 * BLOCK
BEHIND = 4 * BLOCK
AHEAD = 2 * BLOCK
WINDOW = 128
SPARE = WINDOW - 2 * UNIT
PAIR = 2 * HEAD_DIM
SMALL = 16
PAYLOAD = BEHIND + 16
TILE = 256
EDGE_LIMIT, OWN_LIMIT, LIMIT = 56, 49, 48
F32 = jnp.float32
BF16 = jnp.bfloat16
NEG = -1e30


def column_of(row):
    n = row.shape[1]
    same = lax.broadcasted_iota(jnp.int32, (n, n), 0) == lax.broadcasted_iota(jnp.int32, (n, n), 1)
    column = jnp.sum(jnp.where(same, row, 0.0), axis=1, keepdims=True)
    return jnp.broadcast_to(column, (n, 128))


def own_segments(small_ref, seg_ref, own):
    for at in range(0, own, 128):
        n = min(128, own - at)
        row = small_ref[0:1, at : at + n].astype(F32)
        seg_ref[BEHIND + at : BEHIND + at + n, :] = column_of(row)


def edge_segments(behind_ref, ahead_ref, seg_ref):
    end = seg_ref.shape[0] - SPARE
    seg_ref[0:BEHIND, :] = column_of(behind_ref[BEHIND : BEHIND + 1, 0:BEHIND].astype(F32))
    seg_ref[end - AHEAD : end, :] = column_of(ahead_ref[BEHIND : BEHIND + 1, 0:AHEAD].astype(F32))
    seg_ref[end : end + SPARE, :] = jnp.full((SPARE, 128), -1.0, F32)


def build_mask(unit, seg_ref, bias_ref):
    start = unit * UNIT
    if not isinstance(unit, int):
        start = pl.multiple_of(start, 16)
    window = seg_ref[pl.ds(start - UNIT, WINDOW), :]
    r = lax.broadcasted_iota(jnp.int32, (WINDOW, WINDOW), 0)
    c = lax.broadcasted_iota(jnp.int32, (WINDOW, WINDOW), 1)
    keys = jnp.sum(jnp.where(r == c, window, 0.0), axis=0, keepdims=True)
    queries = seg_ref[pl.ds(start, UNIT), :]
    row = lax.broadcasted_iota(jnp.int32, (UNIT, WINDOW), 0)
    col = lax.broadcasted_iota(jnp.int32, (UNIT, WINDOW), 1)
    first = jnp.where(row < BLOCK, 0, BLOCK)
    band = (col >= first) & (col < first + 4 * BLOCK)
    bias_ref[unit] = jnp.where(band & (queries == keys), 0.0, NEG)


def build_masks(units, seg_ref, bias_ref):
    def one(unit, carry):
        build_mask(unit, seg_ref, bias_ref)
        return carry

    lax.fori_loop(units[0], units[1], one, 0)


def normalize(h_ref, normed_ref, gain, first, last):
    def one(i, carry):
        at = pl.ds(pl.multiple_of(first + i * UNIT, 16), UNIT)
        h = h_ref[at, :]
        scale = lax.rsqrt(jnp.mean(h * h, axis=-1, keepdims=True) + 1e-06)
        normed_ref[at, :] = (h * scale * gain).astype(BF16)
        return carry

    lax.fori_loop(0, (last - first) // UNIT, one, 0)


def project(normed_ref, w_ref, first, last, out_ref, places):
    width = w_ref.shape[1]
    tile = min(TILE, width)
    for at in range(0, width, tile):
        cols = slice(at, at + tile)
        out = jnp.dot(
            normed_ref[first:last, :], w_ref[:, cols], preferred_element_type=F32
        ).astype(BF16)
        done = 0
        for rows, place in places:
            out_ref[place : place + rows, cols] = out[done : done + rows]
            done += rows


def attend(first, last, q_ref, k_ref, v_ref, att_ref, bias_ref, score_ref, prob_ref):
    pairs = q_ref.shape[1] // PAIR
    ones = jnp.ones((WINDOW, PAIR), BF16)
    factor = HEAD_DIM**-0.5 * math.log2(math.e)

    def at(unit):
        start = pl.multiple_of(unit * UNIT, 16)
        return pl.ds(start, UNIT), pl.ds(pl.multiple_of(start - UNIT, 16), WINDOW)

    def score(unit):
        rows, window = at(unit)
        one = lax.broadcasted_iota(jnp.int32, (UNIT, PAIR), 1) < HEAD_DIM
        for p in range(pairs):
            lanes = slice(p * PAIR, (p + 1) * PAIR)
            q = q_ref[rows, lanes]
            zero = jnp.zeros_like(q)
            both = jnp.concatenate([jnp.where(one, q, zero), jnp.where(one, zero, q)], axis=0)
            score_ref[2 * p * UNIT : 2 * (p + 1) * UNIT, :] = lax.dot_general(
                both, k_ref[window, lanes], (((1,), (1,)), ((), ())), preferred_element_type=F32
            )

    def soften(unit):
        bias = bias_ref[unit]
        for head in range(2 * pairs):
            rows = slice(head * UNIT, (head + 1) * UNIT)
            s = score_ref[rows, :] * factor + bias
            prob_ref[rows, :] = jnp.exp2(s - jnp.max(s, axis=-1, keepdims=True)).astype(BF16)

    def mix(unit):
        rows, window = at(unit)
        one = lax.broadcasted_iota(jnp.int32, (UNIT, PAIR), 1) < HEAD_DIM
        for p in range(pairs):
            lanes = slice(p * PAIR, (p + 1) * PAIR)
            values = jnp.concatenate([v_ref[window, lanes], ones], axis=1)
            out = jnp.dot(
                prob_ref[2 * p * UNIT : 2 * (p + 1) * UNIT, :], values, preferred_element_type=F32
            )
            mixed = jnp.where(one, out[:UNIT, :PAIR], out[UNIT:, :PAIR])
            sums = jnp.where(one, out[:UNIT, PAIR:], out[UNIT:, PAIR:])
            att_ref[rows, lanes] = (mixed / sums).astype(BF16)

    score(first)
    soften(first)
    score(first + 1)

    def one(unit, carry):
        mix(unit)
        soften(unit + 1)
        score(unit + 2)
        return carry

    lax.fori_loop(first, last - 2, one, 0)
    mix(last - 2)
    soften(last - 1)
    mix(last - 1)


def edge_kernel(
    state_hbm, cond_hbm, ids_hbm, time_hbm, gain_hbm,
    cross_ref, core_ref, small_ref,
    state_last, cond_last, state_first, cond_first, ids_ref, time_ref, gain_ref, sems,
):
    own = state_hbm.shape[0]
    copies = [
        pltpu.make_async_copy(source, target, sems.at[i])
        for i, (source, target) in enumerate(
            (
                (state_hbm.at[pl.ds(own - BEHIND, BEHIND)], state_last),
                (cond_hbm.at[pl.ds(own - BEHIND, BEHIND)], cond_last),
                (state_hbm.at[pl.ds(0, AHEAD)], state_first),
                (cond_hbm.at[pl.ds(0, AHEAD)], cond_first),
                (ids_hbm, ids_ref),
                (time_hbm, time_ref),
                (gain_hbm, gain_ref),
            )
        )
    ]
    for copy in copies:
        copy.start()
    even = lax.rem(lax.axis_index("seq"), 2) == 0
    for copy in copies:
        copy.wait()

    depth = core_ref.shape[1]

    def number_row(ids):
        blank = jnp.zeros((1, depth - ids.shape[1]), F32)
        return jnp.concatenate([(ids + 1).astype(F32), blank], axis=1)

    vectors = [ref[...].astype(F32).reshape(1, -1) for ref in (time_ref, gain_ref)]
    blank = jnp.zeros((SMALL - 3, depth), F32)
    small_ref[...] = jnp.concatenate([number_row(ids_ref[...]), *vectors, blank], axis=0).astype(BF16)

    def fill(ref, state, cond, ids):
        rows = state.shape[0]
        ref[0:rows, :] = (state[...].astype(F32) + cond[...].astype(F32)).astype(BF16)
        if rows < BEHIND:
            ref[rows:BEHIND, :] = jnp.zeros((BEHIND - rows, depth), BF16)
        ref[BEHIND:, :] = jnp.broadcast_to(number_row(ids), (PAYLOAD - BEHIND, depth)).astype(BF16)

    def fill_both(to_next, to_previous):
        fill(to_next, state_last, cond_last, ids_ref[:, own - BEHIND :])
        fill(to_previous, state_first, cond_first, ids_ref[:, :BEHIND])

    @pl.when(even)
    def _():
        fill_both(core_ref, cross_ref)

    @pl.when(jnp.logical_not(even))
    def _():
        fill_both(cross_ref, core_ref)


def own_kernel(
    small_ref, state_hbm, cond_hbm, wqkv_hbm,
    state_ref, cond_ref, q_ref, k_ref, v_ref,
    wqkv, normed_ref, sems,
):
    own = state_ref.shape[0]
    copies = [
        pltpu.make_async_copy(source, target, sems.at[i])
        for i, (source, target) in enumerate(
            (
                (state_hbm, state_ref),
                (cond_hbm, cond_ref),
                (wqkv_hbm.at[1], wqkv.at[1]),
                (wqkv_hbm.at[2], wqkv.at[2]),
                (wqkv_hbm.at[0], wqkv.at[0]),
            )
        )
    ]
    for copy in copies:
        copy.start()
    gain = small_ref[2:3, :].astype(F32)
    copies[0].wait()
    copies[1].wait()

    def one(i, carry):
        at = pl.ds(pl.multiple_of(i * UNIT, 16), UNIT)
        h = state_ref[at, :].astype(F32) + cond_ref[at, :].astype(F32)
        scale = lax.rsqrt(jnp.mean(h * h, axis=-1, keepdims=True) + 1e-06)
        normed_ref[at, :] = (h * scale * gain).astype(BF16)
        return carry

    lax.fori_loop(0, own // UNIT, one, 0)
    for which, copy, out_ref in ((1, copies[2], k_ref), (2, copies[3], v_ref), (0, copies[4], q_ref)):
        copy.wait()
        project(normed_ref, wqkv.at[which], 0, own, out_ref, [(own, 0)])


def rest_kernel(
    cross_ref, core_ref, small_ref, state_ref, cond_ref, q_own, k_own, v_own,
    wqkv_hbm, wout_hbm,
    out_ref,
    wqkv, wout, behind_ref, ahead_ref, halo_ref, h_ref,
    normed_ref, q_ref, k_ref, v_ref, att_ref, seg_ref, bias_ref, score_ref, prob_ref,
    sems,
):
    own = state_ref.shape[0]
    end = BEHIND + own
    total = end + AHEAD
    copies = [
        pltpu.make_async_copy(source, target, sems.at[i])
        for i, (source, target) in enumerate(
            (
                (wqkv_hbm.at[1], wqkv.at[1]),
                (wqkv_hbm.at[2], wqkv.at[2]),
                (wqkv_hbm.at[0], wqkv.at[0]),
                (wout_hbm, wout),
            )
        )
    ]
    for copy in copies:
        copy.start()
    half_time = 0.5 * small_ref[1:2, :].astype(F32)
    gain = small_ref[2:3, :].astype(F32)
    even = lax.rem(lax.axis_index("seq"), 2) == 0

    def take(before, after):
        behind_ref[...] = before[...]
        ahead_ref[...] = after[...]

    @pl.when(even)
    def _():
        take(cross_ref, core_ref)

    @pl.when(jnp.logical_not(even))
    def _():
        take(core_ref, cross_ref)

    own_segments(small_ref, seg_ref, own)
    edge_segments(behind_ref, ahead_ref, seg_ref)
    build_masks((1, total // UNIT), seg_ref, bias_ref)
    for ref, rows, place in ((behind_ref, BEHIND, 0), (ahead_ref, AHEAD, BEHIND)):
        h = ref[0:rows, :].astype(F32)
        scale = lax.rsqrt(jnp.mean(h * h, axis=-1, keepdims=True) + 1e-06)
        halo_ref[place : place + rows, :] = (h * scale * gain).astype(BF16)
    for ref, whole in ((q_ref, q_own), (k_ref, k_own), (v_ref, v_own)):
        ref[BEHIND:end, :] = whole[...]
    clear_spare((k_ref, v_ref))
    both = [(BEHIND, 0), (AHEAD, end)]
    copies[0].wait()
    project(halo_ref, wqkv.at[1], 0, BEHIND + AHEAD, k_ref, both)
    copies[1].wait()
    project(halo_ref, wqkv.at[2], 0, BEHIND + AHEAD, v_ref, both)
    copies[2].wait()
    project(halo_ref, wqkv.at[0], UNIT, BEHIND + AHEAD, q_ref, [(UNIT, UNIT), (AHEAD, end)])
    attend(1, total // UNIT, q_ref, k_ref, v_ref, att_ref, bias_ref, score_ref, prob_ref)
    copies[3].wait()
    depth = wout.shape[1]
    for at in range(0, depth, TILE):
        cols = slice(at, at + TILE)
        moved = 0.5 * jnp.dot(att_ref[UNIT:total, :], wout[:, cols], preferred_element_type=F32)
        moved = moved + half_time[:, cols]
        h_ref[UNIT:BEHIND, cols] = behind_ref[UNIT:BEHIND, cols].astype(F32) + moved[:UNIT]
        h_ref[BEHIND:end, cols] = (
            state_ref[:, cols].astype(F32) + cond_ref[:, cols].astype(F32)
        ) + moved[UNIT : UNIT + own]
        h_ref[end:total, cols] = ahead_ref[0:AHEAD, cols].astype(F32) + moved[UNIT + own :]

    normalize(h_ref, normed_ref, gain, UNIT, total)
    project(normed_ref, wqkv.at[1], UNIT, total, k_ref, [(total - UNIT, UNIT)])
    project(normed_ref, wqkv.at[2], UNIT, total, v_ref, [(total - UNIT, UNIT)])
    project(normed_ref, wqkv.at[0], BEHIND, end, q_ref, [(own, BEHIND)])
    attend(
        BEHIND // UNIT, end // UNIT, q_ref, k_ref, v_ref, att_ref, bias_ref, score_ref, prob_ref
    )
    for at in range(0, depth, TILE):
        cols = slice(at, at + TILE)
        moved = jnp.dot(att_ref[BEHIND:end, :], wout[:, cols], preferred_element_type=F32)
        x = h_ref[BEHIND:end, cols] - cond_ref[:, cols].astype(F32) - half_time[:, cols]
        out_ref[:, cols] = (x + 0.5 * moved).astype(BF16)


def clear_spare(refs):
    for ref in refs:
        ref[ref.shape[0] - SPARE :, :] = jnp.zeros((SPARE, ref.shape[1]), ref.dtype)


def one_step(
    final, h_ref, small_ref, behind_ref, ahead_ref, wqkv, wout,
    out_ref,
    normed_ref, q_ref, k_ref, v_ref, att_ref, seg_ref, bias_ref, score_ref, prob_ref,
):
    total = h_ref.shape[0]
    own = total - BEHIND - AHEAD
    kv_first = UNIT if final else 0
    first, last = (BEHIND, BEHIND + own) if final else (UNIT, total)
    own_segments(small_ref, seg_ref, own)
    edge_segments(behind_ref, ahead_ref, seg_ref)
    build_masks((1, total // UNIT), seg_ref, bias_ref)
    clear_spare((k_ref, v_ref))
    normalize(h_ref, normed_ref, small_ref[2:3, :].astype(F32), kv_first, total)
    project(normed_ref, wqkv.at[1], kv_first, total, k_ref, [(total - kv_first, kv_first)])
    project(normed_ref, wqkv.at[2], kv_first, total, v_ref, [(total - kv_first, kv_first)])
    project(normed_ref, wqkv.at[0], first, last, q_ref, [(last - first, first)])
    attend(
        first // UNIT, last // UNIT,
        q_ref, k_ref, v_ref, att_ref, bias_ref, score_ref, prob_ref,
    )
    for at in range(0, wout.shape[1], TILE):
        cols = slice(at, at + TILE)
        out_ref[:, cols] = jnp.dot(
            att_ref[first:last, :], wout[:, cols], preferred_element_type=F32
        ).astype(BF16)


def shards(state, condition, time_vector, norm_gain, w_qkv, w_out, utterance_ids):
    own, depth = state.shape
    width = w_qkv.shape[2]
    total = BEHIND + own + AHEAD
    parts = lax.axis_size("mp")
    count = lax.axis_size("seq")
    ids = utterance_ids.reshape(1, own)
    vmem = pl.BlockSpec(memory_space=pltpu.VMEM)
    hbm = pl.BlockSpec(memory_space=pltpu.HBM)

    def limit(mib):
        return pltpu.CompilerParams(vmem_limit_bytes=mib * 2**20)

    cross, core, small = pl.pallas_call(
        edge_kernel,
        out_shape=[jax.ShapeDtypeStruct((rows, depth), BF16) for rows in (PAYLOAD, PAYLOAD, SMALL)],
        in_specs=[hbm] * 5,
        out_specs=[vmem] * 3,
        scratch_shapes=[pltpu.VMEM((BEHIND, depth), BF16)] * 2
        + [pltpu.VMEM((AHEAD, depth), BF16)] * 2
        + [pltpu.VMEM((1, own), jnp.int32)]
        + [pltpu.VMEM((depth,), BF16)] * 2
        + [pltpu.SemaphoreType.DMA((7,))],
        compiler_params=limit(EDGE_LIMIT),
    )(state, condition, ids, time_vector, norm_gain)
    ends = [(i, i + 1) for i in range(1, count - 1, 2)]
    cross = lax.ppermute(cross, "seq", ends + [(j, i) for i, j in ends])
    ends = [(i, i + 1) for i in range(0, count - 1, 2)]
    core = lax.ppermute(core, "seq", ends + [(j, i) for i, j in ends])

    work = [((total, depth), BF16), ((total, width), BF16)]
    work += [((total + SPARE, width), BF16)] * 2
    work += [
        ((total, width), BF16),
        ((total + SPARE, 128), F32),
        ((total // UNIT, UNIT, WINDOW), F32),
        ((width // HEAD_DIM * UNIT, WINDOW), F32),
        ((width // HEAD_DIM * UNIT, WINDOW), BF16),
    ]
    if parts == 1:
        kept = [jax.ShapeDtypeStruct((own, depth), BF16)] * 2
        kept = pl.pallas_call(
            own_kernel,
            out_shape=kept + [jax.ShapeDtypeStruct((own, width), BF16)] * 3,
            in_specs=[vmem] + [hbm] * 3,
            out_specs=[vmem] * 5,
            scratch_shapes=[pltpu.VMEM(w_qkv.shape, BF16), pltpu.VMEM((own, depth), BF16)]
            + [pltpu.SemaphoreType.DMA((5,))],
            compiler_params=limit(OWN_LIMIT),
            cost_estimate=pl.CostEstimate(
                flops=6 * own * depth * width, bytes_accessed=2 * 4 * depth * width, transcendentals=0
            ),
        )(small, state, condition, w_qkv)
        first = [(w_qkv.shape, BF16), (w_out.shape, BF16)] + [((PAYLOAD, depth), BF16)] * 2
        first += [((BEHIND + AHEAD, depth), BF16), ((total, depth), F32)]
        return pl.pallas_call(
            rest_kernel,
            out_shape=jax.ShapeDtypeStruct((own, depth), BF16),
            in_specs=[vmem] * 8 + [hbm] * 2,
            out_specs=vmem,
            scratch_shapes=[pltpu.VMEM(*one) for one in first + work]
            + [pltpu.SemaphoreType.DMA((4,))],
            compiler_params=limit(LIMIT),
        )(cross, core, small, *kept, w_qkv, w_out)

    even = lax.axis_index("seq") % 2 == 0
    behind = jnp.where(even, cross, core)
    ahead = jnp.where(even, core, cross)

    def terms(h, final):
        rows = own if final else total - UNIT
        mine = pl.pallas_call(
            functools.partial(one_step, final),
            out_shape=jax.ShapeDtypeStruct((rows, depth), BF16),
            in_specs=[vmem] * 6,
            out_specs=vmem,
            scratch_shapes=[pltpu.VMEM(*one) for one in work],
            compiler_params=limit(LIMIT),
        )(h, small, behind, ahead, w_qkv, w_out)
        return lax.psum(mine, "mp").astype(F32)

    start = state.astype(F32)
    h = jnp.concatenate(
        [behind[:BEHIND].astype(F32), start + condition.astype(F32), ahead[:AHEAD].astype(F32)]
    )
    velocity = terms(h, False)
    later = jnp.pad(velocity, ((UNIT, 0), (0, 0))) * 0.5 + 0.5 * time_vector.astype(F32)
    x = start + 0.5 * velocity[UNIT : UNIT + own] + 0.5 * terms(h + later, True)
    share = depth // parts
    mine = lax.dynamic_slice_in_dim(x, lax.axis_index("mp") * share, share, 1)
    return mine.astype(BF16)


def solution(mesh):
    in_specs = (
        P("seq", None),
        P("seq", None),
        P(),
        P(),
        P(None, None, "mp"),
        P("mp", None),
        P("seq"),
    )
    out_specs = P("seq", "mp")
    return jax.shard_map(shards, mesh=mesh, in_specs=in_specs, out_specs=out_specs, check_vma=False)
```

time: 40.8 us -> 35.1 us (0.86)
  the two profiles are of different devices: /device:TPU:27 before, /device:TPU:0 now
where the time goes in v3:
time: 35.1 us; the launch traced here: 34.9 us
  Pallas kernels  29.1 us (83%)
  starting transfers between devices  5.03 us (14%)
  local copies, waits for them, and re-layouts  0.76 us (2%)
    pallas_call x1, Pallas kernels, shards(): pl.pallas_call(rest_kernel, out_shape=jax.ShapeDtypeStruct((own, depth),...  20.7 us
    pallas_call x1, Pallas kernels, shards(): pl.pallas_call(own_kernel, out_shape=kept + [jax.ShapeDtypeStruct((own, w...  6.34 us
    ppermute x1, starting transfers between devices, shards(): core = lax.ppermute(core, 'seq', ends + [(j, i) for i, j in ends])  4.35 us
    pallas_call x1, Pallas kernels, shards(): pl.pallas_call(edge_kernel, out_shape=[jax.ShapeDtypeStruct((rows, depth)...  2.05 us
    unnamed x2, local copies, waits for them, and re-layouts  0.76 us
  transfers between devices with their start and end apart: 2, of which 0 were waited for; matrix products, arithmetic and copies ran while one was open for 0% of the time, Pallas kernels for 18%

profile of v3, /device:TPU:0, one launch (start us, length us, event | category | flops | bytes accessed | tf_op | source)
XLA Modules:
  0.0 34.9 jit_solution(4853091936491173882)
XLA Ops:
  0.0 2.1 %shard_map.73 = (bf16[112,1024]{1,0:T(8,128)(2,1)}, bf16[112,1024]{1,0:T(8,128)(2,1)}, bf16[16,1024]{1,0:T(8,128)(2,1)}) custom-call(bf16[480,1024]{1,0:T(8,128)(2,1)} %state_hbm.3, bf16[480,1024]{1,0:T(8,128)(2,1)} %cond_hbm.3, s32[1,480]{1,0:T(1,128)} %bitcast.1, bf16[1024]{0:T(1024)(128)(2,1)} %time_hbm.1, bf16[1024]{0:T(1024)(128)(2,1)} %gain_hbm.1), custom_call_target="tpu_custom_call" | custom-call | tf_op jit(solution)/shard_map/pallas_call | solution.py:378
  2.1 0.7 %collective-permute-start = (bf16[112,1024]{1,0:T(8,128)(2,1)}, bf16[112,1024]{1,0:T(8,128)(2,1)S(1)}, u32[]{:S(2)}, u32[]{:S(2)}) collective-permute-start(bf16[112,1024]{1,0:T(8,128)(2,1)} %get-tuple-element.13), channel_id=1, source_target_pairs={{1,2},{3,4},{5,6},{7,8},{9,10},{11,12},{13,14},{15,16},{17,18},{19... | collective-permute-start | bytes 688136 | tf_op jit(solution)/shard_map/ppermute | solution.py:391
  2.7 4.4 %collective-permute-start.1 = (bf16[112,1024]{1,0:T(8,128)(2,1)}, bf16[112,1024]{1,0:T(8,128)(2,1)S(1)}, u32[]{:S(2)}, u32[]{:S(2)}) collective-permute-start(bf16[112,1024]{1,0:T(8,128)(2,1)} %get-tuple-element.14), channel_id=1, source_target_pairs={{0,1},{2,3},{4,5},{6,7},{8,9},{10,11},{12,13},{14,15},{16,17},{18,... | collective-permute-start | bytes 688136 | tf_op jit(solution)/shard_map/ppermute | solution.py:393
  7.1 0.0 copy-start
  7.1 0.8 %copy-done = bf16[16,1024]{1,0:T(8,128)(2,1)S(1)} copy-done((bf16[16,1024]{1,0:T(8,128)(2,1)S(1)}, bf16[16,1024]{1,0:T(8,128)(2,1)}, u32[]{:S(2)}) %copy-start) | copy-done | bytes 32792
  7.9 6.3 %shard_map.74 = (bf16[480,1024]{1,0:T(8,128)(2,1)S(1)}, bf16[480,1024]{1,0:T(8,128)(2,1)S(1)}, bf16[480,1024]{1,0:T(8,128)(2,1)S(1)}, bf16[480,1024]{1,0:T(8,128)(2,1)S(1)}, bf16[480,1024]{1,0:T(8,128)(2,1)S(1)}) custom-call(bf16[16,1024]{1,0:T(8,128)(2,1)S(1)} %copy-done, bf16[480,1024]{1,0:T(8,128)(2,1)} %state_hbm.3, bf16[480,1024]{1,0:T(8,128)(2,1)} %cond_hbm.3, ...), custom_call_target="tpu_custom_call" | custom-call | flops 3019898880 | bytes 8388608 | tf_op jit(solution)/shard_map/pallas_call | solution.py:406
  14.2 0.0 collective-permute-done.cross_ref
  14.2 0.0 collective-permute-done.1.core_ref
  14.2 20.7 %shard_map.75 = bf16[480,1024]{1,0:T(8,128)(2,1)} custom-call(bf16[112,1024]{1,0:T(8,128)(2,1)S(1)} %collective-permute-done.cross_ref, bf16[112,1024]{1,0:T(8,128)(2,1)S(1)} %collective-permute-done.1.core_ref, bf16[16,1024]{1,0:T(8,128)(2,1)S(1)} %copy-done, bf16[480,1024]{1,0:T(8,128)(2,1)S(1)} %get-tuple-element.16.state_ref, ...), custom_call_target="tpu_custom_call" | custom-call | tf_op jit(solution)/shard_map/pallas_call | solution.py:420
Async XLA Ops:
  2.1 12.1 %collective-permute-start = (bf16[112,1024]{1,0:T(8,128)(2,1)}, bf16[112,1024]{1,0:T(8,128)(2,1)S(1)}, u32[]{:S(2)}, u32[]{:S(2)}) collective-permute-start(bf16[112,1024]{1,0:T(8,128)(2,1)} %get-tuple-element.13), channel_id=1, source_target_pairs={{1,2},{3,4},{5,6},{7,8},{9,10},{11,12},{13,14},{15,16},{17,18},{19... | collective-permute-start | bytes 688136 | tf_op jit(solution)/shard_map/ppermute | solution.py:391
  2.7 11.5 %collective-permute-start.1 = (bf16[112,1024]{1,0:T(8,128)(2,1)}, bf16[112,1024]{1,0:T(8,128)(2,1)S(1)}, u32[]{:S(2)}, u32[]{:S(2)}) collective-permute-start(bf16[112,1024]{1,0:T(8,128)(2,1)} %get-tuple-element.14), channel_id=1, source_target_pairs={{0,1},{2,3},{4,5},{6,7},{8,9},{10,11},{12,13},{14,15},{16,17},{18,... | collective-permute-start | bytes 688136 | tf_op jit(solution)/shard_map/ppermute | solution.py:393
  7.1 0.8 %copy-start = (bf16[16,1024]{1,0:T(8,128)(2,1)S(1)}, bf16[16,1024]{1,0:T(8,128)(2,1)}, u32[]{:S(2)}) copy-start(bf16[16,1024]{1,0:T(8,128)(2,1)} %get-tuple-element.15.small_ref) | copy-start | bytes 98308

commit v4 on v3

--- a/solution.py
+++ b/solution.py
@@ -19,7 +19,7 @@
 SMALL = 16
 PAYLOAD = BEHIND + 16
 TILE = 256
-EDGE_LIMIT, OWN_LIMIT, LIMIT = 56, 49, 48
+EDGE_LIMIT, OWN_LIMIT, LIMIT = 56, 48, 48
 F32 = jnp.float32
 BF16 = jnp.bfloat16
 NEG = -1e30
@@ -81,11 +81,27 @@
     lax.fori_loop(0, (last - first) // UNIT, one, 0)
 
 
-def project(normed_ref, w_ref, first, last, out_ref, places):
+def width_tiles(w_ref):
+    return w_ref.shape[1] // min(TILE, w_ref.shape[1])
+
+
+def tile_copies(w_hbm, w_ref, sems, first_sem):
+    tile = min(TILE, w_ref.shape[1])
+    return [
+        pltpu.make_async_copy(
+            w_hbm.at[:, pl.ds(i * tile, tile)], w_ref.at[:, pl.ds(i * tile, tile)], sems.at[first_sem + i]
+        )
+        for i in range(w_ref.shape[1] // tile)
+    ]
+
+
+def project(normed_ref, w_ref, first, last, out_ref, places, arriving=None):
     width = w_ref.shape[1]
     tile = min(TILE, width)
     for at in range(0, width, tile):
         cols = slice(at, at + tile)
+        if arriving is not None:
+            arriving[at // tile].wait()
         out = jnp.dot(
             normed_ref[first:last, :], w_ref[:, cols], preferred_element_type=F32
         ).astype(BF16)
@@ -210,27 +226,28 @@
 
 def own_kernel(
     small_ref, state_hbm, cond_hbm, wqkv_hbm,
-    state_ref, cond_ref, q_ref, k_ref, v_ref,
-    wqkv, normed_ref, sems,
+    state_ref, cond_ref, q_ref, k_ref, v_ref, seg_ref, bias_ref,
+    wk_ref, wv_ref, wq_ref, normed_ref, sems,
 ):
     own = state_ref.shape[0]
     copies = [
-        pltpu.make_async_copy(source, target, sems.at[i])
-        for i, (source, target) in enumerate(
-            (
-                (state_hbm, state_ref),
-                (cond_hbm, cond_ref),
-                (wqkv_hbm.at[1], wqkv.at[1]),
-                (wqkv_hbm.at[2], wqkv.at[2]),
-                (wqkv_hbm.at[0], wqkv.at[0]),
-            )
-        )
-    ]
-    for copy in copies:
+        pltpu.make_async_copy(state_hbm, state_ref, sems.at[0]),
+        pltpu.make_async_copy(cond_hbm, cond_ref, sems.at[1]),
+    ]
+    tiles = width_tiles(wk_ref)
+    weights = [
+        tile_copies(wqkv_hbm.at[which], w_ref, sems, 2 + i * tiles)
+        for i, (which, w_ref) in enumerate(((1, wk_ref), (2, wv_ref), (0, wq_ref)))
+    ]
+    for copy in copies + weights[0]:
         copy.start()
     gain = small_ref[2:3, :].astype(F32)
+    own_segments(small_ref, seg_ref, own)
+    build_masks((3, own // UNIT + 1), seg_ref, bias_ref)
     copies[0].wait()
     copies[1].wait()
+    for copy in weights[1] + weights[2]:
+        copy.start()
 
     def one(i, carry):
         at = pl.ds(pl.multiple_of(i * UNIT, 16), UNIT)
@@ -240,34 +257,29 @@
         return carry
 
     lax.fori_loop(0, own // UNIT, one, 0)
-    for which, copy, out_ref in ((1, copies[2], k_ref), (2, copies[3], v_ref), (0, copies[4], q_ref)):
-        copy.wait()
-        project(normed_ref, wqkv.at[which], 0, own, out_ref, [(own, 0)])
+    for w_ref, arriving, out_ref in zip((wk_ref, wv_ref, wq_ref), weights, (k_ref, v_ref, q_ref)):
+        project(normed_ref, w_ref, 0, own, out_ref, [(own, 0)], arriving)
 
 
 def rest_kernel(
-    cross_ref, core_ref, small_ref, state_ref, cond_ref, q_own, k_own, v_own,
+    cross_ref, core_ref, small_ref, state_ref, cond_ref, q_own, k_own, v_own, seg_own, bias_own,
     wqkv_hbm, wout_hbm,
-    out_ref,
-    wqkv, wout, behind_ref, ahead_ref, halo_ref, h_ref,
+    out_hbm,
+    wk_ref, wv_ref, wq_ref, wout, behind_ref, ahead_ref, halo_ref, h_ref, out_ref,
     normed_ref, q_ref, k_ref, v_ref, att_ref, seg_ref, bias_ref, score_ref, prob_ref,
     sems,
 ):
     own = state_ref.shape[0]
+    units = own // UNIT
     end = BEHIND + own
     total = end + AHEAD
-    copies = [
-        pltpu.make_async_copy(source, target, sems.at[i])
-        for i, (source, target) in enumerate(
-            (
-                (wqkv_hbm.at[1], wqkv.at[1]),
-                (wqkv_hbm.at[2], wqkv.at[2]),
-                (wqkv_hbm.at[0], wqkv.at[0]),
-                (wout_hbm, wout),
-            )
-        )
-    ]
-    for copy in copies:
+    tiles = width_tiles(wk_ref)
+    weights = [
+        tile_copies(wqkv_hbm.at[which], w_ref, sems, i * tiles)
+        for i, (which, w_ref) in enumerate(((1, wk_ref), (2, wv_ref), (0, wq_ref)))
+    ]
+    wout_copy = pltpu.make_async_copy(wout_hbm, wout, sems.at[3 * tiles])
+    for copy in weights[0]:
         copy.start()
     half_time = 0.5 * small_ref[1:2, :].astype(F32)
     gain = small_ref[2:3, :].astype(F32)
@@ -285,25 +297,27 @@
     def _():
         take(core_ref, cross_ref)
 
-    own_segments(small_ref, seg_ref, own)
+    seg_ref[BEHIND:end, :] = seg_own[BEHIND:end, :]
     edge_segments(behind_ref, ahead_ref, seg_ref)
-    build_masks((1, total // UNIT), seg_ref, bias_ref)
+    bias_ref[3 : units + 1] = bias_own[3 : units + 1]
+    for unit in (1, 2, units + 1, units + 2):
+        build_mask(unit, seg_ref, bias_ref)
     for ref, rows, place in ((behind_ref, BEHIND, 0), (ahead_ref, AHEAD, BEHIND)):
         h = ref[0:rows, :].astype(F32)
         scale = lax.rsqrt(jnp.mean(h * h, axis=-1, keepdims=True) + 1e-06)
         halo_ref[place : place + rows, :] = (h * scale * gain).astype(BF16)
     for ref, whole in ((q_ref, q_own), (k_ref, k_own), (v_ref, v_own)):
         ref[BEHIND:end, :] = whole[...]
+    for copy in weights[1] + weights[2] + [wout_copy]:
+        copy.start()
     clear_spare((k_ref, v_ref))
     both = [(BEHIND, 0), (AHEAD, end)]
-    copies[0].wait()
-    project(halo_ref, wqkv.at[1], 0, BEHIND + AHEAD, k_ref, both)
-    copies[1].wait()
-    project(halo_ref, wqkv.at[2], 0, BEHIND + AHEAD, v_ref, both)
-    copies[2].wait()
-    project(halo_ref, wqkv.at[0], UNIT, BEHIND + AHEAD, q_ref, [(UNIT, UNIT), (AHEAD, end)])
+    edges = [(UNIT, UNIT), (AHEAD, end)]
+    project(halo_ref, wk_ref, 0, BEHIND + AHEAD, k_ref, both, weights[0])
+    project(halo_ref, wv_ref, 0, BEHIND + AHEAD, v_ref, both, weights[1])
+    project(halo_ref, wq_ref, UNIT, BEHIND + AHEAD, q_ref, edges, weights[2])
     attend(1, total // UNIT, q_ref, k_ref, v_ref, att_ref, bias_ref, score_ref, prob_ref)
-    copies[3].wait()
+    wout_copy.wait()
     depth = wout.shape[1]
     for at in range(0, depth, TILE):
         cols = slice(at, at + TILE)
@@ -316,17 +330,24 @@
         h_ref[end:total, cols] = ahead_ref[0:AHEAD, cols].astype(F32) + moved[UNIT + own :]
 
     normalize(h_ref, normed_ref, gain, UNIT, total)
-    project(normed_ref, wqkv.at[1], UNIT, total, k_ref, [(total - UNIT, UNIT)])
-    project(normed_ref, wqkv.at[2], UNIT, total, v_ref, [(total - UNIT, UNIT)])
-    project(normed_ref, wqkv.at[0], BEHIND, end, q_ref, [(own, BEHIND)])
+    project(normed_ref, wk_ref, UNIT, total, k_ref, [(total - UNIT, UNIT)])
+    project(normed_ref, wv_ref, UNIT, total, v_ref, [(total - UNIT, UNIT)])
+    project(normed_ref, wq_ref, BEHIND, end, q_ref, [(own, BEHIND)])
     attend(
         BEHIND // UNIT, end // UNIT, q_ref, k_ref, v_ref, att_ref, bias_ref, score_ref, prob_ref
     )
-    for at in range(0, depth, TILE):
+    sent = []
+    for i, at in enumerate(range(0, depth, TILE)):
         cols = slice(at, at + TILE)
         moved = jnp.dot(att_ref[BEHIND:end, :], wout[:, cols], preferred_element_type=F32)
         x = h_ref[BEHIND:end, cols] - cond_ref[:, cols].astype(F32) - half_time[:, cols]
         out_ref[:, cols] = (x + 0.5 * moved).astype(BF16)
+        tile = pl.ds(at, TILE)
+        sem = sems.at[3 * tiles + 1 + i]
+        sent.append(pltpu.make_async_copy(out_ref.at[:, tile], out_hbm.at[:, tile], sem))
+        sent[-1].start()
+    for copy in sent:
+        copy.wait()
 
 
 def clear_spare(refs):
@@ -373,7 +394,7 @@
     hbm = pl.BlockSpec(memory_space=pltpu.HBM)
 
     def limit(mib):
-        return pltpu.CompilerParams(vmem_limit_bytes=mib * 2**20)
+        return pltpu.CompilerParams(vmem_limit_bytes=int(mib * 2**20))
 
     cross, core, small = pl.pallas_call(
         edge_kernel,
@@ -402,28 +423,30 @@
         ((width // HEAD_DIM * UNIT, WINDOW), BF16),
     ]
     if parts == 1:
-        kept = [jax.ShapeDtypeStruct((own, depth), BF16)] * 2
+        tiles = width // min(TILE, width)
+        kept = [(state.shape, BF16)] * 2 + [((own, width), BF16)] * 3
+        kept += [((total + SPARE, 128), F32), ((total // UNIT, UNIT, WINDOW), F32)]
         kept = pl.pallas_call(
             own_kernel,
-            out_shape=kept + [jax.ShapeDtypeStruct((own, width), BF16)] * 3,
+            out_shape=[jax.ShapeDtypeStruct(*one) for one in kept],
             in_specs=[vmem] + [hbm] * 3,
-            out_specs=[vmem] * 5,
-            scratch_shapes=[pltpu.VMEM(w_qkv.shape, BF16), pltpu.VMEM((own, depth), BF16)]
-            + [pltpu.SemaphoreType.DMA((5,))],
+            out_specs=[vmem] * 7,
+            scratch_shapes=[pltpu.VMEM((depth, width), BF16)] * 3
+            + [pltpu.VMEM((own, depth), BF16), pltpu.SemaphoreType.DMA((2 + 3 * tiles,))],
             compiler_params=limit(OWN_LIMIT),
             cost_estimate=pl.CostEstimate(
                 flops=6 * own * depth * width, bytes_accessed=2 * 4 * depth * width, transcendentals=0
             ),
         )(small, state, condition, w_qkv)
-        first = [(w_qkv.shape, BF16), (w_out.shape, BF16)] + [((PAYLOAD, depth), BF16)] * 2
-        first += [((BEHIND + AHEAD, depth), BF16), ((total, depth), F32)]
+        first = [((depth, width), BF16)] * 3 + [(w_out.shape, BF16)] + [((PAYLOAD, depth), BF16)] * 2
+        first += [((BEHIND + AHEAD, depth), BF16), ((total, depth), F32), ((own, depth), BF16)]
         return pl.pallas_call(
             rest_kernel,
             out_shape=jax.ShapeDtypeStruct((own, depth), BF16),
-            in_specs=[vmem] * 8 + [hbm] * 2,
-            out_specs=vmem,
+            in_specs=[vmem] * 10 + [hbm] * 2,
+            out_specs=hbm,
             scratch_shapes=[pltpu.VMEM(*one) for one in first + work]
-            + [pltpu.SemaphoreType.DMA((4,))],
+            + [pltpu.SemaphoreType.DMA((1 + 3 * tiles + depth // TILE,))],
             compiler_params=limit(LIMIT),
         )(cross, core, small, *kept, w_qkv, w_out)
 

time: 35.1 us -> 40.9 us (1.17)
  Pallas kernels: 29.1 us -> 34.7 us
    pallas_call x1, Pallas kernels: 6.34 us -> 10.8 us  [shards(): pl.pallas_call(own_kernel, out_shape=[jax.ShapeDtypeStruct(*one) for one...]
    pallas_call x1, Pallas kernels: 20.7 us -> 21.9 us  [shards(): pl.pallas_call(rest_kernel, out_shape=jax.ShapeDtypeStruct((own, depth),...]
  transfers between devices with their start and end apart: 2 -> 2, of which waited for: 0 -> 0; matrix products, arithmetic and copies ran while one was open for 0% -> 0% of each run, Pallas kernels for 18% -> 26%
where the time goes in v4:
time: 40.9 us; the launch traced here: 40.7 us
  Pallas kernels  34.7 us (85%)
  starting transfers between devices  5.03 us (12%)
  local copies, waits for them, and re-layouts  0.76 us (2%)
    pallas_call x1, Pallas kernels, shards(): pl.pallas_call(rest_kernel, out_shape=jax.ShapeDtypeStruct((own, depth),...  21.9 us
    pallas_call x1, Pallas kernels, shards(): pl.pallas_call(own_kernel, out_shape=[jax.ShapeDtypeStruct(*one) for one...  10.8 us
    ppermute x1, starting transfers between devices, shards(): core = lax.ppermute(core, 'seq', ends + [(j, i) for i, j in ends])  4.35 us
    pallas_call x1, Pallas kernels, shards(): pl.pallas_call(edge_kernel, out_shape=[jax.ShapeDtypeStruct((rows, depth)...  2.05 us
  transfers between devices with their start and end apart: 2, of which 0 were waited for; matrix products, arithmetic and copies ran while one was open for 0% of the time, Pallas kernels for 26%

profile of v4, /device:TPU:0, one launch (start us, length us, event | category | flops | bytes accessed | tf_op | source)
XLA Modules:
  0.0 40.7 jit_solution(4773233865608676667)
XLA Ops:
  0.0 2.1 %shard_map.73 = (bf16[112,1024]{1,0:T(8,128)(2,1)}, bf16[112,1024]{1,0:T(8,128)(2,1)}, bf16[16,1024]{1,0:T(8,128)(2,1)}) custom-call(bf16[480,1024]{1,0:T(8,128)(2,1)} %state_hbm.3, bf16[480,1024]{1,0:T(8,128)(2,1)} %cond_hbm.3, s32[1,480]{1,0:T(1,128)} %bitcast.1, bf16[1024]{0:T(1024)(128)(2,1)} %time_hbm.1, bf16[1024]{0:T(1024)(128)(2,1)} %gain_hbm.1), custom_call_target="tpu_custom_call" | custom-call | tf_op jit(solution)/shard_map/pallas_call | solution.py:399
  2.1 0.7 %collective-permute-start = (bf16[112,1024]{1,0:T(8,128)(2,1)}, bf16[112,1024]{1,0:T(8,128)(2,1)S(1)}, u32[]{:S(2)}, u32[]{:S(2)}) collective-permute-start(bf16[112,1024]{1,0:T(8,128)(2,1)} %get-tuple-element.15), channel_id=1, source_target_pairs={{1,2},{3,4},{5,6},{7,8},{9,10},{11,12},{13,14},{15,16},{17,18},{19... | collective-permute-start | bytes 688136 | tf_op jit(solution)/shard_map/ppermute | solution.py:412
  2.7 4.4 %collective-permute-start.1 = (bf16[112,1024]{1,0:T(8,128)(2,1)}, bf16[112,1024]{1,0:T(8,128)(2,1)S(1)}, u32[]{:S(2)}, u32[]{:S(2)}) collective-permute-start(bf16[112,1024]{1,0:T(8,128)(2,1)} %get-tuple-element.16), channel_id=1, source_target_pairs={{0,1},{2,3},{4,5},{6,7},{8,9},{10,11},{12,13},{14,15},{16,17},{18,... | collective-permute-start | bytes 688136 | tf_op jit(solution)/shard_map/ppermute | solution.py:414
  7.1 0.0 copy-start
  7.1 0.8 %copy-done = bf16[16,1024]{1,0:T(8,128)(2,1)S(1)} copy-done((bf16[16,1024]{1,0:T(8,128)(2,1)S(1)}, bf16[16,1024]{1,0:T(8,128)(2,1)}, u32[]{:S(2)}) %copy-start) | copy-done | bytes 32792
  7.9 10.8 %shard_map.74 = (bf16[480,1024]{1,0:T(8,128)(2,1)S(1)}, bf16[480,1024]{1,0:T(8,128)(2,1)S(1)}, bf16[480,1024]{1,0:T(8,128)(2,1)S(1)}, bf16[480,1024]{1,0:T(8,128...) custom-call(bf16[16,1024]{1,0:T(8,128)(2,1)S(1)} %copy-done, ...), custom_call_target="tpu_custom_call" | custom-call | flops 3019898880 | bytes 8388608 | tf_op jit(solution)/shard_map/pallas_call | solution.py:429
  18.6 0.0 collective-permute-done.cross_ref
  18.7 0.0 collective-permute-done.1.core_ref
  18.7 21.9 %shard_map.75 = bf16[480,1024]{1,0:T(8,128)(2,1)} custom-call(bf16[112,1024]{1,0:T(8,128)(2,1)S(1)} %collective-permute-done.cross_ref, bf16[112,1024]{1,0:T(8,128)(2,1)S(1)} %collective-permute-done.1.core_ref, bf16[16,1024]{1,0:T(8,128)(2,1)S(1)} %copy-done, bf16[480,1024]{1,0:T(8,128)(2,1)S(1)} %get-tuple-element.18.state_ref, ...), custom_call_target="tpu_custom_call" | custom-call | tf_op jit(solution)/shard_map/pallas_call | solution.py:443
Async XLA Ops:
  2.1 16.6 %collective-permute-start = (bf16[112,1024]{1,0:T(8,128)(2,1)}, bf16[112,1024]{1,0:T(8,128)(2,1)S(1)}, u32[]{:S(2)}, u32[]{:S(2)}) collective-permute-start(bf16[112,1024]{1,0:T(8,128)(2,1)} %get-tuple-element.15), channel_id=1, source_target_pairs={{1,2},{3,4},{5,6},{7,8},{9,10},{11,12},{13,14},{15,16},{17,18},{19... | collective-permute-start | bytes 688136 | tf_op jit(solution)/shard_map/ppermute | solution.py:412
  2.7 15.9 %collective-permute-start.1 = (bf16[112,1024]{1,0:T(8,128)(2,1)}, bf16[112,1024]{1,0:T(8,128)(2,1)S(1)}, u32[]{:S(2)}, u32[]{:S(2)}) collective-permute-start(bf16[112,1024]{1,0:T(8,128)(2,1)} %get-tuple-element.16), channel_id=1, source_target_pairs={{0,1},{2,3},{4,5},{6,7},{8,9},{10,11},{12,13},{14,15},{16,17},{18,... | collective-permute-start | bytes 688136 | tf_op jit(solution)/shard_map/ppermute | solution.py:414
  7.1 0.8 %copy-start = (bf16[16,1024]{1,0:T(8,128)(2,1)S(1)}, bf16[16,1024]{1,0:T(8,128)(2,1)}, u32[]{:S(2)}) copy-start(bf16[16,1024]{1,0:T(8,128)(2,1)} %get-tuple-element.17.small_ref) | copy-start | bytes 98308

commit v5 on v4

--- a/solution.py
+++ b/solution.py
@@ -16,6 +16,7 @@
 WINDOW = 128
 SPARE = WINDOW - 2 * UNIT
 PAIR = 2 * HEAD_DIM
+FOUR = 4
 SMALL = 16
 PAYLOAD = BEHIND + 16
 TILE = 256
@@ -81,27 +82,11 @@
     lax.fori_loop(0, (last - first) // UNIT, one, 0)
 
 
-def width_tiles(w_ref):
-    return w_ref.shape[1] // min(TILE, w_ref.shape[1])
-
-
-def tile_copies(w_hbm, w_ref, sems, first_sem):
-    tile = min(TILE, w_ref.shape[1])
-    return [
-        pltpu.make_async_copy(
-            w_hbm.at[:, pl.ds(i * tile, tile)], w_ref.at[:, pl.ds(i * tile, tile)], sems.at[first_sem + i]
-        )
-        for i in range(w_ref.shape[1] // tile)
-    ]
-
-
-def project(normed_ref, w_ref, first, last, out_ref, places, arriving=None):
+def project(normed_ref, w_ref, first, last, out_ref, places):
     width = w_ref.shape[1]
     tile = min(TILE, width)
     for at in range(0, width, tile):
         cols = slice(at, at + tile)
-        if arriving is not None:
-            arriving[at // tile].wait()
         out = jnp.dot(
             normed_ref[first:last, :], w_ref[:, cols], preferred_element_type=F32
         ).astype(BF16)
@@ -111,9 +96,9 @@
             done += rows
 
 
-def attend(first, last, q_ref, k_ref, v_ref, att_ref, bias_ref, score_ref, prob_ref):
-    pairs = q_ref.shape[1] // PAIR
-    ones = jnp.ones((WINDOW, PAIR), BF16)
+def attend(first, last, q_ref, k_ref, v_ref, att_ref, bias_ref, score_ref, prob_ref, sum_ref):
+    wide = FOUR * HEAD_DIM
+    groups = q_ref.shape[1] // wide
     factor = HEAD_DIM**-0.5 * math.log2(math.e)
 
     def at(unit):
@@ -122,35 +107,46 @@
 
     def score(unit):
         rows, window = at(unit)
-        one = lax.broadcasted_iota(jnp.int32, (UNIT, PAIR), 1) < HEAD_DIM
-        for p in range(pairs):
-            lanes = slice(p * PAIR, (p + 1) * PAIR)
+        head = lax.broadcasted_iota(jnp.int32, (UNIT, wide), 1) // HEAD_DIM
+        for g in range(groups):
+            lanes = slice(g * wide, (g + 1) * wide)
             q = q_ref[rows, lanes]
             zero = jnp.zeros_like(q)
-            both = jnp.concatenate([jnp.where(one, q, zero), jnp.where(one, zero, q)], axis=0)
-            score_ref[2 * p * UNIT : 2 * (p + 1) * UNIT, :] = lax.dot_general(
-                both, k_ref[window, lanes], (((1,), (1,)), ((), ())), preferred_element_type=F32
+            stacked = jnp.concatenate([jnp.where(head == j, q, zero) for j in range(FOUR)], axis=0)
+            score_ref[FOUR * g * UNIT : FOUR * (g + 1) * UNIT, :] = lax.dot_general(
+                stacked, k_ref[window, lanes], (((1,), (1,)), ((), ())), preferred_element_type=F32
             )
 
     def soften(unit):
         bias = bias_ref[unit]
-        for head in range(2 * pairs):
-            rows = slice(head * UNIT, (head + 1) * UNIT)
+        for j in range(FOUR * groups):
+            rows = slice(j * UNIT, (j + 1) * UNIT)
             s = score_ref[rows, :] * factor + bias
-            prob_ref[rows, :] = jnp.exp2(s - jnp.max(s, axis=-1, keepdims=True)).astype(BF16)
+            expo = jnp.exp2(s - jnp.max(s, axis=-1, keepdims=True))
+            prob_ref[rows, :] = expo.astype(BF16)
+            total = jnp.sum(expo, axis=-1, keepdims=True)
+            sum_ref[rows, :] = jnp.broadcast_to(total, (UNIT, PAIR))
 
     def mix(unit):
         rows, window = at(unit)
         one = lax.broadcasted_iota(jnp.int32, (UNIT, PAIR), 1) < HEAD_DIM
-        for p in range(pairs):
-            lanes = slice(p * PAIR, (p + 1) * PAIR)
-            values = jnp.concatenate([v_ref[window, lanes], ones], axis=1)
+        for g in range(groups):
+            lanes = slice(g * wide, (g + 1) * wide)
+            top = FOUR * g * UNIT
             out = jnp.dot(
-                prob_ref[2 * p * UNIT : 2 * (p + 1) * UNIT, :], values, preferred_element_type=F32
+                prob_ref[top : top + FOUR * UNIT, :], v_ref[window, lanes], preferred_element_type=F32
             )
-            mixed = jnp.where(one, out[:UNIT, :PAIR], out[UNIT:, :PAIR])
-            sums = jnp.where(one, out[:UNIT, PAIR:], out[UNIT:, PAIR:])
-            att_ref[rows, lanes] = (mixed / sums).astype(BF16)
+            for p in range(FOUR // 2):
+                low, high = 2 * p * UNIT, (2 * p + 1) * UNIT
+                cols = slice(p * PAIR, (p + 1) * PAIR)
+                mixed = jnp.where(one, out[low : low + UNIT, cols], out[high : high + UNIT, cols])
+                sums = jnp.where(
+                    one,
+                    sum_ref[top + low : top + low + UNIT, :],
+                    sum_ref[top + high : top + high + UNIT, :],
+                )
+                mine = slice(g * wide + p * PAIR, g * wide + (p + 1) * PAIR)
+                att_ref[rows, mine] = (mixed / sums).astype(BF16)
 
     score(first)
     soften(first)
@@ -234,19 +230,18 @@
         pltpu.make_async_copy(state_hbm, state_ref, sems.at[0]),
         pltpu.make_async_copy(cond_hbm, cond_ref, sems.at[1]),
     ]
-    tiles = width_tiles(wk_ref)
     weights = [
-        tile_copies(wqkv_hbm.at[which], w_ref, sems, 2 + i * tiles)
-        for i, (which, w_ref) in enumerate(((1, wk_ref), (2, wv_ref), (0, wq_ref)))
+        pltpu.make_async_copy(wqkv_hbm.at[which], w_ref, sems.at[2 + which])
+        for which, w_ref in ((1, wk_ref), (2, wv_ref), (0, wq_ref))
     ]
-    for copy in copies + weights[0]:
+    for copy in copies + weights[:1]:
         copy.start()
     gain = small_ref[2:3, :].astype(F32)
     own_segments(small_ref, seg_ref, own)
     build_masks((3, own // UNIT + 1), seg_ref, bias_ref)
     copies[0].wait()
     copies[1].wait()
-    for copy in weights[1] + weights[2]:
+    for copy in weights[1:]:
         copy.start()
 
     def one(i, carry):
@@ -257,8 +252,9 @@
         return carry
 
     lax.fori_loop(0, own // UNIT, one, 0)
-    for w_ref, arriving, out_ref in zip((wk_ref, wv_ref, wq_ref), weights, (k_ref, v_ref, q_ref)):
-        project(normed_ref, w_ref, 0, own, out_ref, [(own, 0)], arriving)
+    for w_ref, copy, out_ref in zip((wk_ref, wv_ref, wq_ref), weights, (k_ref, v_ref, q_ref)):
+        copy.wait()
+        project(normed_ref, w_ref, 0, own, out_ref, [(own, 0)])
 
 
 def rest_kernel(
@@ -266,21 +262,19 @@
     wqkv_hbm, wout_hbm,
     out_hbm,
     wk_ref, wv_ref, wq_ref, wout, behind_ref, ahead_ref, halo_ref, h_ref, out_ref,
-    normed_ref, q_ref, k_ref, v_ref, att_ref, seg_ref, bias_ref, score_ref, prob_ref,
+    normed_ref, q_ref, k_ref, v_ref, att_ref, seg_ref, bias_ref, score_ref, prob_ref, sum_ref,
     sems,
 ):
     own = state_ref.shape[0]
     units = own // UNIT
     end = BEHIND + own
     total = end + AHEAD
-    tiles = width_tiles(wk_ref)
     weights = [
-        tile_copies(wqkv_hbm.at[which], w_ref, sems, i * tiles)
-        for i, (which, w_ref) in enumerate(((1, wk_ref), (2, wv_ref), (0, wq_ref)))
+        pltpu.make_async_copy(wqkv_hbm.at[which], w_ref, sems.at[which])
+        for which, w_ref in ((1, wk_ref), (2, wv_ref), (0, wq_ref))
     ]
-    wout_copy = pltpu.make_async_copy(wout_hbm, wout, sems.at[3 * tiles])
-    for copy in weights[0]:
-        copy.start()
+    wout_copy = pltpu.make_async_copy(wout_hbm, wout, sems.at[3])
+    weights[0].start()
     half_time = 0.5 * small_ref[1:2, :].astype(F32)
     gain = small_ref[2:3, :].astype(F32)
     even = lax.rem(lax.axis_index("seq"), 2) == 0
@@ -308,15 +302,18 @@
         halo_ref[place : place + rows, :] = (h * scale * gain).astype(BF16)
     for ref, whole in ((q_ref, q_own), (k_ref, k_own), (v_ref, v_own)):
         ref[BEHIND:end, :] = whole[...]
-    for copy in weights[1] + weights[2] + [wout_copy]:
+    for copy in weights[1:] + [wout_copy]:
         copy.start()
     clear_spare((k_ref, v_ref))
     both = [(BEHIND, 0), (AHEAD, end)]
     edges = [(UNIT, UNIT), (AHEAD, end)]
-    project(halo_ref, wk_ref, 0, BEHIND + AHEAD, k_ref, both, weights[0])
-    project(halo_ref, wv_ref, 0, BEHIND + AHEAD, v_ref, both, weights[1])
-    project(halo_ref, wq_ref, UNIT, BEHIND + AHEAD, q_ref, edges, weights[2])
-    attend(1, total // UNIT, q_ref, k_ref, v_ref, att_ref, bias_ref, score_ref, prob_ref)
+    weights[0].wait()
+    project(halo_ref, wk_ref, 0, BEHIND + AHEAD, k_ref, both)
+    weights[1].wait()
+    project(halo_ref, wv_ref, 0, BEHIND + AHEAD, v_ref, both)
+    weights[2].wait()
+    project(halo_ref, wq_ref, UNIT, BEHIND + AHEAD, q_ref, edges)
+    attend(1, total // UNIT, q_ref, k_ref, v_ref, att_ref, bias_ref, score_ref, prob_ref, sum_ref)
     wout_copy.wait()
     depth = wout.shape[1]
     for at in range(0, depth, TILE):
@@ -334,17 +331,19 @@
     project(normed_ref, wv_ref, UNIT, total, v_ref, [(total - UNIT, UNIT)])
     project(normed_ref, wq_ref, BEHIND, end, q_ref, [(own, BEHIND)])
     attend(
-        BEHIND // UNIT, end // UNIT, q_ref, k_ref, v_ref, att_ref, bias_ref, score_ref, prob_ref
+        BEHIND // UNIT, end // UNIT, q_ref, k_ref, v_ref, att_ref, bias_ref, score_ref, prob_ref, sum_ref
     )
     sent = []
-    for i, at in enumerate(range(0, depth, TILE)):
-        cols = slice(at, at + TILE)
-        moved = jnp.dot(att_ref[BEHIND:end, :], wout[:, cols], preferred_element_type=F32)
-        x = h_ref[BEHIND:end, cols] - cond_ref[:, cols].astype(F32) - half_time[:, cols]
-        out_ref[:, cols] = (x + 0.5 * moved).astype(BF16)
-        tile = pl.ds(at, TILE)
-        sem = sems.at[3 * tiles + 1 + i]
-        sent.append(pltpu.make_async_copy(out_ref.at[:, tile], out_hbm.at[:, tile], sem))
+    for half in range(2):
+        mine = slice(half * own // 2, (half + 1) * own // 2)
+        rows = slice(BEHIND + mine.start, BEHIND + mine.stop)
+        for at in range(0, depth, TILE):
+            cols = slice(at, at + TILE)
+            moved = jnp.dot(att_ref[rows, :], wout[:, cols], preferred_element_type=F32)
+            x = h_ref[rows, cols] - cond_ref[mine, cols].astype(F32) - half_time[:, cols]
+            out_ref[mine, cols] = (x + 0.5 * moved).astype(BF16)
+        part = pl.ds(mine.start, own // 2)
+        sent.append(pltpu.make_async_copy(out_ref.at[part], out_hbm.at[part], sems.at[4 + half]))
         sent[-1].start()
     for copy in sent:
         copy.wait()
@@ -358,7 +357,7 @@
 def one_step(
     final, h_ref, small_ref, behind_ref, ahead_ref, wqkv, wout,
     out_ref,
-    normed_ref, q_ref, k_ref, v_ref, att_ref, seg_ref, bias_ref, score_ref, prob_ref,
+    normed_ref, q_ref, k_ref, v_ref, att_ref, seg_ref, bias_ref, score_ref, prob_ref, sum_ref,
 ):
     total = h_ref.shape[0]
     own = total - BEHIND - AHEAD
@@ -374,7 +373,7 @@
     project(normed_ref, wqkv.at[0], first, last, q_ref, [(last - first, first)])
     attend(
         first // UNIT, last // UNIT,
-        q_ref, k_ref, v_ref, att_ref, bias_ref, score_ref, prob_ref,
+        q_ref, k_ref, v_ref, att_ref, bias_ref, score_ref, prob_ref, sum_ref,
     )
     for at in range(0, wout.shape[1], TILE):
         cols = slice(at, at + TILE)
@@ -421,9 +420,9 @@
         ((total // UNIT, UNIT, WINDOW), F32),
         ((width // HEAD_DIM * UNIT, WINDOW), F32),
         ((width // HEAD_DIM * UNIT, WINDOW), BF16),
+        ((width // HEAD_DIM * UNIT, PAIR), F32),
     ]
     if parts == 1:
-        tiles = width // min(TILE, width)
         kept = [(state.shape, BF16)] * 2 + [((own, width), BF16)] * 3
         kept += [((total + SPARE, 128), F32), ((total // UNIT, UNIT, WINDOW), F32)]
         kept = pl.pallas_call(
@@ -432,7 +431,7 @@
             in_specs=[vmem] + [hbm] * 3,
             out_specs=[vmem] * 7,
             scratch_shapes=[pltpu.VMEM((depth, width), BF16)] * 3
-            + [pltpu.VMEM((own, depth), BF16), pltpu.SemaphoreType.DMA((2 + 3 * tiles,))],
+            + [pltpu.VMEM((own, depth), BF16), pltpu.SemaphoreType.DMA((5,))],
             compiler_params=limit(OWN_LIMIT),
             cost_estimate=pl.CostEstimate(
                 flops=6 * own * depth * width, bytes_accessed=2 * 4 * depth * width, transcendentals=0
@@ -446,7 +445,7 @@
             in_specs=[vmem] * 10 + [hbm] * 2,
             out_specs=hbm,
             scratch_shapes=[pltpu.VMEM(*one) for one in first + work]
-            + [pltpu.SemaphoreType.DMA((1 + 3 * tiles + depth // TILE,))],
+            + [pltpu.SemaphoreType.DMA((6,))],
             compiler_params=limit(LIMIT),
         )(cross, core, small, *kept, w_qkv, w_out)
 

time: 40.9 us -> 37.5 us (0.917)
  Pallas kernels: 34.7 us -> 31.5 us
    pallas_call x1, Pallas kernels: 10.8 us -> 6.34 us  [shards(): pl.pallas_call(own_kernel, out_shape=[jax.ShapeDtypeStruct(*one) for one...]
    pallas_call x1, Pallas kernels: 21.9 us -> 23.1 us  [shards(): pl.pallas_call(rest_kernel, out_shape=jax.ShapeDtypeStruct((own, depth),...]
  transfers between devices with their start and end apart: 2 -> 2, of which waited for: 0 -> 0; matrix products, arithmetic and copies ran while one was open for 0% -> 0% of each run, Pallas kernels for 26% -> 17%
where the time goes in v5:
time: 37.5 us; the launch traced here: 37.3 us
  Pallas kernels  31.5 us (84%)
  starting transfers between devices  5.03 us (13%)
  local copies, waits for them, and re-layouts  0.76 us (2%)
    pallas_call x1, Pallas kernels, shards(): pl.pallas_call(rest_kernel, out_shape=jax.ShapeDtypeStruct((own, depth),...  23.1 us
    pallas_call x1, Pallas kernels, shards(): pl.pallas_call(own_kernel, out_shape=[jax.ShapeDtypeStruct(*one) for one...  6.34 us
    ppermute x1, starting transfers between devices, shards(): core = lax.ppermute(core, 'seq', ends + [(j, i) for i, j in ends])  4.35 us
    pallas_call x1, Pallas kernels, shards(): pl.pallas_call(edge_kernel, out_shape=[jax.ShapeDtypeStruct((rows, depth)...  2.05 us
    unnamed x2, local copies, waits for them, and re-layouts  0.76 us
  transfers between devices with their start and end apart: 2, of which 0 were waited for; matrix products, arithmetic and copies ran while one was open for 0% of the time, Pallas kernels for 17%

profile of v5, /device:TPU:0, one launch (start us, length us, event | category | flops | bytes accessed | tf_op | source)
XLA Modules:
  0.0 37.3 jit_solution(195896150895150060)
XLA Ops:
  0.0 2.1 %shard_map.73 = (bf16[112,1024]{1,0:T(8,128)(2,1)}, bf16[112,1024]{1,0:T(8,128)(2,1)}, bf16[16,1024]{1,0:T(8,128)(2,1)}) custom-call(bf16[480,1024]{1,0:T(8,128)(2,1)} %state_hbm.3, bf16[480,1024]{1,0:T(8,128)(2,1)} %cond_hbm.3, s32[1,480]{1,0:T(1,128)} %bitcast.1, bf16[1024]{0:T(1024)(128)(2,1)} %time_hbm.1, bf16[1024]{0:T(1024)(128)(2,1)} %gain_hbm.1), custom_call_target="tpu_custom_call" | custom-call | tf_op jit(solution)/shard_map/pallas_call | solution.py:398
  2.1 0.7 %collective-permute-start = (bf16[112,1024]{1,0:T(8,128)(2,1)}, bf16[112,1024]{1,0:T(8,128)(2,1)S(1)}, u32[]{:S(2)}, u32[]{:S(2)}) collective-permute-start(bf16[112,1024]{1,0:T(8,128)(2,1)} %get-tuple-element.15), channel_id=1, source_target_pairs={{1,2},{3,4},{5,6},{7,8},{9,10},{11,12},{13,14},{15,16},{17,18},{19... | collective-permute-start | bytes 688136 | tf_op jit(solution)/shard_map/ppermute | solution.py:411
  2.7 4.4 %collective-permute-start.1 = (bf16[112,1024]{1,0:T(8,128)(2,1)}, bf16[112,1024]{1,0:T(8,128)(2,1)S(1)}, u32[]{:S(2)}, u32[]{:S(2)}) collective-permute-start(bf16[112,1024]{1,0:T(8,128)(2,1)} %get-tuple-element.16), channel_id=1, source_target_pairs={{0,1},{2,3},{4,5},{6,7},{8,9},{10,11},{12,13},{14,15},{16,17},{18,... | collective-permute-start | bytes 688136 | tf_op jit(solution)/shard_map/ppermute | solution.py:413
  7.1 0.0 copy-start
  7.1 0.8 %copy-done = bf16[16,1024]{1,0:T(8,128)(2,1)S(1)} copy-done((bf16[16,1024]{1,0:T(8,128)(2,1)S(1)}, bf16[16,1024]{1,0:T(8,128)(2,1)}, u32[]{:S(2)}) %copy-start) | copy-done | bytes 32792
  7.9 6.3 %shard_map.74 = (bf16[480,1024]{1,0:T(8,128)(2,1)S(1)}, bf16[480,1024]{1,0:T(8,128)(2,1)S(1)}, bf16[480,1024]{1,0:T(8,128)(2,1)S(1)}, bf16[480,1024]{1,0:T(8,128...) custom-call(bf16[16,1024]{1,0:T(8,128)(2,1)S(1)} %copy-done, ...), custom_call_target="tpu_custom_call" | custom-call | flops 3019898880 | bytes 8388608 | tf_op jit(solution)/shard_map/pallas_call | solution.py:428
  14.2 0.0 collective-permute-done.cross_ref
  14.2 0.0 collective-permute-done.1.core_ref
  14.2 23.1 %shard_map.75 = bf16[480,1024]{1,0:T(8,128)(2,1)} custom-call(bf16[112,1024]{1,0:T(8,128)(2,1)S(1)} %collective-permute-done.cross_ref, bf16[112,1024]{1,0:T(8,128)(2,1)S(1)} %collective-permute-done.1.core_ref, bf16[16,1024]{1,0:T(8,128)(2,1)S(1)} %copy-done, bf16[480,1024]{1,0:T(8,128)(2,1)S(1)} %get-tuple-element.18.state_ref, ...), custom_call_target="tpu_custom_call" | custom-call | tf_op jit(solution)/shard_map/pallas_call | solution.py:442
Async XLA Ops:
  2.1 12.1 %collective-permute-start = (bf16[112,1024]{1,0:T(8,128)(2,1)}, bf16[112,1024]{1,0:T(8,128)(2,1)S(1)}, u32[]{:S(2)}, u32[]{:S(2)}) collective-permute-start(bf16[112,1024]{1,0:T(8,128)(2,1)} %get-tuple-element.15), channel_id=1, source_target_pairs={{1,2},{3,4},{5,6},{7,8},{9,10},{11,12},{13,14},{15,16},{17,18},{19... | collective-permute-start | bytes 688136 | tf_op jit(solution)/shard_map/ppermute | solution.py:411
  2.7 11.5 %collective-permute-start.1 = (bf16[112,1024]{1,0:T(8,128)(2,1)}, bf16[112,1024]{1,0:T(8,128)(2,1)S(1)}, u32[]{:S(2)}, u32[]{:S(2)}) collective-permute-start(bf16[112,1024]{1,0:T(8,128)(2,1)} %get-tuple-element.16), channel_id=1, source_target_pairs={{0,1},{2,3},{4,5},{6,7},{8,9},{10,11},{12,13},{14,15},{16,17},{18,... | collective-permute-start | bytes 688136 | tf_op jit(solution)/shard_map/ppermute | solution.py:413
  7.1 0.8 %copy-start = (bf16[16,1024]{1,0:T(8,128)(2,1)S(1)}, bf16[16,1024]{1,0:T(8,128)(2,1)}, u32[]{:S(2)}) copy-start(bf16[16,1024]{1,0:T(8,128)(2,1)} %get-tuple-element.17.small_ref) | copy-start | bytes 98308

commit v6 on v5

--- a/solution.py
+++ b/solution.py
@@ -17,6 +17,7 @@
 SPARE = WINDOW - 2 * UNIT
 PAIR = 2 * HEAD_DIM
 FOUR = 4
+SUM_LOW, SUM_HIGH = 2.0**-60, 2.0**100
 SMALL = 16
 PAYLOAD = BEHIND + 16
 TILE = 256
@@ -96,7 +97,7 @@
             done += rows
 
 
-def attend(first, last, q_ref, k_ref, v_ref, att_ref, bias_ref, score_ref, prob_ref, sum_ref):
+def attend(first, last, q_ref, k_ref, v_ref, att_ref, bias_ref, score_ref, prob_ref, range_ref):
     wide = FOUR * HEAD_DIM
     groups = q_ref.shape[1] // wide
     factor = HEAD_DIM**-0.5 * math.log2(math.e)
@@ -117,15 +118,20 @@
                 stacked, k_ref[window, lanes], (((1,), (1,)), ((), ())), preferred_element_type=F32
             )
 
-    def soften(unit):
+    def soften(unit, shift=False):
         bias = bias_ref[unit]
+        low, high = range_ref[0], range_ref[1]
         for j in range(FOUR * groups):
             rows = slice(j * UNIT, (j + 1) * UNIT)
             s = score_ref[rows, :] * factor + bias
-            expo = jnp.exp2(s - jnp.max(s, axis=-1, keepdims=True))
-            prob_ref[rows, :] = expo.astype(BF16)
+            if shift:
+                s = s - jnp.max(s, axis=-1, keepdims=True)
+            expo = jnp.exp2(s)
             total = jnp.sum(expo, axis=-1, keepdims=True)
-            sum_ref[rows, :] = jnp.broadcast_to(total, (UNIT, PAIR))
+            low, high = jnp.minimum(low, total), jnp.maximum(high, total)
+            prob_ref[rows, :] = (expo * pl.reciprocal(total, approx=True)).astype(BF16)
+        range_ref[0] = low
+        range_ref[1] = high
 
     def mix(unit):
         rows, window = at(unit)
@@ -140,14 +146,9 @@
                 low, high = 2 * p * UNIT, (2 * p + 1) * UNIT
                 cols = slice(p * PAIR, (p + 1) * PAIR)
                 mixed = jnp.where(one, out[low : low + UNIT, cols], out[high : high + UNIT, cols])
-                sums = jnp.where(
-                    one,
-                    sum_ref[top + low : top + low + UNIT, :],
-                    sum_ref[top + high : top + high + UNIT, :],
-                )
-                mine = slice(g * wide + p * PAIR, g * wide + (p + 1) * PAIR)
-                att_ref[rows, mine] = (mixed / sums).astype(BF16)
-
+                att_ref[rows, g * wide + p * PAIR : g * wide + (p + 1) * PAIR] = mixed.astype(BF16)
+
+    range_ref[...] = jnp.ones_like(range_ref)
     score(first)
     soften(first)
     score(first + 1)
@@ -162,12 +163,23 @@
     mix(last - 2)
     soften(last - 1)
     mix(last - 1)
+    fine = (jnp.min(range_ref[0]) >= SUM_LOW) & (jnp.max(range_ref[1]) <= SUM_HIGH)
+
+    @pl.when(jnp.logical_not(fine))
+    def _():
+        def shifted(unit, carry):
+            score(unit)
+            soften(unit, shift=True)
+            mix(unit)
+            return carry
+
+        lax.fori_loop(first, last, shifted, 0)
 
 
 def edge_kernel(
     state_hbm, cond_hbm, ids_hbm, time_hbm, gain_hbm,
-    cross_ref, core_ref, small_ref,
-    state_last, cond_last, state_first, cond_first, ids_ref, time_ref, gain_ref, sems,
+    cross_ref, core_ref, small_hbm,
+    small_ref, state_last, cond_last, state_first, cond_first, ids_ref, time_ref, gain_ref, sems,
 ):
     own = state_hbm.shape[0]
     copies = [
@@ -199,6 +211,8 @@
     vectors = [ref[...].astype(F32).reshape(1, -1) for ref in (time_ref, gain_ref)]
     blank = jnp.zeros((SMALL - 3, depth), F32)
     small_ref[...] = jnp.concatenate([number_row(ids_ref[...]), *vectors, blank], axis=0).astype(BF16)
+    kept = pltpu.make_async_copy(small_ref, small_hbm.at[pl.ds(0, SMALL)], sems.at[7])
+    kept.start()
 
     def fill(ref, state, cond, ids):
         rows = state.shape[0]
@@ -219,16 +233,19 @@
     def _():
         fill_both(cross_ref, core_ref)
 
+    kept.wait()
+
 
 def own_kernel(
-    small_ref, state_hbm, cond_hbm, wqkv_hbm,
-    state_ref, cond_ref, q_ref, k_ref, v_ref, seg_ref, bias_ref,
+    small_hbm, state_hbm, cond_hbm, wqkv_hbm,
+    small_ref, state_ref, cond_ref, q_ref, k_ref, v_ref, seg_ref, bias_ref,
     wk_ref, wv_ref, wq_ref, normed_ref, sems,
 ):
     own = state_ref.shape[0]
     copies = [
         pltpu.make_async_copy(state_hbm, state_ref, sems.at[0]),
         pltpu.make_async_copy(cond_hbm, cond_ref, sems.at[1]),
+        pltpu.make_async_copy(small_hbm.at[pl.ds(0, SMALL)], small_ref, sems.at[5]),
     ]
     weights = [
         pltpu.make_async_copy(wqkv_hbm.at[which], w_ref, sems.at[2 + which])
@@ -236,6 +253,7 @@
     ]
     for copy in copies + weights[:1]:
         copy.start()
+    copies[2].wait()
     gain = small_ref[2:3, :].astype(F32)
     own_segments(small_ref, seg_ref, own)
     build_masks((3, own // UNIT + 1), seg_ref, bias_ref)
@@ -260,9 +278,9 @@
 def rest_kernel(
     cross_ref, core_ref, small_ref, state_ref, cond_ref, q_own, k_own, v_own, seg_own, bias_own,
     wqkv_hbm, wout_hbm,
-    out_hbm,
-    wk_ref, wv_ref, wq_ref, wout, behind_ref, ahead_ref, halo_ref, h_ref, out_ref,
-    normed_ref, q_ref, k_ref, v_ref, att_ref, seg_ref, bias_ref, score_ref, prob_ref, sum_ref,
+    out_ref,
+    wk_ref, wv_ref, wq_ref, wout, behind_ref, ahead_ref, halo_ref, h_ref,
+    normed_ref, q_ref, k_ref, v_ref, att_ref, seg_ref, bias_ref, score_ref, prob_ref, range_ref,
     sems,
 ):
     own = state_ref.shape[0]
@@ -313,7 +331,7 @@
     project(halo_ref, wv_ref, 0, BEHIND + AHEAD, v_ref, both)
     weights[2].wait()
     project(halo_ref, wq_ref, UNIT, BEHIND + AHEAD, q_ref, edges)
-    attend(1, total // UNIT, q_ref, k_ref, v_ref, att_ref, bias_ref, score_ref, prob_ref, sum_ref)
+    attend(1, total // UNIT, q_ref, k_ref, v_ref, att_ref, bias_ref, score_ref, prob_ref, range_ref)
     wout_copy.wait()
     depth = wout.shape[1]
     for at in range(0, depth, TILE):
@@ -331,22 +349,13 @@
     project(normed_ref, wv_ref, UNIT, total, v_ref, [(total - UNIT, UNIT)])
     project(normed_ref, wq_ref, BEHIND, end, q_ref, [(own, BEHIND)])
     attend(
-        BEHIND // UNIT, end // UNIT, q_ref, k_ref, v_ref, att_ref, bias_ref, score_ref, prob_ref, sum_ref
+        BEHIND // UNIT, end // UNIT, q_ref, k_ref, v_ref, att_ref, bias_ref, score_ref, prob_ref, range_ref
     )
-    sent = []
-    for half in range(2):
-        mine = slice(half * own // 2, (half + 1) * own // 2)
-        rows = slice(BEHIND + mine.start, BEHIND + mine.stop)
-        for at in range(0, depth, TILE):
-            cols = slice(at, at + TILE)
-            moved = jnp.dot(att_ref[rows, :], wout[:, cols], preferred_element_type=F32)
-            x = h_ref[rows, cols] - cond_ref[mine, cols].astype(F32) - half_time[:, cols]
-            out_ref[mine, cols] = (x + 0.5 * moved).astype(BF16)
-        part = pl.ds(mine.start, own // 2)
-        sent.append(pltpu.make_async_copy(out_ref.at[part], out_hbm.at[part], sems.at[4 + half]))
-        sent[-1].start()
-    for copy in sent:
-        copy.wait()
+    for at in range(0, depth, TILE):
+        cols = slice(at, at + TILE)
+        moved = jnp.dot(att_ref[BEHIND:end, :], wout[:, cols], preferred_element_type=F32)
+        x = h_ref[BEHIND:end, cols] - cond_ref[:, cols].astype(F32) - half_time[:, cols]
+        out_ref[:, cols] = (x + 0.5 * moved).astype(BF16)
 
 
 def clear_spare(refs):
@@ -357,7 +366,7 @@
 def one_step(
     final, h_ref, small_ref, behind_ref, ahead_ref, wqkv, wout,
     out_ref,
-    normed_ref, q_ref, k_ref, v_ref, att_ref, seg_ref, bias_ref, score_ref, prob_ref, sum_ref,
+    normed_ref, q_ref, k_ref, v_ref, att_ref, seg_ref, bias_ref, score_ref, prob_ref, range_ref,
 ):
     total = h_ref.shape[0]
     own = total - BEHIND - AHEAD
@@ -373,7 +382,7 @@
     project(normed_ref, wqkv.at[0], first, last, q_ref, [(last - first, first)])
     attend(
         first // UNIT, last // UNIT,
-        q_ref, k_ref, v_ref, att_ref, bias_ref, score_ref, prob_ref, sum_ref,
+        q_ref, k_ref, v_ref, att_ref, bias_ref, score_ref, prob_ref, range_ref,
     )
     for at in range(0, wout.shape[1], TILE):
         cols = slice(at, at + TILE)
@@ -397,14 +406,15 @@
 
     cross, core, small = pl.pallas_call(
         edge_kernel,
-        out_shape=[jax.ShapeDtypeStruct((rows, depth), BF16) for rows in (PAYLOAD, PAYLOAD, SMALL)],
+        out_shape=[jax.ShapeDtypeStruct((rows, depth), BF16) for rows in (PAYLOAD, PAYLOAD, 2 * own)],
         in_specs=[hbm] * 5,
-        out_specs=[vmem] * 3,
-        scratch_shapes=[pltpu.VMEM((BEHIND, depth), BF16)] * 2
+        out_specs=[vmem, vmem, hbm],
+        scratch_shapes=[pltpu.VMEM((SMALL, depth), BF16)]
+        + [pltpu.VMEM((BEHIND, depth), BF16)] * 2
         + [pltpu.VMEM((AHEAD, depth), BF16)] * 2
         + [pltpu.VMEM((1, own), jnp.int32)]
         + [pltpu.VMEM((depth,), BF16)] * 2
-        + [pltpu.SemaphoreType.DMA((7,))],
+        + [pltpu.SemaphoreType.DMA((8,))],
         compiler_params=limit(EDGE_LIMIT),
     )(state, condition, ids, time_vector, norm_gain)
     ends = [(i, i + 1) for i in range(1, count - 1, 2)]
@@ -420,36 +430,37 @@
         ((total // UNIT, UNIT, WINDOW), F32),
         ((width // HEAD_DIM * UNIT, WINDOW), F32),
         ((width // HEAD_DIM * UNIT, WINDOW), BF16),
-        ((width // HEAD_DIM * UNIT, PAIR), F32),
+        ((2, UNIT, PAIR), F32),
     ]
     if parts == 1:
-        kept = [(state.shape, BF16)] * 2 + [((own, width), BF16)] * 3
+        kept = [((SMALL, depth), BF16)] + [(state.shape, BF16)] * 2 + [((own, width), BF16)] * 3
         kept += [((total + SPARE, 128), F32), ((total // UNIT, UNIT, WINDOW), F32)]
         kept = pl.pallas_call(
             own_kernel,
             out_shape=[jax.ShapeDtypeStruct(*one) for one in kept],
-            in_specs=[vmem] + [hbm] * 3,
-            out_specs=[vmem] * 7,
+            in_specs=[hbm] * 4,
+            out_specs=[vmem] * 8,
             scratch_shapes=[pltpu.VMEM((depth, width), BF16)] * 3
-            + [pltpu.VMEM((own, depth), BF16), pltpu.SemaphoreType.DMA((5,))],
+            + [pltpu.VMEM((own, depth), BF16), pltpu.SemaphoreType.DMA((6,))],
             compiler_params=limit(OWN_LIMIT),
             cost_estimate=pl.CostEstimate(
                 flops=6 * own * depth * width, bytes_accessed=2 * 4 * depth * width, transcendentals=0
             ),
         )(small, state, condition, w_qkv)
         first = [((depth, width), BF16)] * 3 + [(w_out.shape, BF16)] + [((PAYLOAD, depth), BF16)] * 2
-        first += [((BEHIND + AHEAD, depth), BF16), ((total, depth), F32), ((own, depth), BF16)]
+        first += [((BEHIND + AHEAD, depth), BF16), ((total, depth), F32)]
         return pl.pallas_call(
             rest_kernel,
             out_shape=jax.ShapeDtypeStruct((own, depth), BF16),
             in_specs=[vmem] * 10 + [hbm] * 2,
-            out_specs=hbm,
+            out_specs=vmem,
             scratch_shapes=[pltpu.VMEM(*one) for one in first + work]
-            + [pltpu.SemaphoreType.DMA((6,))],
+            + [pltpu.SemaphoreType.DMA((4,))],
             compiler_params=limit(LIMIT),
-        )(cross, core, small, *kept, w_qkv, w_out)
+        )(cross, core, *kept, w_qkv, w_out)
 
     even = lax.axis_index("seq") % 2 == 0
+    small = small[:SMALL]
     behind = jnp.where(even, cross, core)
     ahead = jnp.where(even, core, cross)
 

time: 37.5 us -> 47.7 us (1.27)
  the two profiles are of different devices: /device:TPU:0 before, /device:TPU:11 now
where the time goes in v6:
time: 47.7 us; the launch traced here: 47.2 us
  Pallas kernels  42.9 us (90%)
  starting transfers between devices  3.75 us (8%)
  waiting for transfers between devices  0.48 us (1%)
    pallas_call x1, Pallas kernels, shards(): pl.pallas_call(rest_kernel, out_shape=jax.ShapeDtypeStruct((own, depth),...  33.7 us
    pallas_call x1, Pallas kernels, shards(): pl.pallas_call(own_kernel, out_shape=[jax.ShapeDtypeStruct(*one) for one...  6.61 us
    ppermute x1, starting transfers between devices, shards(): cross = lax.ppermute(cross, 'seq', ends + [(j, i) for i, j in ends])  3.68 us
    pallas_call x1, Pallas kernels, shards(): pl.pallas_call(edge_kernel, out_shape=[jax.ShapeDtypeStruct((rows, depth)...  2.59 us
  transfers between devices with their start and end apart: 2, of which 1 were waited for; matrix products, arithmetic and copies ran while one was open for 0% of the time, Pallas kernels for 14%

profile of v6, /device:TPU:11, one launch (start us, length us, event | category | flops | bytes accessed | tf_op | source)
XLA Modules:
  0.0 47.2 jit_solution(109599681038099015)
XLA Ops:
  0.0 2.6 %shard_map.73 = (bf16[112,1024]{1,0:T(8,128)(2,1)}, bf16[112,1024]{1,0:T(8,128)(2,1)}, bf16[960,1024]{1,0:T(8,128)(2,1)}) custom-call(bf16[480,1024]{1,0:T(8,128)(2,1)} %state_hbm.3, bf16[480,1024]{1,0:T(8,128)(2,1)} %cond_hbm.3, s32[1,480]{1,0:T(1,128)} %bitcast.1, bf16[1024]{0:T(1024)(128)(2,1)} %time_hbm.1, bf16[1024]{0:T(1024)(128)(2,1)} %gain_hbm.1), custom_call_target="tpu_custom_call" | custom-call | tf_op jit(solution)/shard_map/pallas_call | solution.py:407
  2.6 3.7 %collective-permute-start = (bf16[112,1024]{1,0:T(8,128)(2,1)}, bf16[112,1024]{1,0:T(8,128)(2,1)S(1)}, u32[]{:S(2)}, u32[]{:S(2)}) collective-permute-start(bf16[112,1024]{1,0:T(8,128)(2,1)} %get-tuple-element.16), channel_id=1, source_target_pairs={{1,2},{3,4},{5,6},{7,8},{9,10},{11,12},{13,14},{15,16},{17,18},{19... | collective-permute-start | bytes 688136 | tf_op jit(solution)/shard_map/ppermute | solution.py:421
  6.3 0.1 collective-permute-start.1
  6.4 6.6 %shard_map.74 = (bf16[16,1024]{1,0:T(8,128)(2,1)S(1)}, bf16[480,1024]{1,0:T(8,128)(2,1)S(1)}, bf16[480,1024]{1,0:T(8,128)(2,1)S(1)}, bf16[480,1024]{1,0:T(8,128)...) custom-call(bf16[960,1024]{1,0:T(8,128)(2,1)} %get-tuple-element.18., ...), custom_call_target="tpu_custom_call" | custom-call | flops 3019898880 | bytes 8388608 | tf_op jit(solution)/shard_map/pallas_call | solution.py:438
  13.0 0.5 %collective-permute-done.cross_ref = bf16[112,1024]{1,0:T(8,128)(2,1)S(1)} collective-permute-done((bf16[112,1024]{1,0:T(8,128)(2,1)}, bf16[112,1024]{1,0:T(8,128)(2,1)S(1)}, u32[]{:S(2)}, u32[]{:S(2)}) %collective-permute-start) | collective-permute-done | bytes 229408 | tf_op jit(solution)/shard_map/ppermute | solution.py:421
  13.5 0.0 collective-permute-done.1.core_ref
  13.5 33.7 %shard_map.75 = bf16[480,1024]{1,0:T(8,128)(2,1)} custom-call(bf16[112,1024]{1,0:T(8,128)(2,1)S(1)} %collective-permute-done.cross_ref, bf16[112,1024]{1,0:T(8,128)(2,1)S(1)} %collective-permute-done.1.core_ref, bf16[16,1024]{1,0:T(8,128)(2,1)S(1)} %get-tuple-element.19.small_ref, bf16[480,1024]{1,0:T(8,128)(2,1)S(1)} %get-tuple-element.20.state_ref, ...), custom_call_target="tpu_custom_call" | custom-call | tf_op jit(solution)/shard_map/pallas_call | solution.py:452
Async XLA Ops:
  2.6 10.9 %collective-permute-start = (bf16[112,1024]{1,0:T(8,128)(2,1)}, bf16[112,1024]{1,0:T(8,128)(2,1)S(1)}, u32[]{:S(2)}, u32[]{:S(2)}) collective-permute-start(bf16[112,1024]{1,0:T(8,128)(2,1)} %get-tuple-element.16), channel_id=1, source_target_pairs={{1,2},{3,4},{5,6},{7,8},{9,10},{11,12},{13,14},{15,16},{17,18},{19... | collective-permute-start | bytes 688136 | tf_op jit(solution)/shard_map/ppermute | solution.py:421
  6.3 7.2 %collective-permute-start.1 = (bf16[112,1024]{1,0:T(8,128)(2,1)}, bf16[112,1024]{1,0:T(8,128)(2,1)S(1)}, u32[]{:S(2)}, u32[]{:S(2)}) collective-permute-start(bf16[112,1024]{1,0:T(8,128)(2,1)} %get-tuple-element.17), channel_id=1, source_target_pairs={{0,1},{2,3},{4,5},{6,7},{8,9},{10,11},{12,13},{14,15},{16,17},{18,... | collective-permute-start | bytes 688136 | tf_op jit(solution)/shard_map/ppermute | solution.py:423

commit v7 on v6

--- a/solution.py
+++ b/solution.py
@@ -97,7 +97,7 @@
             done += rows
 
 
-def attend(first, last, q_ref, k_ref, v_ref, att_ref, bias_ref, score_ref, prob_ref, range_ref):
+def attend(first, last, q_ref, k_ref, v_ref, att_ref, bias_ref, range_ref, group_refs):
     wide = FOUR * HEAD_DIM
     groups = q_ref.shape[1] // wide
     factor = HEAD_DIM**-0.5 * math.log2(math.e)
@@ -106,71 +106,74 @@
         start = pl.multiple_of(unit * UNIT, 16)
         return pl.ds(start, UNIT), pl.ds(pl.multiple_of(start - UNIT, 16), WINDOW)
 
-    def score(unit):
+    score_refs, prob_refs = group_refs[:groups], group_refs[groups:]
+
+    def score(unit, g):
         rows, window = at(unit)
         head = lax.broadcasted_iota(jnp.int32, (UNIT, wide), 1) // HEAD_DIM
-        for g in range(groups):
-            lanes = slice(g * wide, (g + 1) * wide)
-            q = q_ref[rows, lanes]
-            zero = jnp.zeros_like(q)
-            stacked = jnp.concatenate([jnp.where(head == j, q, zero) for j in range(FOUR)], axis=0)
-            score_ref[FOUR * g * UNIT : FOUR * (g + 1) * UNIT, :] = lax.dot_general(
-                stacked, k_ref[window, lanes], (((1,), (1,)), ((), ())), preferred_element_type=F32
-            )
-
-    def soften(unit, shift=False):
+        lanes = slice(g * wide, (g + 1) * wide)
+        q = q_ref[rows, lanes]
+        zero = jnp.zeros_like(q)
+        stacked = jnp.concatenate([jnp.where(head == j, q, zero) for j in range(FOUR)], axis=0)
+        score_refs[g][...] = lax.dot_general(
+            stacked, k_ref[window, lanes], (((1,), (1,)), ((), ())), preferred_element_type=F32
+        )
+
+    def soften(unit, g, shift=False):
         bias = bias_ref[unit]
         low, high = range_ref[0], range_ref[1]
-        for j in range(FOUR * groups):
+        for j in range(FOUR):
             rows = slice(j * UNIT, (j + 1) * UNIT)
-            s = score_ref[rows, :] * factor + bias
+            s = score_refs[g][rows, :] * factor + bias
             if shift:
                 s = s - jnp.max(s, axis=-1, keepdims=True)
             expo = jnp.exp2(s)
             total = jnp.sum(expo, axis=-1, keepdims=True)
             low, high = jnp.minimum(low, total), jnp.maximum(high, total)
-            prob_ref[rows, :] = (expo * pl.reciprocal(total, approx=True)).astype(BF16)
+            prob_refs[g][rows, :] = (expo * pl.reciprocal(total, approx=True)).astype(BF16)
         range_ref[0] = low
         range_ref[1] = high
 
-    def mix(unit):
+    def mix(unit, g):
         rows, window = at(unit)
         one = lax.broadcasted_iota(jnp.int32, (UNIT, PAIR), 1) < HEAD_DIM
+        lanes = slice(g * wide, (g + 1) * wide)
+        out = jnp.dot(prob_refs[g][...], v_ref[window, lanes], preferred_element_type=F32)
+        for p in range(FOUR // 2):
+            low, high = 2 * p * UNIT, (2 * p + 1) * UNIT
+            cols = slice(p * PAIR, (p + 1) * PAIR)
+            mixed = jnp.where(one, out[low : low + UNIT, cols], out[high : high + UNIT, cols])
+            att_ref[rows, g * wide + p * PAIR : g * wide + (p + 1) * PAIR] = mixed.astype(BF16)
+
+    def stages(mixed=None, softened=None, scored=None):
         for g in range(groups):
-            lanes = slice(g * wide, (g + 1) * wide)
-            top = FOUR * g * UNIT
-            out = jnp.dot(
-                prob_ref[top : top + FOUR * UNIT, :], v_ref[window, lanes], preferred_element_type=F32
-            )
-            for p in range(FOUR // 2):
-                low, high = 2 * p * UNIT, (2 * p + 1) * UNIT
-                cols = slice(p * PAIR, (p + 1) * PAIR)
-                mixed = jnp.where(one, out[low : low + UNIT, cols], out[high : high + UNIT, cols])
-                att_ref[rows, g * wide + p * PAIR : g * wide + (p + 1) * PAIR] = mixed.astype(BF16)
+            if mixed is not None:
+                mix(mixed, g)
+            if softened is not None:
+                soften(softened, g)
+            if scored is not None:
+                score(scored, g)
 
     range_ref[...] = jnp.ones_like(range_ref)
-    score(first)
-    soften(first)
-    score(first + 1)
+    stages(scored=first)
+    stages(softened=first, scored=first + 1)
 
     def one(unit, carry):
-        mix(unit)
-        soften(unit + 1)
-        score(unit + 2)
+        stages(unit, unit + 1, unit + 2)
         return carry
 
     lax.fori_loop(first, last - 2, one, 0)
-    mix(last - 2)
-    soften(last - 1)
-    mix(last - 1)
+    stages(mixed=last - 2, softened=last - 1)
+    stages(mixed=last - 1)
     fine = (jnp.min(range_ref[0]) >= SUM_LOW) & (jnp.max(range_ref[1]) <= SUM_HIGH)
 
     @pl.when(jnp.logical_not(fine))
     def _():
         def shifted(unit, carry):
-            score(unit)
-            soften(unit, shift=True)
-            mix(unit)
+            for g in range(groups):
+                score(unit, g)
+                soften(unit, g, shift=True)
+                mix(unit, g)
             return carry
 
         lax.fori_loop(first, last, shifted, 0)
@@ -178,8 +181,8 @@
 
 def edge_kernel(
     state_hbm, cond_hbm, ids_hbm, time_hbm, gain_hbm,
-    cross_ref, core_ref, small_hbm,
-    small_ref, state_last, cond_last, state_first, cond_first, ids_ref, time_ref, gain_ref, sems,
+    cross_hbm, core_hbm, small_hbm,
+    cross_ref, core_ref, small_ref, state_last, cond_last, state_first, cond_first, ids_ref, time_ref, gain_ref, sems,
 ):
     own = state_hbm.shape[0]
     copies = [
@@ -211,8 +214,12 @@
     vectors = [ref[...].astype(F32).reshape(1, -1) for ref in (time_ref, gain_ref)]
     blank = jnp.zeros((SMALL - 3, depth), F32)
     small_ref[...] = jnp.concatenate([number_row(ids_ref[...]), *vectors, blank], axis=0).astype(BF16)
-    kept = pltpu.make_async_copy(small_ref, small_hbm.at[pl.ds(0, SMALL)], sems.at[7])
-    kept.start()
+    leaving = [
+        pltpu.make_async_copy(small_ref, small_hbm.at[pl.ds(0, SMALL)], sems.at[7]),
+        pltpu.make_async_copy(cross_ref, cross_hbm, sems.at[8]),
+        pltpu.make_async_copy(core_ref, core_hbm, sems.at[9]),
+    ]
+    leaving[0].start()
 
     def fill(ref, state, cond, ids):
         rows = state.shape[0]
@@ -233,7 +240,10 @@
     def _():
         fill_both(cross_ref, core_ref)
 
-    kept.wait()
+    leaving[1].start()
+    leaving[2].start()
+    for copy in leaving:
+        copy.wait()
 
 
 def own_kernel(
@@ -280,8 +290,7 @@
     wqkv_hbm, wout_hbm,
     out_ref,
     wk_ref, wv_ref, wq_ref, wout, behind_ref, ahead_ref, halo_ref, h_ref,
-    normed_ref, q_ref, k_ref, v_ref, att_ref, seg_ref, bias_ref, score_ref, prob_ref, range_ref,
-    sems,
+    normed_ref, q_ref, k_ref, v_ref, att_ref, seg_ref, bias_ref, range_ref, sems, *group_refs,
 ):
     own = state_ref.shape[0]
     units = own // UNIT
@@ -331,7 +340,7 @@
     project(halo_ref, wv_ref, 0, BEHIND + AHEAD, v_ref, both)
     weights[2].wait()
     project(halo_ref, wq_ref, UNIT, BEHIND + AHEAD, q_ref, edges)
-    attend(1, total // UNIT, q_ref, k_ref, v_ref, att_ref, bias_ref, score_ref, prob_ref, range_ref)
+    attend(1, total // UNIT, q_ref, k_ref, v_ref, att_ref, bias_ref, range_ref, group_refs)
     wout_copy.wait()
     depth = wout.shape[1]
     for at in range(0, depth, TILE):
@@ -349,7 +358,7 @@
     project(normed_ref, wv_ref, UNIT, total, v_ref, [(total - UNIT, UNIT)])
     project(normed_ref, wq_ref, BEHIND, end, q_ref, [(own, BEHIND)])
     attend(
-        BEHIND // UNIT, end // UNIT, q_ref, k_ref, v_ref, att_ref, bias_ref, score_ref, prob_ref, range_ref
+        BEHIND // UNIT, end // UNIT, q_ref, k_ref, v_ref, att_ref, bias_ref, range_ref, group_refs
     )
     for at in range(0, depth, TILE):
         cols = slice(at, at + TILE)
@@ -366,7 +375,7 @@
 def one_step(
     final, h_ref, small_ref, behind_ref, ahead_ref, wqkv, wout,
     out_ref,
-    normed_ref, q_ref, k_ref, v_ref, att_ref, seg_ref, bias_ref, score_ref, prob_ref, range_ref,
+    normed_ref, q_ref, k_ref, v_ref, att_ref, seg_ref, bias_ref, range_ref, *group_refs,
 ):
     total = h_ref.shape[0]
     own = total - BEHIND - AHEAD
@@ -382,7 +391,7 @@
     project(normed_ref, wqkv.at[0], first, last, q_ref, [(last - first, first)])
     attend(
         first // UNIT, last // UNIT,
-        q_ref, k_ref, v_ref, att_ref, bias_ref, score_ref, prob_ref, range_ref,
+        q_ref, k_ref, v_ref, att_ref, bias_ref, range_ref, group_refs,
     )
     for at in range(0, wout.shape[1], TILE):
         cols = slice(at, at + TILE)
@@ -408,13 +417,14 @@
         edge_kernel,
         out_shape=[jax.ShapeDtypeStruct((rows, depth), BF16) for rows in (PAYLOAD, PAYLOAD, 2 * own)],
         in_specs=[hbm] * 5,
-        out_specs=[vmem, vmem, hbm],
-        scratch_shapes=[pltpu.VMEM((SMALL, depth), BF16)]
+        out_specs=[hbm] * 3,
+        scratch_shapes=[pltpu.VMEM((PAYLOAD, depth), BF16)] * 2
+        + [pltpu.VMEM((SMALL, depth), BF16)]
         + [pltpu.VMEM((BEHIND, depth), BF16)] * 2
         + [pltpu.VMEM((AHEAD, depth), BF16)] * 2
         + [pltpu.VMEM((1, own), jnp.int32)]
         + [pltpu.VMEM((depth,), BF16)] * 2
-        + [pltpu.SemaphoreType.DMA((8,))],
+        + [pltpu.SemaphoreType.DMA((10,))],
         compiler_params=limit(EDGE_LIMIT),
     )(state, condition, ids, time_vector, norm_gain)
     ends = [(i, i + 1) for i in range(1, count - 1, 2)]
@@ -428,10 +438,10 @@
         ((total, width), BF16),
         ((total + SPARE, 128), F32),
         ((total // UNIT, UNIT, WINDOW), F32),
-        ((width // HEAD_DIM * UNIT, WINDOW), F32),
-        ((width // HEAD_DIM * UNIT, WINDOW), BF16),
         ((2, UNIT, PAIR), F32),
     ]
+    groups = [((FOUR * UNIT, WINDOW), kind) for kind in (F32, BF16) for _ in range(width // (FOUR * HEAD_DIM))]
+    groups = [pltpu.VMEM(*one) for one in groups]
     if parts == 1:
         kept = [((SMALL, depth), BF16)] + [(state.shape, BF16)] * 2 + [((own, width), BF16)] * 3
         kept += [((total + SPARE, 128), F32), ((total // UNIT, UNIT, WINDOW), F32)]
@@ -455,7 +465,8 @@
             in_specs=[vmem] * 10 + [hbm] * 2,
             out_specs=vmem,
             scratch_shapes=[pltpu.VMEM(*one) for one in first + work]
-            + [pltpu.SemaphoreType.DMA((4,))],
+            + [pltpu.SemaphoreType.DMA((4,))]
+            + groups,
             compiler_params=limit(LIMIT),
         )(cross, core, *kept, w_qkv, w_out)
 
@@ -471,7 +482,7 @@
             out_shape=jax.ShapeDtypeStruct((rows, depth), BF16),
             in_specs=[vmem] * 6,
             out_specs=vmem,
-            scratch_shapes=[pltpu.VMEM(*one) for one in work],
+            scratch_shapes=[pltpu.VMEM(*one) for one in work] + groups,
             compiler_params=limit(LIMIT),
         )(h, small, behind, ahead, w_qkv, w_out)
         return lax.psum(mine, "mp").astype(F32)

time: 47.7 us -> 56.9 us (1.19)
  the two profiles are of different devices: /device:TPU:11 before, /device:TPU:7 now
where the time goes in v7:
time: 56.9 us; the launch traced here: 56 us
  Pallas kernels  52.2 us (92%)
  starting transfers between devices  3.75 us (7%)
    pallas_call x1, Pallas kernels, shards(): pl.pallas_call(rest_kernel, out_shape=jax.ShapeDtypeStruct((own, depth),...  43.5 us
    pallas_call x1, Pallas kernels, shards(): pl.pallas_call(own_kernel, out_shape=[jax.ShapeDtypeStruct(*one) for one...  6.61 us
    ppermute x1, starting transfers between devices, shards(): cross = lax.ppermute(cross, 'seq', ends + [(j, i) for i, j in ends])  3.68 us
    pallas_call x1, Pallas kernels, shards(): pl.pallas_call(edge_kernel, out_shape=[jax.ShapeDtypeStruct((rows, depth)...  2.09 us
  transfers between devices with their start and end apart: 2, of which 0 were waited for; matrix products, arithmetic and copies ran while one was open for 0% of the time, Pallas kernels for 12%

profile of v7, /device:TPU:7, one launch (start us, length us, event | category | flops | bytes accessed | tf_op | source)
XLA Modules:
  0.0 56.0 jit_solution(14139225087328819820)
XLA Ops:
  0.0 2.1 %shard_map.73 = (bf16[112,1024]{1,0:T(8,128)(2,1)}, bf16[112,1024]{1,0:T(8,128)(2,1)}, bf16[960,1024]{1,0:T(8,128)(2,1)}) custom-call(bf16[480,1024]{1,0:T(8,128)(2,1)} %state_hbm.3, bf16[480,1024]{1,0:T(8,128)(2,1)} %cond_hbm.3, s32[1,480]{1,0:T(1,128)} %bitcast.1, bf16[1024]{0:T(1024)(128)(2,1)} %time_hbm.1, bf16[1024]{0:T(1024)(128)(2,1)} %gain_hbm.1), custom_call_target="tpu_custom_call" | custom-call | tf_op jit(solution)/shard_map/pallas_call | solution.py:416
  2.1 3.7 %collective-permute-start = (bf16[112,1024]{1,0:T(8,128)(2,1)}, bf16[112,1024]{1,0:T(8,128)(2,1)S(1)}, u32[]{:S(2)}, u32[]{:S(2)}) collective-permute-start(bf16[112,1024]{1,0:T(8,128)(2,1)} %get-tuple-element.16), channel_id=1, source_target_pairs={{1,2},{3,4},{5,6},{7,8},{9,10},{11,12},{13,14},{15,16},{17,18},{19... | collective-permute-start | bytes 688136 | tf_op jit(solution)/shard_map/ppermute | solution.py:431
  5.8 0.1 collective-permute-start.1
  5.9 6.6 %shard_map.74 = (bf16[16,1024]{1,0:T(8,128)(2,1)S(1)}, bf16[480,1024]{1,0:T(8,128)(2,1)S(1)}, bf16[480,1024]{1,0:T(8,128)(2,1)S(1)}, bf16[480,1024]{1,0:T(8,128)...) custom-call(bf16[960,1024]{1,0:T(8,128)(2,1)} %get-tuple-element.18., ...), custom_call_target="tpu_custom_call" | custom-call | flops 3019898880 | bytes 8388608 | tf_op jit(solution)/shard_map/pallas_call | solution.py:448
  12.5 0.0 collective-permute-done.cross_ref
  12.5 0.0 collective-permute-done.1.core_ref
  12.5 43.5 %shard_map.75 = bf16[480,1024]{1,0:T(8,128)(2,1)} custom-call(bf16[112,1024]{1,0:T(8,128)(2,1)S(1)} %collective-permute-done.cross_ref, bf16[112,1024]{1,0:T(8,128)(2,1)S(1)} %collective-permute-done.1.core_ref, bf16[16,1024]{1,0:T(8,128)(2,1)S(1)} %get-tuple-element.19.small_ref, bf16[480,1024]{1,0:T(8,128)(2,1)S(1)} %get-tuple-element.20.state_ref, ...), custom_call_target="tpu_custom_call" | custom-call | tf_op jit(solution)/shard_map/pallas_call | solution.py:462
Async XLA Ops:
  2.1 10.4 %collective-permute-start = (bf16[112,1024]{1,0:T(8,128)(2,1)}, bf16[112,1024]{1,0:T(8,128)(2,1)S(1)}, u32[]{:S(2)}, u32[]{:S(2)}) collective-permute-start(bf16[112,1024]{1,0:T(8,128)(2,1)} %get-tuple-element.16), channel_id=1, source_target_pairs={{1,2},{3,4},{5,6},{7,8},{9,10},{11,12},{13,14},{15,16},{17,18},{19... | collective-permute-start | bytes 688136 | tf_op jit(solution)/shard_map/ppermute | solution.py:431
  5.8 6.7 %collective-permute-start.1 = (bf16[112,1024]{1,0:T(8,128)(2,1)}, bf16[112,1024]{1,0:T(8,128)(2,1)S(1)}, u32[]{:S(2)}, u32[]{:S(2)}) collective-permute-start(bf16[112,1024]{1,0:T(8,128)(2,1)} %get-tuple-element.17), channel_id=1, source_target_pairs={{0,1},{2,3},{4,5},{6,7},{8,9},{10,11},{12,13},{14,15},{16,17},{18,... | collective-permute-start | bytes 688136 | tf_op jit(solution)/shard_map/ppermute | solution.py:433

commit v8 on v7

--- a/solution.py
+++ b/solution.py
@@ -21,6 +21,7 @@
 SMALL = 16
 PAYLOAD = BEHIND + 16
 TILE = 256
+ROWS = 16
 EDGE_LIMIT, OWN_LIMIT, LIMIT = 56, 48, 48
 F32 = jnp.float32
 BF16 = jnp.bfloat16
@@ -65,22 +66,23 @@
 
 
 def build_masks(units, seg_ref, bias_ref):
-    def one(unit, carry):
+    for unit in range(*units):
         build_mask(unit, seg_ref, bias_ref)
+
+
+def normalize(load, normed_ref, gain, first, last):
+    groups = (last - first) // ROWS
+    many = max(n for n in range(1, 13) if groups % n == 0)
+
+    def one(i, carry):
+        for j in range(many):
+            at = pl.ds(pl.multiple_of(first + (i * many + j) * ROWS, ROWS), ROWS)
+            h = load(at)
+            scale = lax.rsqrt(jnp.mean(h * h, axis=-1, keepdims=True) + 1e-06)
+            normed_ref[at, :] = (h * scale * gain).astype(BF16)
         return carry
 
-    lax.fori_loop(units[0], units[1], one, 0)
-
-
-def normalize(h_ref, normed_ref, gain, first, last):
-    def one(i, carry):
-        at = pl.ds(pl.multiple_of(first + i * UNIT, 16), UNIT)
-        h = h_ref[at, :]
-        scale = lax.rsqrt(jnp.mean(h * h, axis=-1, keepdims=True) + 1e-06)
-        normed_ref[at, :] = (h * scale * gain).astype(BF16)
-        return carry
-
-    lax.fori_loop(0, (last - first) // UNIT, one, 0)
+    lax.fori_loop(0, groups // many, one, 0)
 
 
 def project(normed_ref, w_ref, first, last, out_ref, places):
@@ -158,11 +160,16 @@
     stages(scored=first)
     stages(softened=first, scored=first + 1)
 
-    def one(unit, carry):
+    def two(i, carry):
+        unit = first + 2 * i
         stages(unit, unit + 1, unit + 2)
+        stages(unit + 1, unit + 2, unit + 3)
         return carry
 
-    lax.fori_loop(first, last - 2, one, 0)
+    passes = (last - 2 - first) // 2
+    lax.fori_loop(0, passes, two, 0)
+    if first + 2 * passes < last - 2:
+        stages(last - 3, last - 2, last - 1)
     stages(mixed=last - 2, softened=last - 1)
     stages(mixed=last - 1)
     fine = (jnp.min(range_ref[0]) >= SUM_LOW) & (jnp.max(range_ref[1]) <= SUM_HIGH)
@@ -272,14 +279,10 @@
     for copy in weights[1:]:
         copy.start()
 
-    def one(i, carry):
-        at = pl.ds(pl.multiple_of(i * UNIT, 16), UNIT)
-        h = state_ref[at, :].astype(F32) + cond_ref[at, :].astype(F32)
-        scale = lax.rsqrt(jnp.mean(h * h, axis=-1, keepdims=True) + 1e-06)
-        normed_ref[at, :] = (h * scale * gain).astype(BF16)
-        return carry
-
-    lax.fori_loop(0, own // UNIT, one, 0)
+    def hidden(at):
+        return state_ref[at, :].astype(F32) + cond_ref[at, :].astype(F32)
+
+    normalize(hidden, normed_ref, gain, 0, own)
     for w_ref, copy, out_ref in zip((wk_ref, wv_ref, wq_ref), weights, (k_ref, v_ref, q_ref)):
         copy.wait()
         project(normed_ref, w_ref, 0, own, out_ref, [(own, 0)])
@@ -353,7 +356,7 @@
         ) + moved[UNIT : UNIT + own]
         h_ref[end:total, cols] = ahead_ref[0:AHEAD, cols].astype(F32) + moved[UNIT + own :]
 
-    normalize(h_ref, normed_ref, gain, UNIT, total)
+    normalize(lambda at: h_ref[at, :], normed_ref, gain, UNIT, total)
     project(normed_ref, wk_ref, UNIT, total, k_ref, [(total - UNIT, UNIT)])
     project(normed_ref, wv_ref, UNIT, total, v_ref, [(total - UNIT, UNIT)])
     project(normed_ref, wq_ref, BEHIND, end, q_ref, [(own, BEHIND)])
@@ -385,7 +388,8 @@
     edge_segments(behind_ref, ahead_ref, seg_ref)
     build_masks((1, total // UNIT), seg_ref, bias_ref)
     clear_spare((k_ref, v_ref))
-    normalize(h_ref, normed_ref, small_ref[2:3, :].astype(F32), kv_first, total)
+    gain = small_ref[2:3, :].astype(F32)
+    normalize(lambda at: h_ref[at, :], normed_ref, gain, kv_first, total)
     project(normed_ref, wqkv.at[1], kv_first, total, k_ref, [(total - kv_first, kv_first)])
     project(normed_ref, wqkv.at[2], kv_first, total, v_ref, [(total - kv_first, kv_first)])
     project(normed_ref, wqkv.at[0], first, last, q_ref, [(last - first, first)])

time: 56.9 us -> 54.4 us (0.956)
  the two profiles are of different devices: /device:TPU:7 before, /device:TPU:27 now
where the time goes in v8:
time: 54.4 us; the launch traced here: 54.2 us
  Pallas kernels  49.2 us (90%)
  starting transfers between devices  3.75 us (7%)
  waiting for transfers between devices  1.26 us (2%)
    pallas_call x1, Pallas kernels, shards(): pl.pallas_call(rest_kernel, out_shape=jax.ShapeDtypeStruct((own, depth),...  41.3 us
    pallas_call x1, Pallas kernels, shards(): pl.pallas_call(own_kernel, out_shape=[jax.ShapeDtypeStruct(*one) for one...  5.83 us
    ppermute x1, starting transfers between devices, shards(): cross = lax.ppermute(cross, 'seq', ends + [(j, i) for i, j in ends])  3.68 us
    pallas_call x1, Pallas kernels, shards(): pl.pallas_call(edge_kernel, out_shape=[jax.ShapeDtypeStruct((rows, depth)...  2.09 us
    ppermute x1, waiting for transfers between devices, shards(): cross = lax.ppermute(cross, 'seq', ends + [(j, i) for i, j in ends])  1.26 us
  transfers between devices with their start and end apart: 2, of which 1 were waited for; matrix products, arithmetic and copies ran while one was open for 0% of the time, Pallas kernels for 11%

profile of v8, /device:TPU:27, one launch (start us, length us, event | category | flops | bytes accessed | tf_op | source)
XLA Modules:
  0.0 54.2 jit_solution(17224178222162491197)
XLA Ops:
  0.0 2.1 %shard_map.73 = (bf16[112,1024]{1,0:T(8,128)(2,1)}, bf16[112,1024]{1,0:T(8,128)(2,1)}, bf16[960,1024]{1,0:T(8,128)(2,1)}) custom-call(bf16[480,1024]{1,0:T(8,128)(2,1)} %state_hbm.3, bf16[480,1024]{1,0:T(8,128)(2,1)} %cond_hbm.3, s32[1,480]{1,0:T(1,128)} %bitcast.1, bf16[1024]{0:T(1024)(128)(2,1)} %time_hbm.1, bf16[1024]{0:T(1024)(128)(2,1)} %gain_hbm.1), custom_call_target="tpu_custom_call" | custom-call | tf_op jit(solution)/shard_map/pallas_call | solution.py:420
  2.1 3.7 %collective-permute-start = (bf16[112,1024]{1,0:T(8,128)(2,1)}, bf16[112,1024]{1,0:T(8,128)(2,1)S(1)}, u32[]{:S(2)}, u32[]{:S(2)}) collective-permute-start(bf16[112,1024]{1,0:T(8,128)(2,1)} %get-tuple-element.16), channel_id=1, source_target_pairs={{1,2},{3,4},{5,6},{7,8},{9,10},{11,12},{13,14},{15,16},{17,18},{19... | collective-permute-start | bytes 688136 | tf_op jit(solution)/shard_map/ppermute | solution.py:435
  5.8 0.1 collective-permute-start.1
  5.9 5.8 %shard_map.74 = (bf16[16,1024]{1,0:T(8,128)(2,1)S(1)}, bf16[480,1024]{1,0:T(8,128)(2,1)S(1)}, bf16[480,1024]{1,0:T(8,128)(2,1)S(1)}, bf16[480,1024]{1,0:T(8,128)...) custom-call(bf16[960,1024]{1,0:T(8,128)(2,1)} %get-tuple-element.18., ...), custom_call_target="tpu_custom_call" | custom-call | flops 3019898880 | bytes 8388608 | tf_op jit(solution)/shard_map/pallas_call | solution.py:452
  11.7 1.3 %collective-permute-done.cross_ref = bf16[112,1024]{1,0:T(8,128)(2,1)S(1)} collective-permute-done((bf16[112,1024]{1,0:T(8,128)(2,1)}, bf16[112,1024]{1,0:T(8,128)(2,1)S(1)}, u32[]{:S(2)}, u32[]{:S(2)}) %collective-permute-start) | collective-permute-done | bytes 229408 | tf_op jit(solution)/shard_map/ppermute | solution.py:435
  13.0 0.0 collective-permute-done.1.core_ref
  13.0 41.3 %shard_map.75 = bf16[480,1024]{1,0:T(8,128)(2,1)} custom-call(bf16[112,1024]{1,0:T(8,128)(2,1)S(1)} %collective-permute-done.cross_ref, bf16[112,1024]{1,0:T(8,128)(2,1)S(1)} %collective-permute-done.1.core_ref, bf16[16,1024]{1,0:T(8,128)(2,1)S(1)} %get-tuple-element.19.small_ref, bf16[480,1024]{1,0:T(8,128)(2,1)S(1)} %get-tuple-element.20.state_ref, ...), custom_call_target="tpu_custom_call" | custom-call | tf_op jit(solution)/shard_map/pallas_call | solution.py:466
Async XLA Ops:
  2.1 10.9 %collective-permute-start = (bf16[112,1024]{1,0:T(8,128)(2,1)}, bf16[112,1024]{1,0:T(8,128)(2,1)S(1)}, u32[]{:S(2)}, u32[]{:S(2)}) collective-permute-start(bf16[112,1024]{1,0:T(8,128)(2,1)} %get-tuple-element.16), channel_id=1, source_target_pairs={{1,2},{3,4},{5,6},{7,8},{9,10},{11,12},{13,14},{15,16},{17,18},{19... | collective-permute-start | bytes 688136 | tf_op jit(solution)/shard_map/ppermute | solution.py:435
  5.8 7.2 %collective-permute-start.1 = (bf16[112,1024]{1,0:T(8,128)(2,1)}, bf16[112,1024]{1,0:T(8,128)(2,1)S(1)}, u32[]{:S(2)}, u32[]{:S(2)}) collective-permute-start(bf16[112,1024]{1,0:T(8,128)(2,1)} %get-tuple-element.17), channel_id=1, source_target_pairs={{0,1},{2,3},{4,5},{6,7},{8,9},{10,11},{12,13},{14,15},{16,17},{18,... | collective-permute-start | bytes 688136 | tf_op jit(solution)/shard_map/ppermute | solution.py:437
